TPU v7x, 32 devices: a whole 2x2x4 slice. The times are simulated.
32 devices in a mesh: section: 4 (over z), dp: 8 (over y, x, core).
Axes of the slice: x: 2, y: 2, z: 4, core: 2. Of those that a mesh axis runs over, the one named last changes fastest.
Arguments:
- pending_predecessor_pair: float32 [4, 2, 8, 16, 16, 512], P('section', None, 'dp'), may hold values from -6 to 6
- incoming_stem_images: float32 [3, 8, 16, 16, 512], P(None, 'dp'), may hold values from -6 to 6
- spatial_filter_entries: float32 [4, 4, 9, 512], P('section', None, None, 'dp'), may hold values from -2 to 2
- mixing_matrix_entries: float32 [4, 4, 512, 512], P('section', None, 'dp'), may hold values from -0.25 to 0.25
Outputs:
- emitted: float32 [4, 4, 8, 16, 16, 512], P('section', None, 'dp')
All inputs are finite; a program needn't handle non-finite values.
Results may differ from a plain program's by a relative error of at most 0.00015.
Values sent between devices are 32-bit elements; how exact they have to be, the bound alone decides.
No kernel may reach another device: no remote copies, remote signals or barrier semaphores. Data moves between devices by JAX's collectives and lax.ppermute only.
A program may use at most 64 MiB of HBM per device.

v0:
```python
import functools

import jax
import jax.numpy as jnp
from jax import lax
from jax.experimental import pallas as pl
from jax.experimental.pallas import tpu as pltpu
from jax.sharding import PartitionSpec as P

F32 = jnp.float32
BF16 = jnp.bfloat16
VMEM_LIMIT = 16 * 1024 * 1024
LANES = 128
TAP_ROWS = 16


def swap(x, axis, bit):
    size = lax.axis_size(axis)
    return lax.ppermute(x, axis, [(i, i ^ bit) for i in range(size)])


def from_behind(x, axis, first=0, around=False):
    size = lax.axis_size(axis)
    pairs = [(i, i + 1) for i in range(first, size - 1)]
    return lax.ppermute(x, axis, pairs + [(size - 1, 0)] * (around and size > 1))


def from_ahead(x, axis):
    return lax.ppermute(x, axis, [(i + 1, i) for i in range(lax.axis_size(axis) - 1)])


def after(x, *others):
    return lax.optimization_barrier((x, *others))[0]


def begin(source, target, sem):
    copy = pltpu.make_async_copy(source, target, sem)
    copy.start()
    return copy


def split(x):
    high = x.astype(BF16)
    return high, (x - high.astype(F32)).astype(BF16)


def call(kernel, outs, operands, scratch, copies, cost, apart=(), outs_apart=(), aliases=None, limit=VMEM_LIMIT):
    def spec(x, i, apart):
        space = pl.ANY if i in apart else pltpu.SMEM if x.dtype == jnp.int32 else pltpu.VMEM
        return pl.BlockSpec(memory_space=space)

    return pl.pallas_call(
        kernel,
        out_shape=outs,
        in_specs=[spec(x, i, apart) for i, x in enumerate(operands)],
        out_specs=tuple(spec(x, i, outs_apart) for i, x in enumerate(outs)),
        scratch_shapes=[pltpu.VMEM(*s) for s in scratch] + [pltpu.SemaphoreType.DMA((copies,))],
        input_output_aliases=aliases or {},
        compiler_params=pltpu.CompilerParams(vmem_limit_bytes=limit),
        cost_estimate=cost,
    )(*operands)


def cost(shape, convolutions):
    rows, columns, channels = shape
    size = rows * columns * channels
    return pl.CostEstimate(
        flops=6 * convolutions * size * channels,
        bytes_accessed=4 * (3 * size + convolutions * channels * channels),
        transcendentals=0,
    )


def shifted(u, by):
    side = u.shape[1]
    column = lax.broadcasted_iota(jnp.int32, u.shape, 1)
    outside = 0 if by == 1 else side - 1
    return jnp.where(column == outside, 0.0, pltpu.roll(u, by % side, 1))


def depthwise(source, table, branch, low, width):
    x = jnp.maximum(source[:, :, low : low + width], 0.0)
    nothing = jnp.zeros((1,) + x.shape[1:], F32)
    above = jnp.concatenate([nothing, x[:-1]], 0)
    below = jnp.concatenate([x[1:], nothing], 0)
    tap = [table[low // width, branch, k : k + 1, :].reshape(1, 1, width) for k in range(9)]
    by_column = [above * tap[j] + x * tap[3 + j] + below * tap[6 + j] for j in range(3)]
    return shifted(by_column[0], 1) + by_column[1] + shifted(by_column[2], -1)


def separable(source, table, highs, lows, branch):
    rows, columns, channels = source.shape
    width = min(LANES, channels)
    depth = min(256, channels)
    total = None
    for k in range(0, channels, depth):
        parts = []
        for low in range(k, k + depth, width):
            mixed_in = depthwise(source, table, branch, low, width)
            parts.append(split(mixed_in.reshape(rows * columns, width)))
        high = jnp.concatenate([p[0] for p in parts], 1)
        low = jnp.concatenate([p[1] for p in parts], 1)
        matrix_high = highs[branch, k : k + depth, :]
        matrix_low = lows[branch, k : k + depth, :]
        product = jnp.dot(high, matrix_high, preferred_element_type=F32)
        product = product + jnp.dot(low, matrix_high, preferred_element_type=F32)
        product = product + jnp.dot(high, matrix_low, preferred_element_type=F32)
        total = product if total is None else total + product
    return total.reshape(source.shape)


def fetch(tick, at, section, stems, got, held, sem):
    for s in range(at):

        @pl.when(section == s)
        def _(s=s):
            begin(stems.at[tick - 1 - s], held, sem)

    @pl.when(section >= at)
    def _():
        begin(got, held, sem)

    return pltpu.make_async_copy(got, held, sem)


def early_kernel(tick, section, stems, got, table, highs, lows, out, held, sem):
    fetch(tick, min(tick, 2), section[0], stems, got, held, sem.at[0]).wait()
    out[...] = separable(held, table, highs, lows, 1)


def late_kernel(tick, ticks, section, stems, got, early, table, highs, lows, past, *rest):
    outs, (newest, first, second, sem) = rest[-(6 if tick < ticks - 1 else 5) : -4], rest[-4:]
    emitted = outs[0]
    store = begin(past, emitted.at[tick - 1], sem.at[1])
    fetch(tick, min(tick, 1), section[0], stems, got, newest, sem.at[0]).wait()
    first[...] = separable(newest, table, highs, lows, 0) + early[...]
    second[...] = separable(first, table, highs, lows, 2) + newest[...]
    output = newest if tick == ticks - 1 else outs[1]
    output[...] = separable(second, table, highs, lows, 3) + first[...]
    store.wait()
    if tick == ticks - 1:
        begin(output, emitted.at[tick], sem.at[0]).wait()


def early_part(tick, section, stems, got, weights):
    shape = got.shape
    return call(
        functools.partial(early_kernel, tick),
        (jax.ShapeDtypeStruct(shape, F32),),
        (section, stems, got, *weights),
        [(shape, F32)],
        1,
        cost(shape, 1),
        apart=(1, 2),
    )[0]


def late_part(tick, ticks, section, stems, got, early, weights, past, emitted):
    shape = got.shape
    last = tick == ticks - 1
    whole = jax.ShapeDtypeStruct((ticks,) + shape, F32)
    operands = (section, stems, got, early, *weights, past)
    return call(
        functools.partial(late_kernel, tick, ticks),
        (whole,) if last else (whole, jax.ShapeDtypeStruct(shape, F32)),
        operands if emitted is None else operands + (emitted,),
        [(shape, F32)] * 3,
        2,
        cost(shape, 3),
        apart=(1, 2, 8),
        outs_apart=(0,),
        aliases=None if emitted is None else {8: 0},
    )


def join(key, lower, position, uppers, count, branches, block, highs, lows):
    for u in range(uppers):
        at = u * lower + ((position & (lower - 1)) ^ key)
        row = pl.multiple_of(at * count, count)
        for i in branches:
            high, low = split(block(u, i))
            highs[i, pl.ds(row, count), :] = high
            lows[i, pl.ds(row, count), :] = low


def near_kernel(keys, lower, position, *refs):
    pieces, (highs, lows, _) = refs[:-3], refs[-3:]
    for key, piece in zip(keys, pieces):
        uppers, branches, count, _ = piece.shape
        block = lambda u, i, piece=piece: piece[u, i]
        join(key, lower, position[0], uppers, count, range(branches), block, highs, lows)


def near_part(position, blocks, lower):
    uppers, branches, _, channels = blocks[0].shape
    matrices = jax.ShapeDtypeStruct((branches, channels, channels), BF16)
    return call(
        functools.partial(near_kernel, list(blocks), lower),
        (matrices, matrices),
        (position, *blocks.values()),
        [],
        1,
        pl.CostEstimate(flops=0, bytes_accessed=8 * matrices.size, transcendentals=0),
    )


def halves_kernel(x, y, *refs):
    taps, (one, two, sem) = refs[:-3], refs[-3:]
    uppers, branches, count, _ = x.shape
    half = branches // 2
    copies = []
    for u in range(uppers):
        for i in range(half):
            rows = pl.ds(i * count, count)
            n = 2 * (u * half + i)
            copies.append(begin(y.at[u, i], one.at[u, rows], sem.at[n]))
            copies.append(begin(x.at[u, half + i], two.at[u, rows], sem.at[n + 1]))
    for chip in taps:
        for out in (one, two):
            for n in range(branches):
                out[0, half * count : half * count + 9, n * LANES : (n + 1) * LANES] = chip[n]
    for copy in copies:
        copy.wait()


def halves(x, y, *taps):
    uppers, branches, count, channels = x.shape
    half = branches // 2
    out = jax.ShapeDtypeStruct((uppers, half * count + TAP_ROWS * len(taps), channels), F32)
    work = pl.CostEstimate(flops=0, bytes_accessed=4 * x.size, transcendentals=0)
    return call(halves_kernel, (out, out), (x, y, *taps), [], 2 * half * uppers, work)


def first_kernel(n_far, n_taps, lower, position, newest, pair, highs_in, lows_in, *refs):
    far, taps, refs = refs[:n_far], refs[n_far : n_far + n_taps], refs[n_far + n_taps :]
    out, highs, lows, table, earlier, first, second, sem = refs
    load = begin(pair.at[0], earlier, sem.at[0])
    branches, channels, _ = highs.shape
    half = branches // 2
    if n_taps == 1:
        table[...] = taps[0][...]
    else:
        chip = position[0] // 2
        for n in range(branches):
            table[chip, n] = taps[0][n]
            table[chip ^ 3, n] = taps[1][n]
            for j in (1, 2):
                block = far[2 * j - 2]
                row = block.shape[1] - TAP_ROWS
                table[chip ^ j, n] = block[0, row : row + 9, n * LANES : (n + 1) * LANES]
    for j, piece in enumerate(far):
        uppers = piece.shape[0]
        count = channels // (uppers * lower)
        which = range(half) if j < 2 else range(half, branches)

        def block(u, i, piece=piece, which=which, count=count):
            at = (i - which[0]) * count
            return piece[u, at : at + count, :]

        join(6 + j % 2, lower, position[0], uppers, count, which, block, highs, lows)
    first[...] = separable(newest, table, highs, lows, 0)
    load.wait()
    first[...] += separable(earlier, table, highs, lows, 1)
    second[...] = separable(first, table, highs, lows, 2) + newest[...]
    out[...] = separable(second, table, highs, lows, 3) + first[...]


def first_part(position, newest, pair, matrices, far, lower, taps):
    shape, channels = newest.shape, newest.shape[-1]
    branches = matrices[0].shape[0]
    lanes = min(LANES, channels)
    like = [jax.ShapeDtypeStruct(m.shape, m.dtype) for m in matrices]
    return call(
        functools.partial(first_kernel, len(far), len(taps), lower),
        (
            jax.ShapeDtypeStruct(shape, F32),
            *like,
            jax.ShapeDtypeStruct((channels // lanes, branches, 9, lanes), F32),
        ),
        (position, newest, pair, *matrices, *far, *taps),
        [(shape, F32)] * 3,
        1,
        cost(shape, 4),
        apart=(2,),
        aliases={3: 1, 4: 2},
    )


def doubled(x, axis, bit, dim):
    other = swap(x, axis, bit)
    upper = (lax.axis_index(axis) & bit) != 0
    return jnp.where(upper, jnp.concatenate([other, x], dim), jnp.concatenate([x, other], dim))


def near_taps(taps, axis):
    size = lax.axis_size(axis)
    branches, count, width = taps.shape
    if size == 8 and 2 * width == LANES:
        chip = doubled(taps, axis, 1, 2)
        return chip, swap(chip, axis, 6)
    if size & (size - 1):
        taps = lax.all_gather(taps, axis, axis=2, tiled=True)
    else:
        bit = 1
        while bit < size:
            taps = doubled(taps, axis, bit, 2)
            bit *= 2
    channels = taps.shape[-1]
    lanes = min(LANES, channels)
    taps = taps.reshape(branches, count, channels // lanes, lanes)
    return (taps.transpose(2, 0, 1, 3),)


def from_neighbours(shard, axis):
    shard = shard[None]
    bit = 8
    while bit < lax.axis_size(axis):
        shard = doubled(shard, axis, bit, 0)
        bit *= 2
    return shard, swap(shard, axis, 2), swap(shard, axis, 4)


def body(pair, stems, taps, matrices):
    section = lax.axis_index("section").astype(jnp.int32).reshape(1)
    position = lax.axis_index("dp").astype(jnp.int32).reshape(1)
    stems = stems[:, 0]
    ticks = stems.shape[0] + 1
    pair = pair[0, :, 0]
    newest = pair[1]
    size = lax.axis_size("dp")
    taps = near_taps(after(taps[0], section, position), "dp")
    passed_on = from_behind(after(newest, taps[0]), "section", around=True)
    if size & (size - 1) or size < 8:
        lower, far = 1, ()
        partial = near_part(position, {0: lax.all_gather(matrices[0], "dp")}, lower)
    else:
        lower = 8
        own, x, y = from_neighbours(matrices[0], "dp")
        near = {0: own, 1: swap(own, "dp", 1), 2: x, 4: y}
        one, two = halves(after(x, near[1], *taps), y, *taps[: len(taps) - 1])
        x_late, y_late, *_ = lax.optimization_barrier((x, y, one, two))
        near.update({3: swap(x_late, "dp", 1), 5: swap(y_late, "dp", 1)})
        one, two = swap(one, "dp", 2), swap(two, "dp", 4)
        partial = near_part(after(position, passed_on), near, lower)
        one, two, *_ = lax.optimization_barrier((one, two, *partial))
        far = (one, swap(one, "dp", 1), two, swap(two, "dp", 1))
    output, *weights, table = first_part(position, newest, pair, partial, far, lower, taps)
    weights = (table, *weights)
    emitted = None
    for tick in range(1, ticks):
        earlier, newest, past = passed_on, from_behind(output, "section"), output
        if tick < ticks - 1:
            passed_on = from_behind(newest, "section", 1)
        early = early_part(tick, section, stems, earlier, weights)
        emitted, *output = late_part(
            tick, ticks, section, stems, newest, early, weights, past, emitted
        )
        output = output[0] if output else None
    return emitted[None, :, None]


def solution(mesh):
    placed = (
        P("section", None, "dp", None, None, None),
        P(None, "dp", None, None, None),
        P("section", None, None, "dp"),
        P("section", None, "dp", None),
    )
    return jax.shard_map(
        body,
        mesh=mesh,
        in_specs=placed,
        out_specs=P("section", None, "dp", None, None, None),
        check_vma=False,
    )
```

profile of v0, /device:TPU:16, one launch (start us, length us, event | category | flops | bytes accessed | tf_op | source)
XLA Modules:
  0.0 103.1 jit_solution(1809549782341482722)
XLA Ops:
  0.0 1.5 %collective-permute-start.3 = (f32[1,4,64,512]{3,2,1,0:T(8,128)}, f32[1,4,64,512]{3,2,1,0:T(8,128)S(1)}, u32[]{:S(2)}, u32[]{:S(2)}) collective-permute-start(f32[1,4,64,512]{3,2,1,0:T(8,128)} %refs_0_.1), channel_id=1, source_target_pairs={{0,2},{1,3},{2,0},{3,1},{4,6},{5,7},{6,4},{7,5},{8,10},{9,11},{10,... | collective-permute-start | bytes 1572872 | tf_op jit(solution)/shard_map/ppermute | solution.py:19
  1.5 1.5 %collective-permute-start.4 = (f32[1,4,64,512]{3,2,1,0:T(8,128)}, f32[1,4,64,512]{3,2,1,0:T(8,128)S(1)}, u32[]{:S(2)}, u32[]{:S(2)}) collective-permute-start(f32[1,4,64,512]{3,2,1,0:T(8,128)} %refs_0_.1), channel_id=1, source_target_pairs={{0,4},{1,5},{2,6},{3,7},{4,0},{5,1},{6,2},{7,3},{8,12},{9,13},{10,... | collective-permute-start | bytes 1572872 | tf_op jit(solution)/shard_map/ppermute | solution.py:19
  4.0 1.0 collective-permute-done
  5.6 1.1 %slice_bitcast_fusion.newest = f32[16,16,512]{2,1,0:T(8,128)S(1)} fusion(f32[1,2,1,16,16,512]{5,4,3,2,1,0:T(8,128)} %param.4), kind=kLoop, calls=%fused_computation | loop fusion | bytes 1048576 | tf_op jit(solution)/shard_map/squeeze | solution.py:329
  6.7 1.6 %collective-permute-start.1 = (f32[16,16,512]{2,1,0:T(8,128)S(1)}, f32[16,16,512]{2,1,0:T(8,128)S(1)}, u32[]{:S(2)}, u32[]{:S(2)}) collective-permute-start(f32[16,16,512]{2,1,0:T(8,128)S(1)} %slice_bitcast_fusion.newest), channel_id=1, source_target_pairs={{0,8},{8,16},{16,24},{24,0},{1,9},{9,17},{17,25},{25,1},{2,10},{10... | collective-permute-start | bytes 1572872 | tf_op jit(solution)/shard_map/ppermute | solution.py:25
  8.3 7.3 %collective-permute-done.5.refs_5_ = f32[4,9,128]{2,1,0:T(8,128)S(1)} collective-permute-done((f32[4,9,128]{2,1,0:T(8,128)S(1)}, f32[4,9,128]{2,1,0:T(8,128)S(1)}, u32[]{:S(2)}, u32[]{:S(2)}) %collective-permute-start.5) | collective-permute-done | bytes 18464 | tf_op jit(solution)/shard_map/ppermute | solution.py:19
  15.7 1.1 %collective-permute-done.4.y.refs_3_ = f32[1,4,64,512]{3,2,1,0:T(8,128)S(1)} collective-permute-done((f32[1,4,64,512]{3,2,1,0:T(8,128)}, f32[1,4,64,512]{3,2,1,0:T(8,128)S(1)}, u32[]{:S(2)}, u32[]{:S(2)}) %collective-permute-start.4) | collective-permute-done | bytes 524320 | tf_op jit(solution)/shard_map/ppermute | solution.py:19
  18.6 1.5 %collective-permute-start.9 = (f32[1,144,512]{2,1,0:T(8,128)S(1)}, f32[1,144,512]{2,1,0:T(8,128)S(1)}, u32[]{:S(2)}, u32[]{:S(2)}) collective-permute-start(f32[1,144,512]{2,1,0:T(8,128)S(1)} %get-tuple-element.30), channel_id=1, source_target_pairs={{0,4},{1,5},{2,6},{3,7},{4,0},{5,1},{6,2},{7,3},{8,12},{9,13},{10,... | collective-permute-start | bytes 884744 | tf_op jit(solution)/shard_map/ppermute | solution.py:19
  20.9 6.1 %collective-permute-done.8.refs_0_ = f32[1,144,512]{2,1,0:T(8,128)S(1)} collective-permute-done((f32[1,144,512]{2,1,0:T(8,128)S(1)}, f32[1,144,512]{2,1,0:T(8,128)S(1)}, u32[]{:S(2)}, u32[]{:S(2)}) %collective-permute-start.8) | collective-permute-done | bytes 294944 | tf_op jit(solution)/shard_map/ppermute | solution.py:19
  27.8 1.1 %collective-permute-done.10.refs_1_ = f32[1,144,512]{2,1,0:T(8,128)S(1)} collective-permute-done((f32[1,144,512]{2,1,0:T(8,128)S(1)}, f32[1,144,512]{2,1,0:T(8,128)S(1)}, u32[]{:S(2)}, u32[]{:S(2)}) %collective-permute-start.10) | collective-permute-done | bytes 294944 | tf_op jit(solution)/shard_map/ppermute | solution.py:19
  29.3 3.2 %shard_map.48 = (f32[16,16,512]{2,1,0:T(8,128)S(1)}, bf16[4,512,512]{2,1,0:T(8,128)(2,1)S(1)}, bf16[4,512,512]{2,1,0:T(8,128)(2,1)S(1)}, f32[4,4,9,128]{3,2,1,0:T(8,128)S(1)}) custom-call(s32[1]{0:T(128)} %bitcast.2.position, f32[16,16,512]{2,1,0:T(8,128)S(1)} %slice_bitcast_fusion.newest, ...), custom_call_target="tpu_custom_call", output_to_operand_aliasing={{1}: (3, {}), {2}: (4, {})} | custom-call | flops 1610612736 | bytes 5767168 | tf_op jit(solution)/shard_map/pallas_call | solution.py:52
  32.5 3.5 %collective-permute-start.12 = (f32[16,16,512]{2,1,0:T(8,128)S(1)}, f32[16,16,512]{2,1,0:T(8,128)S(1)}, u32[]{:S(2)}, u32[]{:S(2)}) collective-permute-start(f32[16,16,512]{2,1,0:T(8,128)S(1)} %get-tuple-element.37.past), channel_id=1, source_target_pairs={{0,8},{8,16},{16,24},{1,9},{9,17},{17,25},{2,10},{10,18},{18,26},{... | collective-permute-start | bytes 1572872 | tf_op jit(solution)/shard_map/ppermute | solution.py:25
  36.9 11.5 %collective-permute-done.12.got = f32[16,16,512]{2,1,0:T(8,128)S(1)} collective-permute-done((f32[16,16,512]{2,1,0:T(8,128)S(1)}, f32[16,16,512]{2,1,0:T(8,128)S(1)}, u32[]{:S(2)}, u32[]{:S(2)}) %collective-permute-start.12) | collective-permute-done | bytes 524320 | tf_op jit(solution)/shard_map/ppermute | solution.py:25
  48.4 3.5 %collective-permute-start.14 = (f32[16,16,512]{2,1,0:T(8,128)S(1)}, f32[16,16,512]{2,1,0:T(8,128)S(1)}, u32[]{:S(2)}, u32[]{:S(2)}) collective-permute-start(f32[16,16,512]{2,1,0:T(8,128)S(1)} %collective-permute-done.12.got), channel_id=1, source_target_pairs={{8,16},{16,24},{9,17},{17,25},{10,18},{18,26},{11,19},{19,27},{12,... | collective-permute-start | bytes 1572872 | tf_op jit(solution)/shard_map/ppermute | solution.py:25
  51.8 2.4 %shard_map.50 = (f32[4,16,16,512]{3,2,1,0:T(8,128)}, f32[16,16,512]{2,1,0:T(8,128)S(1)}) custom-call(s32[1]{0:T(128)} %bitcast.section, f32[3,16,16,512]{3,2,1,0:T(8,128)S(1)} %bitcast.13, f32[16,16,512]{2,1,0:T(8,128)S(1)} %collective-permute-done.12.got, f32[16,16,512]{2,1,0:T(8,128)S(1)} %shard_map.49.early, ...), custom_call_target="tpu_custom_call" | custom-call | flops 1207959552 | bytes 4718592 | tf_op jit(solution)/shard_map/pallas_call | solution.py:52
  54.2 1.9 %collective-permute-start.13 = (f32[16,16,512]{2,1,0:T(8,128)S(1)}, f32[16,16,512]{2,1,0:T(8,128)S(1)}, u32[]{:S(2)}, u32[]{:S(2)}) collective-permute-start(f32[16,16,512]{2,1,0:T(8,128)S(1)} %get-tuple-element.41.past), channel_id=1, source_target_pairs={{0,8},{8,16},{16,24},{1,9},{9,17},{17,25},{2,10},{10,18},{18,26},{... | collective-permute-start | bytes 1572872 | tf_op jit(solution)/shard_map/ppermute | solution.py:25
  56.1 9.0 %collective-permute-done.14.got = f32[16,16,512]{2,1,0:T(8,128)S(1)} collective-permute-done((f32[16,16,512]{2,1,0:T(8,128)S(1)}, f32[16,16,512]{2,1,0:T(8,128)S(1)}, u32[]{:S(2)}, u32[]{:S(2)}) %collective-permute-start.14) | collective-permute-done | bytes 524320 | tf_op jit(solution)/shard_map/ppermute | solution.py:25
  66.0 8.6 %collective-permute-done.13.got = f32[16,16,512]{2,1,0:T(8,128)S(1)} collective-permute-done((f32[16,16,512]{2,1,0:T(8,128)S(1)}, f32[16,16,512]{2,1,0:T(8,128)S(1)}, u32[]{:S(2)}, u32[]{:S(2)}) %collective-permute-start.13) | collective-permute-done | bytes 524320 | tf_op jit(solution)/shard_map/ppermute | solution.py:25
  74.6 3.5 %collective-permute-start.16 = (f32[16,16,512]{2,1,0:T(8,128)S(1)}, f32[16,16,512]{2,1,0:T(8,128)S(1)}, u32[]{:S(2)}, u32[]{:S(2)}) collective-permute-start(f32[16,16,512]{2,1,0:T(8,128)S(1)} %collective-permute-done.13.got), channel_id=1, source_target_pairs={{8,16},{16,24},{9,17},{17,25},{10,18},{18,26},{11,19},{19,27},{12,... | collective-permute-start | bytes 1572872 | tf_op jit(solution)/shard_map/ppermute | solution.py:25
  78.1 2.4 %shard_map.52 = (f32[4,16,16,512]{3,2,1,0:T(8,128)}, f32[16,16,512]{2,1,0:T(8,128)S(1)}) custom-call(s32[1]{0:T(128)} %bitcast.section, f32[3,16,16,512]{3,2,1,0:T(8,128)S(1)} %bitcast.15, f32[16,16,512]{2,1,0:T(8,128)S(1)} %collective-permute-done.13.got, f32[16,16,512]{2,1,0:T(8,128)S(1)} %shard_map.51.early, ...), custom_call_target="tpu_custom_call", output_to_operand_aliasing={{0}: (8, {})} | custom-call | flops 1207959552 | bytes 4718592 | tf_op jit(solution)/shard_map/pallas_call | solution.py:52
  80.5 1.9 %collective-permute-start.15 = (f32[16,16,512]{2,1,0:T(8,128)S(1)}, f32[16,16,512]{2,1,0:T(8,128)S(1)}, u32[]{:S(2)}, u32[]{:S(2)}) collective-permute-start(f32[16,16,512]{2,1,0:T(8,128)S(1)} %get-tuple-element.43.past), channel_id=1, source_target_pairs={{0,8},{8,16},{16,24},{1,9},{9,17},{17,25},{2,10},{10,18},{18,26},{... | collective-permute-start | bytes 1572872 | tf_op jit(solution)/shard_map/ppermute | solution.py:25
  82.4 9.0 %collective-permute-done.16.got = f32[16,16,512]{2,1,0:T(8,128)S(1)} collective-permute-done((f32[16,16,512]{2,1,0:T(8,128)S(1)}, f32[16,16,512]{2,1,0:T(8,128)S(1)}, u32[]{:S(2)}, u32[]{:S(2)}) %collective-permute-start.16) | collective-permute-done | bytes 524320 | tf_op jit(solution)/shard_map/ppermute | solution.py:25
  92.3 7.7 %collective-permute-done.15.got = f32[16,16,512]{2,1,0:T(8,128)S(1)} collective-permute-done((f32[16,16,512]{2,1,0:T(8,128)S(1)}, f32[16,16,512]{2,1,0:T(8,128)S(1)}, u32[]{:S(2)}, u32[]{:S(2)}) %collective-permute-start.15) | collective-permute-done | bytes 524320 | tf_op jit(solution)/shard_map/ppermute | solution.py:25
  100.0 3.1 %shard_map.54 = f32[4,16,16,512]{3,2,1,0:T(8,128)} custom-call(s32[1]{0:T(128)} %bitcast.section, f32[3,16,16,512]{3,2,1,0:T(8,128)S(1)} %bitcast.17, f32[16,16,512]{2,1,0:T(8,128)S(1)} %collective-permute-done.15.got, f32[16,16,512]{2,1,0:T(8,128)S(1)} %shard_map.53.early, ...), custom_call_target="tpu_custom_call", output_to_operand_aliasing={{}: (8, {})} | custom-call | flops 1207959552 | bytes 4718592 | tf_op jit(solution)/shard_map/pallas_call | solution.py:52
  (28 shorter events, 8.1 us)
Async XLA Ops:
  0.0 20.5 %copy-start.2 = (f32[1,4,64,512]{3,2,1,0:T(8,128)S(1)}, f32[1,4,64,512]{3,2,1,0:T(8,128)}, u32[]{:S(2)}) copy-start(f32[1,4,64,512]{3,2,1,0:T(8,128)} %refs_0_.1) | copy-start | bytes 1572868
  0.0 15.6 %collective-permute-start.3 = (f32[1,4,64,512]{3,2,1,0:T(8,128)}, f32[1,4,64,512]{3,2,1,0:T(8,128)S(1)}, u32[]{:S(2)}, u32[]{:S(2)}) collective-permute-start(f32[1,4,64,512]{3,2,1,0:T(8,128)} %refs_0_.1), channel_id=1, source_target_pairs={{0,2},{1,3},{2,0},{3,1},{4,6},{5,7},{6,4},{7,5},{8,10},{9,11},{10,... | collective-permute-start | bytes 1572872 | tf_op jit(solution)/shard_map/ppermute | solution.py:19
  1.5 14.2 %collective-permute-start.2 = (f32[1,4,64,512]{3,2,1,0:T(8,128)}, f32[1,4,64,512]{3,2,1,0:T(8,128)S(1)}, u32[]{:S(2)}, u32[]{:S(2)}) collective-permute-start(f32[1,4,64,512]{3,2,1,0:T(8,128)} %refs_0_.1), channel_id=1, source_target_pairs={{0,1},{1,0},{2,3},{3,2},{4,5},{5,4},{6,7},{7,6},{8,9},{9,8},{10,11... | collective-permute-start | bytes 1572872 | tf_op jit(solution)/shard_map/ppermute | solution.py:19
  1.5 15.2 %collective-permute-start.4 = (f32[1,4,64,512]{3,2,1,0:T(8,128)}, f32[1,4,64,512]{3,2,1,0:T(8,128)S(1)}, u32[]{:S(2)}, u32[]{:S(2)}) collective-permute-start(f32[1,4,64,512]{3,2,1,0:T(8,128)} %refs_0_.1), channel_id=1, source_target_pairs={{0,4},{1,5},{2,6},{3,7},{4,0},{5,1},{6,2},{7,3},{8,12},{9,13},{10,... | collective-permute-start | bytes 1572872 | tf_op jit(solution)/shard_map/ppermute | solution.py:19
  3.7 1.2 %collective-permute-start = (f32[4,9,64]{2,1,0:T(8,128)S(1)}, f32[4,9,64]{2,1,0:T(8,128)S(1)}, u32[]{:S(2)}, u32[]{:S(2)}) collective-permute-start(f32[4,9,64]{2,1,0:T(8,128)S(1)} %bitcast.19), channel_id=1, source_target_pairs={{0,1},{1,0},{2,3},{3,2},{4,5},{5,4},{6,7},{7,6},{8,9},{9,8},{10,11... | collective-permute-start | bytes 27656 | tf_op jit(solution)/shard_map/ppermute | solution.py:19
  5.0 10.6 %collective-permute-start.5 = (f32[4,9,128]{2,1,0:T(8,128)S(1)}, f32[4,9,128]{2,1,0:T(8,128)S(1)}, u32[]{:S(2)}, u32[]{:S(2)}) collective-permute-start(f32[4,9,128]{2,1,0:T(8,128)S(1)} %maximum_select_fusion.refs_0_.refs_4_), channel_id=1, source_target_pairs={{0,6},{1,7},{2,4},{3,5},{4,2},{5,3},{6,0},{7,1},{8,14},{9,15},{10,... | collective-permute-start | bytes 55304 | tf_op jit(solution)/shard_map/ppermute | solution.py:19
  6.7 22.6 %copy-start.1 = (f32[1,2,1,16,16,512]{5,4,3,2,1,0:T(8,128)S(1)}, f32[1,2,1,16,16,512]{5,4,3,2,1,0:T(8,128)}, u32[]{:S(2)}) copy-start(f32[1,2,1,16,16,512]{5,4,3,2,1,0:T(8,128)} %param.4) | copy-start | bytes 3145732
  6.7 13.8 %collective-permute-start.1 = (f32[16,16,512]{2,1,0:T(8,128)S(1)}, f32[16,16,512]{2,1,0:T(8,128)S(1)}, u32[]{:S(2)}, u32[]{:S(2)}) collective-permute-start(f32[16,16,512]{2,1,0:T(8,128)S(1)} %slice_bitcast_fusion.newest), channel_id=1, source_target_pairs={{0,8},{8,16},{16,24},{24,0},{1,9},{9,17},{17,25},{25,1},{2,10},{10... | collective-permute-start | bytes 1572872 | tf_op jit(solution)/shard_map/ppermute | solution.py:25
  17.4 3.1 %collective-permute-start.6 = (f32[1,4,64,512]{3,2,1,0:T(8,128)S(1)}, f32[1,4,64,512]{3,2,1,0:T(8,128)S(1)}, u32[]{:S(2)}, u32[]{:S(2)}) collective-permute-start(f32[1,4,64,512]{3,2,1,0:T(8,128)S(1)} %collective-permute-done.3.x.refs_2_), channel_id=1, source_target_pairs={{0,1},{1,0},{2,3},{3,2},{4,5},{5,4},{6,7},{7,6},{8,9},{9,8},{10,11... | collective-permute-start | bytes 1572872 | tf_op jit(solution)/shard_map/ppermute | solution.py:19
  17.5 3.0 %collective-permute-start.7 = (f32[1,4,64,512]{3,2,1,0:T(8,128)S(1)}, f32[1,4,64,512]{3,2,1,0:T(8,128)S(1)}, u32[]{:S(2)}, u32[]{:S(2)}) collective-permute-start(f32[1,4,64,512]{3,2,1,0:T(8,128)S(1)} %collective-permute-done.4.y.refs_3_), channel_id=1, source_target_pairs={{0,1},{1,0},{2,3},{3,2},{4,5},{5,4},{6,7},{7,6},{8,9},{9,8},{10,11... | collective-permute-start | bytes 1572872 | tf_op jit(solution)/shard_map/ppermute | solution.py:19
  18.0 9.0 %collective-permute-start.8 = (f32[1,144,512]{2,1,0:T(8,128)S(1)}, f32[1,144,512]{2,1,0:T(8,128)S(1)}, u32[]{:S(2)}, u32[]{:S(2)}) collective-permute-start(f32[1,144,512]{2,1,0:T(8,128)S(1)} %get-tuple-element.29), channel_id=1, source_target_pairs={{0,2},{1,3},{2,0},{3,1},{4,6},{5,7},{6,4},{7,5},{8,10},{9,11},{10,... | collective-permute-start | bytes 884744 | tf_op jit(solution)/shard_map/ppermute | solution.py:19
  18.6 8.7 %collective-permute-start.9 = (f32[1,144,512]{2,1,0:T(8,128)S(1)}, f32[1,144,512]{2,1,0:T(8,128)S(1)}, u32[]{:S(2)}, u32[]{:S(2)}) collective-permute-start(f32[1,144,512]{2,1,0:T(8,128)S(1)} %get-tuple-element.30), channel_id=1, source_target_pairs={{0,4},{1,5},{2,6},{3,7},{4,0},{5,1},{6,2},{7,3},{8,12},{9,13},{10,... | collective-permute-start | bytes 884744 | tf_op jit(solution)/shard_map/ppermute | solution.py:19
  27.3 1.6 %collective-permute-start.10 = (f32[1,144,512]{2,1,0:T(8,128)S(1)}, f32[1,144,512]{2,1,0:T(8,128)S(1)}, u32[]{:S(2)}, u32[]{:S(2)}) collective-permute-start(f32[1,144,512]{2,1,0:T(8,128)S(1)} %collective-permute-done.8.refs_0_), channel_id=1, source_target_pairs={{0,1},{1,0},{2,3},{3,2},{4,5},{5,4},{6,7},{7,6},{8,9},{9,8},{10,11... | collective-permute-start | bytes 884744 | tf_op jit(solution)/shard_map/ppermute | solution.py:19
  27.3 2.0 %collective-permute-start.11 = (f32[1,144,512]{2,1,0:T(8,128)S(1)}, f32[1,144,512]{2,1,0:T(8,128)S(1)}, u32[]{:S(2)}, u32[]{:S(2)}) collective-permute-start(f32[1,144,512]{2,1,0:T(8,128)S(1)} %collective-permute-done.9.refs_2_), channel_id=1, source_target_pairs={{0,1},{1,0},{2,3},{3,2},{4,5},{5,4},{6,7},{7,6},{8,9},{9,8},{10,11... | collective-permute-start | bytes 884744 | tf_op jit(solution)/shard_map/ppermute | solution.py:19
  29.3 6.7 %copy-start = (f32[3,1,16,16,512]{4,3,2,1,0:T(8,128)S(1)}, f32[3,1,16,16,512]{4,3,2,1,0:T(8,128)}, u32[]{:S(2)}) copy-start(f32[3,1,16,16,512]{4,3,2,1,0:T(8,128)} %param.5) | copy-start | bytes 4718596
  32.5 15.9 %collective-permute-start.12 = (f32[16,16,512]{2,1,0:T(8,128)S(1)}, f32[16,16,512]{2,1,0:T(8,128)S(1)}, u32[]{:S(2)}, u32[]{:S(2)}) collective-permute-start(f32[16,16,512]{2,1,0:T(8,128)S(1)} %get-tuple-element.37.past), channel_id=1, source_target_pairs={{0,8},{8,16},{16,24},{1,9},{9,17},{17,25},{2,10},{10,18},{18,26},{... | collective-permute-start | bytes 1572872 | tf_op jit(solution)/shard_map/ppermute | solution.py:25
  48.4 16.7 %collective-permute-start.14 = (f32[16,16,512]{2,1,0:T(8,128)S(1)}, f32[16,16,512]{2,1,0:T(8,128)S(1)}, u32[]{:S(2)}, u32[]{:S(2)}) collective-permute-start(f32[16,16,512]{2,1,0:T(8,128)S(1)} %collective-permute-done.12.got), channel_id=1, source_target_pairs={{8,16},{16,24},{9,17},{17,25},{10,18},{18,26},{11,19},{19,27},{12,... | collective-permute-start | bytes 1572872 | tf_op jit(solution)/shard_map/ppermute | solution.py:25
  54.2 20.4 %collective-permute-start.13 = (f32[16,16,512]{2,1,0:T(8,128)S(1)}, f32[16,16,512]{2,1,0:T(8,128)S(1)}, u32[]{:S(2)}, u32[]{:S(2)}) collective-permute-start(f32[16,16,512]{2,1,0:T(8,128)S(1)} %get-tuple-element.41.past), channel_id=1, source_target_pairs={{0,8},{8,16},{16,24},{1,9},{9,17},{17,25},{2,10},{10,18},{18,26},{... | collective-permute-start | bytes 1572872 | tf_op jit(solution)/shard_map/ppermute | solution.py:25
  74.6 16.7 %collective-permute-start.16 = (f32[16,16,512]{2,1,0:T(8,128)S(1)}, f32[16,16,512]{2,1,0:T(8,128)S(1)}, u32[]{:S(2)}, u32[]{:S(2)}) collective-permute-start(f32[16,16,512]{2,1,0:T(8,128)S(1)} %collective-permute-done.13.got), channel_id=1, source_target_pairs={{8,16},{16,24},{9,17},{17,25},{10,18},{18,26},{11,19},{19,27},{12,... | collective-permute-start | bytes 1572872 | tf_op jit(solution)/shard_map/ppermute | solution.py:25
  80.5 19.5 %collective-permute-start.15 = (f32[16,16,512]{2,1,0:T(8,128)S(1)}, f32[16,16,512]{2,1,0:T(8,128)S(1)}, u32[]{:S(2)}, u32[]{:S(2)}) collective-permute-start(f32[16,16,512]{2,1,0:T(8,128)S(1)} %get-tuple-element.43.past), channel_id=1, source_target_pairs={{0,8},{8,16},{16,24},{1,9},{9,17},{17,25},{2,10},{10,18},{18,26},{... | collective-permute-start | bytes 1572872 | tf_op jit(solution)/shard_map/ppermute | solution.py:25
where the time goes:
time: 103 us
  waiting for transfers between devices  63.4 us (62%)
  starting transfers between devices  22.8 us (22%)
  Pallas kernels  14.8 us (14%)
  local copies, waits for them, and re-layouts  1.82 us (2%)
    ppermute x6, waiting for transfers between devices, from_behind(): lax.ppermute(x, axis, pairs + [(size - 1, 0)] * (around and size > 1))  46.2 us
    ppermute x11, waiting for transfers between devices, swap(): return lax.ppermute(x, axis, [(i, i ^ bit) for i in range(size)])  17.3 us
    ppermute x6, starting transfers between devices, from_behind(): lax.ppermute(x, axis, pairs + [(size - 1, 0)] * (around and size > 1))  15.9 us
    pallas_call x9, Pallas kernels, call(): pl.pallas_call(kernel, out_shape=outs, in_specs=[spec(x, i, apart) for i,...  14.8 us
    ppermute x11, starting transfers between devices, swap(): return lax.ppermute(x, axis, [(i, i ^ bit) for i in range(size)])  6.92 us
  transfers between devices with their start and end apart: 17, of which 13 were waited for; matrix products, arithmetic and copies ran while one was open for 2% of the time, Pallas kernels for 8%

commit v1 on v0

--- a/solution.py
+++ b/solution.py
@@ -123,29 +123,25 @@
     return pltpu.make_async_copy(got, held, sem)
 
 
-def early_kernel(tick, section, stems, got, table, highs, lows, out, held, sem):
-    fetch(tick, min(tick, 2), section[0], stems, got, held, sem.at[0]).wait()
+def early_kernel(tick, at, section, stems, got, table, highs, lows, out, held, sem):
+    fetch(tick, at, section[0], stems, got, held, sem.at[0]).wait()
     out[...] = separable(held, table, highs, lows, 1)
 
 
-def late_kernel(tick, ticks, section, stems, got, early, table, highs, lows, past, *rest):
-    outs, (newest, first, second, sem) = rest[-(6 if tick < ticks - 1 else 5) : -4], rest[-4:]
-    emitted = outs[0]
+def late_kernel(tick, at, section, stems, got, early, table, highs, lows, past, *rest):
+    emitted, out, newest, first, second, sem = rest[-6:]
     store = begin(past, emitted.at[tick - 1], sem.at[1])
-    fetch(tick, min(tick, 1), section[0], stems, got, newest, sem.at[0]).wait()
+    fetch(tick, at, section[0], stems, got, newest, sem.at[0]).wait()
     first[...] = separable(newest, table, highs, lows, 0) + early[...]
     second[...] = separable(first, table, highs, lows, 2) + newest[...]
-    output = newest if tick == ticks - 1 else outs[1]
-    output[...] = separable(second, table, highs, lows, 3) + first[...]
+    out[...] = separable(second, table, highs, lows, 3) + first[...]
     store.wait()
-    if tick == ticks - 1:
-        begin(output, emitted.at[tick], sem.at[0]).wait()
-
-
-def early_part(tick, section, stems, got, weights):
+
+
+def early_part(tick, at, section, stems, got, weights):
     shape = got.shape
     return call(
-        functools.partial(early_kernel, tick),
+        functools.partial(early_kernel, tick, at),
         (jax.ShapeDtypeStruct(shape, F32),),
         (section, stems, got, *weights),
         [(shape, F32)],
@@ -155,22 +151,60 @@
     )[0]
 
 
-def late_part(tick, ticks, section, stems, got, early, weights, past, emitted):
+def late_part(tick, at, section, stems, got, early, weights, past, emitted, weight=2):
     shape = got.shape
-    last = tick == ticks - 1
-    whole = jax.ShapeDtypeStruct((ticks,) + shape, F32)
+    whole = jax.ShapeDtypeStruct((stems.shape[0] + 1,) + shape, F32)
     operands = (section, stems, got, early, *weights, past)
     return call(
-        functools.partial(late_kernel, tick, ticks),
-        (whole,) if last else (whole, jax.ShapeDtypeStruct(shape, F32)),
+        functools.partial(late_kernel, tick, at),
+        (whole, jax.ShapeDtypeStruct(shape, F32)),
         operands if emitted is None else operands + (emitted,),
         [(shape, F32)] * 3,
         2,
-        cost(shape, 3),
+        cost(shape, 3 * weight),
         apart=(1, 2, 8),
         outs_apart=(0,),
         aliases=None if emitted is None else {8: 0},
     )
+
+
+def stem_kernel(stems, table, highs, lows, out, held, first, second, sem):
+    begin(stems.at[stems.shape[0] - 1], held, sem.at[0]).wait()
+    first[...] = separable(held, table, highs, lows, 0)
+    first[...] += separable(held, table, highs, lows, 1)
+    second[...] = separable(first, table, highs, lows, 2) + held[...]
+    out[...] = separable(second, table, highs, lows, 3) + first[...]
+
+
+def stem_part(stems, weights):
+    shape = stems.shape[1:]
+    a_map = jax.ShapeDtypeStruct(shape, F32)
+    scratch = [(shape, F32)] * 3
+    operands = (stems, *weights)
+    return call(stem_kernel, (a_map,), operands, scratch, 1, cost(shape, 4), apart=(0,))[0]
+
+
+def last_kernel(section, got, own, _, emitted, sem):
+    target = emitted.at[emitted.shape[0] - 1]
+
+    @pl.when(section[0] == 0)
+    def _():
+        begin(own, target, sem.at[0])
+
+    @pl.when(section[0] > 0)
+    def _():
+        begin(got, target, sem.at[0])
+
+    pltpu.make_async_copy(got, target, sem.at[0]).wait()
+
+
+def last_part(section, got, own, emitted):
+    whole = jax.ShapeDtypeStruct(emitted.shape, F32)
+    work = pl.CostEstimate(flops=0, bytes_accessed=8 * got.size, transcendentals=0)
+    operands = (section, got, own, emitted)
+    return call(
+        last_kernel, (whole,), operands, [], 1, work, apart=(3,), outs_apart=(0,), aliases={3: 0}
+    )[0]
 
 
 def join(key, lower, position, uppers, count, branches, block, highs, lows):
@@ -231,6 +265,82 @@
     return call(halves_kernel, (out, out), (x, y, *taps), [], 2 * half * uppers, work)
 
 
+def join_far(far, lower, position, highs, lows):
+    branches, channels, _ = highs.shape
+    half = branches // 2
+    for j, piece in enumerate(far):
+        uppers = piece.shape[0]
+        count = channels // (uppers * lower)
+        which = range(half) if j < 2 else range(half, branches)
+
+        def block(u, i, piece=piece, which=which, count=count):
+            at = (i - which[0]) * count
+            return piece[u, at : at + count, :]
+
+        join(6 + j % 2, lower, position, uppers, count, which, block, highs, lows)
+
+
+def stack_kernel(*refs):
+    pieces, (out, sem) = refs[:-2], refs[-2:]
+    copies = [begin(piece, out.at[i], sem.at[i]) for i, piece in enumerate(pieces)]
+    for copy in copies:
+        copy.wait()
+
+
+def stack(*pieces):
+    n = len(pieces)
+    out = jax.ShapeDtypeStruct((n,) + pieces[0].shape, F32)
+    work = pl.CostEstimate(flops=0, bytes_accessed=8 * n * pieces[0].size, transcendentals=0)
+    return call(stack_kernel, (out,), pieces, [], n, work, apart=range(n))[0]
+
+
+def pack_kernel(one, two, table, out, sem):
+    parts, branches, count, lanes = table.shape
+    rows = (out.shape[1] - branches * TAP_ROWS) // 2
+    copies = []
+    for i, piece in enumerate((one, two)):
+        source = piece.at[:, pl.ds(0, rows)]
+        copies.append(begin(source, out.at[:, pl.ds(i * rows, rows)], sem.at[i]))
+    for n in range(branches):
+        row = 2 * rows + n * TAP_ROWS
+        for p in range(parts):
+            out[0, row : row + count, p * lanes : (p + 1) * lanes] = table[p, n]
+    for copy in copies:
+        copy.wait()
+
+
+def pack(one, two, table, rows):
+    uppers, _, channels = one.shape
+    out = jax.ShapeDtypeStruct((uppers, 2 * rows + table.shape[1] * TAP_ROWS, channels), F32)
+    work = pl.CostEstimate(flops=0, bytes_accessed=16 * one.size, transcendentals=0)
+    return call(pack_kernel, (out,), (one, two, table), [], 2, work)[0]
+
+
+def next_kernel(lower, position, near, near_core, far, far_core, highs, lows, table, _):
+    branches, channels, _ = highs.shape
+    _, uppers, _, count, _ = near.shape
+    for core, (near_blocks, far_blocks) in enumerate(((near, far), (near_core, far_core))):
+        for j in range(3):
+            block = lambda u, i: near_blocks[j, u, i]
+            join(2 * j + core, lower, position[0], uppers, count, range(branches), block, highs, lows)
+        block = lambda u, i: far_blocks[u, i * count : (i + 1) * count, :]
+        join(6 + core, lower, position[0], uppers, count, range(branches), block, highs, lows)
+    parts, _, taps, lanes = table.shape
+    for n in range(branches):
+        row = branches * count + n * TAP_ROWS
+        for p in range(parts):
+            table[p, n] = far[0, row : row + taps, p * lanes : (p + 1) * lanes]
+
+
+def next_part(position, near, near_core, far, far_core, like, lower):
+    table, highs, lows = (jax.ShapeDtypeStruct(w.shape, w.dtype) for w in like)
+    work = pl.CostEstimate(flops=0, bytes_accessed=16 * near.size, transcendentals=0)
+    operands = (position, near, near_core, far, far_core)
+    kernel = functools.partial(next_kernel, lower)
+    highs, lows, table = call(kernel, (highs, lows, table), operands, [], 1, work)
+    return table, highs, lows
+
+
 def first_kernel(n_far, n_taps, lower, position, newest, pair, highs_in, lows_in, *refs):
     far, taps, refs = refs[:n_far], refs[n_far : n_far + n_taps], refs[n_far + n_taps :]
     out, highs, lows, table, earlier, first, second, sem = refs
@@ -248,16 +358,7 @@
                 block = far[2 * j - 2]
                 row = block.shape[1] - TAP_ROWS
                 table[chip ^ j, n] = block[0, row : row + 9, n * LANES : (n + 1) * LANES]
-    for j, piece in enumerate(far):
-        uppers = piece.shape[0]
-        count = channels // (uppers * lower)
-        which = range(half) if j < 2 else range(half, branches)
-
-        def block(u, i, piece=piece, which=which, count=count):
-            at = (i - which[0]) * count
-            return piece[u, at : at + count, :]
-
-        join(6 + j % 2, lower, position[0], uppers, count, which, block, highs, lows)
+    join_far(far, lower, position[0], highs, lows)
     first[...] = separable(newest, table, highs, lows, 0)
     load.wait()
     first[...] += separable(earlier, table, highs, lows, 1)
@@ -326,16 +427,18 @@
     stems = stems[:, 0]
     ticks = stems.shape[0] + 1
     pair = pair[0, :, 0]
+    shard = matrices[0]
     newest = pair[1]
     size = lax.axis_size("dp")
+    simple = size & (size - 1) or size < 8
+    lower = 1 if simple else 8
     taps = near_taps(after(taps[0], section, position), "dp")
     passed_on = from_behind(after(newest, taps[0]), "section", around=True)
-    if size & (size - 1) or size < 8:
-        lower, far = 1, ()
-        partial = near_part(position, {0: lax.all_gather(matrices[0], "dp")}, lower)
+    far = ()
+    if simple:
+        partial = near_part(position, {0: lax.all_gather(shard, "dp")}, lower)
     else:
-        lower = 8
-        own, x, y = from_neighbours(matrices[0], "dp")
+        own, x, y = from_neighbours(shard, "dp")
         near = {0: own, 1: swap(own, "dp", 1), 2: x, 4: y}
         one, two = halves(after(x, near[1], *taps), y, *taps[: len(taps) - 1])
         x_late, y_late, *_ = lax.optimization_barrier((x, y, one, two))
@@ -346,16 +449,40 @@
         far = (one, swap(one, "dp", 1), two, swap(two, "dp", 1))
     output, *weights, table = first_part(position, newest, pair, partial, far, lower, taps)
     weights = (table, *weights)
+
+    if simple:
+        next_shard = lax.all_gather(from_ahead(shard, "section"), "dp")
+        next_weights = (from_ahead(table, "section"), *near_part(position, {0: next_shard}, lower))
+    else:
+        near = lax.optimization_barrier((own, x, y, *partial))[:3]
+        next_near = from_ahead(stack(*near), "section")
+        rows = far[0].shape[1] - TAP_ROWS * (len(taps) - 1)
     emitted = None
-    for tick in range(1, ticks):
+    held = (1, 0, newest)
+    for tick in range(1, ticks - 1):
         earlier, newest, past = passed_on, from_behind(output, "section"), output
-        if tick < ticks - 1:
-            passed_on = from_behind(newest, "section", 1)
-        early = early_part(tick, section, stems, earlier, weights)
-        emitted, *output = late_part(
-            tick, ticks, section, stems, newest, early, weights, past, emitted
+        if tick > 1:
+            earlier = after(earlier, output)
+        passed_on = from_behind(newest, "section", 1)
+        early = early_part(tick, min(tick, 2), section, stems, earlier, weights)
+        if tick == 1 and not simple:
+            next_far = from_ahead(pack(after(far[0], early), far[2], table, rows), "section")
+        emitted, output = late_part(
+            tick, 1, section, stems, newest, early, weights, past, emitted, 12 if tick > 1 else 2
         )
-        output = output[0] if output else None
+        held = (tick, 1, newest)
+        last_early = early
+
+    if not simple:
+        next_near, next_far, _ = lax.optimization_barrier((next_near, next_far, last_early))
+        blocks = next_near, swap(next_near, "dp", 1), next_far, swap(next_far, "dp", 1)
+        next_weights = next_part(position, *blocks, weights, lower)
+    early = early_part(held[0], held[1], section, stems, held[2], next_weights)
+    emitted, ahead = late_part(
+        ticks - 1, 0, section, stems, output, early, next_weights, output, emitted
+    )
+    got = from_behind(ahead, "section")
+    emitted = last_part(section, got, stem_part(stems, weights), emitted)
     return emitted[None, :, None]
 
 

time: 103 us -> 99.2 us (0.963)
  waiting for transfers between devices: 63.4 us -> 51.7 us
  Pallas kernels: 14.8 us -> 18.7 us
  starting transfers between devices: 22.8 us -> 25.7 us
    ppermute x6 -> x5, waiting for transfers between devices: 46.2 us -> 29.4 us  [from_behind(): lax.ppermute(x, axis, pairs + [(size - 1, 0)] * (around and size > 1))]
    ppermute x0 -> x2, waiting for transfers between devices: none -> 7.17 us  [from_ahead(): lax.ppermute(x, axis, [(i + 1, i) for i in range(lax.axis_size(axis) - 1)])]
    ppermute x0 -> x2, starting transfers between devices: none -> 4.84 us  [from_ahead(): lax.ppermute(x, axis, [(i + 1, i) for i in range(lax.axis_size(axis) - 1)])]
    pallas_call x9 -> x14, Pallas kernels: 14.8 us -> 18.7 us  [call(): pl.pallas_call(kernel, out_shape=outs, in_specs=[spec(x, i, apart) for i,...]
    ppermute x6 -> x5, starting transfers between devices: 15.9 us -> 13.4 us  [from_behind(): lax.ppermute(x, axis, pairs + [(size - 1, 0)] * (around and size > 1))]
    ppermute x11 -> x13, waiting for transfers between devices: 17.3 us -> 15.2 us  [swap(): return lax.ppermute(x, axis, [(i, i ^ bit) for i in range(size)])]
    ppermute x11 -> x13, starting transfers between devices: 6.92 us -> 7.43 us  [swap(): return lax.ppermute(x, axis, [(i, i ^ bit) for i in range(size)])]
  transfers between devices with their start and end apart: 17 -> 20, of which waited for: 13 -> 14; matrix products, arithmetic and copies ran while one was open for 2% -> 2% of each run, Pallas kernels for 8% -> 14%
where the time goes in v1:
time: 99.2 us; the launch traced here: 98.4 us
  waiting for transfers between devices  51.7 us (52%)
  starting transfers between devices  25.7 us (26%)
  Pallas kernels  18.7 us (19%)
  local copies, waits for them, and re-layouts  1.82 us (2%)
    ppermute x5, waiting for transfers between devices, from_behind(): lax.ppermute(x, axis, pairs + [(size - 1, 0)] * (around and size > 1))  29.4 us
    pallas_call x14, Pallas kernels, call(): pl.pallas_call(kernel, out_shape=outs, in_specs=[spec(x, i, apart) for i,...  18.7 us
    ppermute x13, waiting for transfers between devices, swap(): return lax.ppermute(x, axis, [(i, i ^ bit) for i in range(size)])  15.2 us
    ppermute x5, starting transfers between devices, from_behind(): lax.ppermute(x, axis, pairs + [(size - 1, 0)] * (around and size > 1))  13.4 us
    ppermute x13, starting transfers between devices, swap(): return lax.ppermute(x, axis, [(i, i ^ bit) for i in range(size)])  7.43 us
    ppermute x2, waiting for transfers between devices, from_ahead(): lax.ppermute(x, axis, [(i + 1, i) for i in range(lax.axis_size(axis) - 1)])  7.17 us
    ppermute x2, starting transfers between devices, from_ahead(): lax.ppermute(x, axis, [(i + 1, i) for i in range(lax.axis_size(axis) - 1)])  4.84 us
  transfers between devices with their start and end apart: 20, of which 14 were waited for; matrix products, arithmetic and copies ran while one was open for 2% of the time, Pallas kernels for 14%

profile of v1, /device:TPU:16, one launch (start us, length us, event | category | flops | bytes accessed | tf_op | source)
XLA Modules:
  0.0 98.4 jit_solution(1060691081077842777)
XLA Ops:
  0.0 1.5 %collective-permute-start.3 = (f32[1,4,64,512]{3,2,1,0:T(8,128)}, f32[1,4,64,512]{3,2,1,0:T(8,128)S(1)}, u32[]{:S(2)}, u32[]{:S(2)}) collective-permute-start(f32[1,4,64,512]{3,2,1,0:T(8,128)} %refs_0_.2), channel_id=1, source_target_pairs={{0,2},{1,3},{2,0},{3,1},{4,6},{5,7},{6,4},{7,5},{8,10},{9,11},{10,... | collective-permute-start | bytes 1572872 | tf_op jit(solution)/shard_map/ppermute | solution.py:19
  1.5 1.5 %collective-permute-start.4 = (f32[1,4,64,512]{3,2,1,0:T(8,128)}, f32[1,4,64,512]{3,2,1,0:T(8,128)S(1)}, u32[]{:S(2)}, u32[]{:S(2)}) collective-permute-start(f32[1,4,64,512]{3,2,1,0:T(8,128)} %refs_0_.2), channel_id=1, source_target_pairs={{0,4},{1,5},{2,6},{3,7},{4,0},{5,1},{6,2},{7,3},{8,12},{9,13},{10,... | collective-permute-start | bytes 1572872 | tf_op jit(solution)/shard_map/ppermute | solution.py:19
  5.6 1.1 %slice_bitcast_fusion.newest = f32[16,16,512]{2,1,0:T(8,128)S(1)} fusion(f32[1,2,1,16,16,512]{5,4,3,2,1,0:T(8,128)} %param.4), kind=kLoop, calls=%fused_computation | loop fusion | bytes 1048576 | tf_op jit(solution)/shard_map/squeeze | solution.py:431
  6.7 1.6 %collective-permute-start.1 = (f32[16,16,512]{2,1,0:T(8,128)S(1)}, f32[16,16,512]{2,1,0:T(8,128)S(1)}, u32[]{:S(2)}, u32[]{:S(2)}) collective-permute-start(f32[16,16,512]{2,1,0:T(8,128)S(1)} %slice_bitcast_fusion.newest), channel_id=1, source_target_pairs={{0,8},{8,16},{16,24},{24,0},{1,9},{9,17},{17,25},{25,1},{2,10},{10... | collective-permute-start | bytes 1572872 | tf_op jit(solution)/shard_map/ppermute | solution.py:25
  8.3 7.3 %collective-permute-done.5.refs_5_ = f32[4,9,128]{2,1,0:T(8,128)S(1)} collective-permute-done((f32[4,9,128]{2,1,0:T(8,128)S(1)}, f32[4,9,128]{2,1,0:T(8,128)S(1)}, u32[]{:S(2)}, u32[]{:S(2)}) %collective-permute-start.5) | collective-permute-done | bytes 18464 | tf_op jit(solution)/shard_map/ppermute | solution.py:19
  15.7 1.1 %collective-permute-done.4.y.refs_3_.refs_2_ = f32[1,4,64,512]{3,2,1,0:T(8,128)S(1)} collective-permute-done((f32[1,4,64,512]{3,2,1,0:T(8,128)}, f32[1,4,64,512]{3,2,1,0:T(8,128)S(1)}, u32[]{:S(2)}, u32[]{:S(2)}) %collective-permute-start.4) | collective-permute-done | bytes 524320 | tf_op jit(solution)/shard_map/ppermute | solution.py:19
  18.6 1.5 %collective-permute-start.9 = (f32[1,144,512]{2,1,0:T(8,128)S(1)}, f32[1,144,512]{2,1,0:T(8,128)S(1)}, u32[]{:S(2)}, u32[]{:S(2)}) collective-permute-start(f32[1,144,512]{2,1,0:T(8,128)S(1)} %get-tuple-element.42), channel_id=1, source_target_pairs={{0,4},{1,5},{2,6},{3,7},{4,0},{5,1},{6,2},{7,3},{8,12},{9,13},{10,... | collective-permute-start | bytes 884744 | tf_op jit(solution)/shard_map/ppermute | solution.py:19
  21.1 2.5 %collective-permute-start.15 = (f32[3,1,4,64,512]{4,3,2,1,0:T(8,128)S(1)}, f32[3,1,4,64,512]{4,3,2,1,0:T(8,128)S(1)}, u32[]{:S(2)}, u32[]{:S(2)}) collective-permute-start(f32[3,1,4,64,512]{4,3,2,1,0:T(8,128)S(1)} %shard_map.53), channel_id=1, source_target_pairs={{8,0},{16,8},{24,16},{9,1},{17,9},{25,17},{10,2},{18,10},{26,18},{... | collective-permute-start | bytes 4718600 | tf_op jit(solution)/shard_map/ppermute | solution.py:29
  23.6 3.5 %collective-permute-done.8.refs_0_.one = f32[1,144,512]{2,1,0:T(8,128)S(1)} collective-permute-done((f32[1,144,512]{2,1,0:T(8,128)S(1)}, f32[1,144,512]{2,1,0:T(8,128)S(1)}, u32[]{:S(2)}, u32[]{:S(2)}) %collective-permute-start.8) | collective-permute-done | bytes 294944 | tf_op jit(solution)/shard_map/ppermute | solution.py:19
  27.8 1.1 %collective-permute-done.10.refs_1_ = f32[1,144,512]{2,1,0:T(8,128)S(1)} collective-permute-done((f32[1,144,512]{2,1,0:T(8,128)S(1)}, f32[1,144,512]{2,1,0:T(8,128)S(1)}, u32[]{:S(2)}, u32[]{:S(2)}) %collective-permute-start.10) | collective-permute-done | bytes 294944 | tf_op jit(solution)/shard_map/ppermute | solution.py:19
  29.3 3.2 %shard_map.48 = (f32[16,16,512]{2,1,0:T(8,128)S(1)}, bf16[4,512,512]{2,1,0:T(8,128)(2,1)S(1)}, bf16[4,512,512]{2,1,0:T(8,128)(2,1)S(1)}, f32[4,4,9,128]{3,2,1,0:T(8,128)S(1)}) custom-call(s32[1]{0:T(128)} %bitcast.2.position, f32[16,16,512]{2,1,0:T(8,128)S(1)} %slice_bitcast_fusion.newest, ...), custom_call_target="tpu_custom_call", output_to_operand_aliasing={{1}: (3, {}), {2}: (4, {})} | custom-call | flops 1610612736 | bytes 5767168 | tf_op jit(solution)/shard_map/pallas_call | solution.py:52
  32.5 3.5 %collective-permute-start.12 = (f32[16,16,512]{2,1,0:T(8,128)S(1)}, f32[16,16,512]{2,1,0:T(8,128)S(1)}, u32[]{:S(2)}, u32[]{:S(2)}) collective-permute-start(f32[16,16,512]{2,1,0:T(8,128)S(1)} %get-tuple-element.49.past), channel_id=1, source_target_pairs={{0,8},{8,16},{16,24},{1,9},{9,17},{17,25},{2,10},{10,18},{18,26},{... | collective-permute-start | bytes 1572872 | tf_op jit(solution)/shard_map/ppermute | solution.py:25
  37.0 2.4 %collective-permute-start.16 = (f32[1,320,512]{2,1,0:T(8,128)S(1)}, f32[1,320,512]{2,1,0:T(8,128)S(1)}, u32[]{:S(2)}, u32[]{:S(2)}) collective-permute-start(f32[1,320,512]{2,1,0:T(8,128)S(1)} %shard_map.54), channel_id=1, source_target_pairs={{8,0},{16,8},{24,16},{9,1},{17,9},{25,17},{10,2},{18,10},{26,18},{... | collective-permute-start | bytes 1966088 | tf_op jit(solution)/shard_map/ppermute | solution.py:29
  39.4 9.0 %collective-permute-done.12.got = f32[16,16,512]{2,1,0:T(8,128)S(1)} collective-permute-done((f32[16,16,512]{2,1,0:T(8,128)S(1)}, f32[16,16,512]{2,1,0:T(8,128)S(1)}, u32[]{:S(2)}, u32[]{:S(2)}) %collective-permute-start.12) | collective-permute-done | bytes 524320 | tf_op jit(solution)/shard_map/ppermute | solution.py:25
  48.4 3.5 %collective-permute-start.14 = (f32[16,16,512]{2,1,0:T(8,128)S(1)}, f32[16,16,512]{2,1,0:T(8,128)S(1)}, u32[]{:S(2)}, u32[]{:S(2)}) collective-permute-start(f32[16,16,512]{2,1,0:T(8,128)S(1)} %collective-permute-done.12.got), channel_id=1, source_target_pairs={{8,16},{16,24},{9,17},{17,25},{10,18},{18,26},{11,19},{19,27},{12,... | collective-permute-start | bytes 1572872 | tf_op jit(solution)/shard_map/ppermute | solution.py:25
  51.9 2.4 %shard_map.50 = (f32[4,16,16,512]{3,2,1,0:T(8,128)}, f32[16,16,512]{2,1,0:T(8,128)S(1)}) custom-call(s32[1]{0:T(128)} %bitcast.section, f32[3,16,16,512]{3,2,1,0:T(8,128)S(1)} %bitcast.13, f32[16,16,512]{2,1,0:T(8,128)S(1)} %collective-permute-done.12.got, f32[16,16,512]{2,1,0:T(8,128)S(1)} %shard_map.49.early, ...), custom_call_target="tpu_custom_call" | custom-call | flops 2415919104 | bytes 7864320 | tf_op jit(solution)/shard_map/pallas_call | solution.py:52
  54.2 1.9 %collective-permute-start.13 = (f32[16,16,512]{2,1,0:T(8,128)S(1)}, f32[16,16,512]{2,1,0:T(8,128)S(1)}, u32[]{:S(2)}, u32[]{:S(2)}) collective-permute-start(f32[16,16,512]{2,1,0:T(8,128)S(1)} %get-tuple-element.53.past), channel_id=1, source_target_pairs={{0,8},{8,16},{16,24},{1,9},{9,17},{17,25},{2,10},{10,18},{18,26},{... | collective-permute-start | bytes 1572872 | tf_op jit(solution)/shard_map/ppermute | solution.py:25
  56.2 9.0 %collective-permute-done.14.got = f32[16,16,512]{2,1,0:T(8,128)S(1)} collective-permute-done((f32[16,16,512]{2,1,0:T(8,128)S(1)}, f32[16,16,512]{2,1,0:T(8,128)S(1)}, u32[]{:S(2)}, u32[]{:S(2)}) %collective-permute-start.14) | collective-permute-done | bytes 524320 | tf_op jit(solution)/shard_map/ppermute | solution.py:25
  66.1 7.2 %collective-permute-done.16.far = f32[1,320,512]{2,1,0:T(8,128)S(1)} collective-permute-done((f32[1,320,512]{2,1,0:T(8,128)S(1)}, f32[1,320,512]{2,1,0:T(8,128)S(1)}, u32[]{:S(2)}, u32[]{:S(2)}) %collective-permute-start.16) | collective-permute-done | bytes 655392 | tf_op jit(solution)/shard_map/ppermute | solution.py:29
  74.7 2.3 %shard_map.52 = (f32[4,16,16,512]{3,2,1,0:T(8,128)}, f32[16,16,512]{2,1,0:T(8,128)S(1)}) custom-call(s32[1]{0:T(128)} %bitcast.section, f32[3,16,16,512]{3,2,1,0:T(8,128)S(1)} %bitcast.15, f32[16,16,512]{2,1,0:T(8,128)S(1)} %collective-permute-done.13.got, f32[16,16,512]{2,1,0:T(8,128)S(1)} %shard_map.51.early, ...), custom_call_target="tpu_custom_call", output_to_operand_aliasing={{0}: (8, {})} | custom-call | flops 14495514624 | bytes 39321600 | tf_op jit(solution)/shard_map/pallas_call | solution.py:52
  79.0 2.5 %shard_map.57 = (f32[4,16,16,512]{3,2,1,0:T(8,128)}, f32[16,16,512]{2,1,0:T(8,128)S(1)}) custom-call(s32[1]{0:T(128)} %bitcast.section, f32[3,16,16,512]{3,2,1,0:T(8,128)S(1)} %bitcast.17, f32[16,16,512]{2,1,0:T(8,128)S(1)} %get-tuple-element.56.got.past, f32[16,16,512]{2,1,0:T(8,128)S(1)} %shard_map.56.early, ...), custom_call_target="tpu_custom_call", output_to_operand_aliasing={{0}: (8, {})} | custom-call | flops 2415919104 | bytes 7864320 | tf_op jit(solution)/shard_map/pallas_call | solution.py:52
  81.5 2.9 %collective-permute-start.19 = (f32[16,16,512]{2,1,0:T(8,128)S(1)}, f32[16,16,512]{2,1,0:T(8,128)S(1)}, u32[]{:S(2)}, u32[]{:S(2)}) collective-permute-start(f32[16,16,512]{2,1,0:T(8,128)S(1)} %get-tuple-element.67), channel_id=1, source_target_pairs={{0,8},{8,16},{16,24},{1,9},{9,17},{17,25},{2,10},{10,18},{18,26},{... | collective-permute-start | bytes 1572872 | tf_op jit(solution)/shard_map/ppermute | solution.py:25
  84.4 2.9 %shard_map.58.own = f32[16,16,512]{2,1,0:T(8,128)S(1)} custom-call(f32[3,16,16,512]{3,2,1,0:T(8,128)S(1)} %bitcast.18, f32[4,4,9,128]{3,2,1,0:T(8,128)S(1)} %get-tuple-element.50.table, bf16[4,512,512]{2,1,0:T(8,128)(2,1)S(1)} %get-tuple-element.51.highs, bf16[4,512,512]{2,1,0:T(8,128)(2,1)S(1)} %get-tuple-element.52.lows), custom_call_target="tpu_custom_call" | custom-call | flops 1610612736 | bytes 5767168 | tf_op jit(solution)/shard_map/pallas_call | solution.py:52
  87.4 10.0 %collective-permute-done.19.got = f32[16,16,512]{2,1,0:T(8,128)S(1)} collective-permute-done((f32[16,16,512]{2,1,0:T(8,128)S(1)}, f32[16,16,512]{2,1,0:T(8,128)S(1)}, u32[]{:S(2)}, u32[]{:S(2)}) %collective-permute-start.19) | collective-permute-done | bytes 524320 | tf_op jit(solution)/shard_map/ppermute | solution.py:25
  (39 shorter events, 12.6 us)
Async XLA Ops:
  0.0 20.5 %copy-start.2 = (f32[1,4,64,512]{3,2,1,0:T(8,128)S(1)}, f32[1,4,64,512]{3,2,1,0:T(8,128)}, u32[]{:S(2)}) copy-start(f32[1,4,64,512]{3,2,1,0:T(8,128)} %refs_0_.2) | copy-start | bytes 1572868
  0.0 15.6 %collective-permute-start.3 = (f32[1,4,64,512]{3,2,1,0:T(8,128)}, f32[1,4,64,512]{3,2,1,0:T(8,128)S(1)}, u32[]{:S(2)}, u32[]{:S(2)}) collective-permute-start(f32[1,4,64,512]{3,2,1,0:T(8,128)} %refs_0_.2), channel_id=1, source_target_pairs={{0,2},{1,3},{2,0},{3,1},{4,6},{5,7},{6,4},{7,5},{8,10},{9,11},{10,... | collective-permute-start | bytes 1572872 | tf_op jit(solution)/shard_map/ppermute | solution.py:19
  1.5 14.2 %collective-permute-start.2 = (f32[1,4,64,512]{3,2,1,0:T(8,128)}, f32[1,4,64,512]{3,2,1,0:T(8,128)S(1)}, u32[]{:S(2)}, u32[]{:S(2)}) collective-permute-start(f32[1,4,64,512]{3,2,1,0:T(8,128)} %refs_0_.2), channel_id=1, source_target_pairs={{0,1},{1,0},{2,3},{3,2},{4,5},{5,4},{6,7},{7,6},{8,9},{9,8},{10,11... | collective-permute-start | bytes 1572872 | tf_op jit(solution)/shard_map/ppermute | solution.py:19
  1.5 15.2 %collective-permute-start.4 = (f32[1,4,64,512]{3,2,1,0:T(8,128)}, f32[1,4,64,512]{3,2,1,0:T(8,128)S(1)}, u32[]{:S(2)}, u32[]{:S(2)}) collective-permute-start(f32[1,4,64,512]{3,2,1,0:T(8,128)} %refs_0_.2), channel_id=1, source_target_pairs={{0,4},{1,5},{2,6},{3,7},{4,0},{5,1},{6,2},{7,3},{8,12},{9,13},{10,... | collective-permute-start | bytes 1572872 | tf_op jit(solution)/shard_map/ppermute | solution.py:19
  3.7 1.2 %collective-permute-start = (f32[4,9,64]{2,1,0:T(8,128)S(1)}, f32[4,9,64]{2,1,0:T(8,128)S(1)}, u32[]{:S(2)}, u32[]{:S(2)}) collective-permute-start(f32[4,9,64]{2,1,0:T(8,128)S(1)} %bitcast.20), channel_id=1, source_target_pairs={{0,1},{1,0},{2,3},{3,2},{4,5},{5,4},{6,7},{7,6},{8,9},{9,8},{10,11... | collective-permute-start | bytes 27656 | tf_op jit(solution)/shard_map/ppermute | solution.py:19
  5.0 10.6 %collective-permute-start.5 = (f32[4,9,128]{2,1,0:T(8,128)S(1)}, f32[4,9,128]{2,1,0:T(8,128)S(1)}, u32[]{:S(2)}, u32[]{:S(2)}) collective-permute-start(f32[4,9,128]{2,1,0:T(8,128)S(1)} %maximum_select_fusion.refs_0_.refs_4_), channel_id=1, source_target_pairs={{0,6},{1,7},{2,4},{3,5},{4,2},{5,3},{6,0},{7,1},{8,14},{9,15},{10,... | collective-permute-start | bytes 55304 | tf_op jit(solution)/shard_map/ppermute | solution.py:19
  6.7 13.8 %collective-permute-start.1 = (f32[16,16,512]{2,1,0:T(8,128)S(1)}, f32[16,16,512]{2,1,0:T(8,128)S(1)}, u32[]{:S(2)}, u32[]{:S(2)}) collective-permute-start(f32[16,16,512]{2,1,0:T(8,128)S(1)} %slice_bitcast_fusion.newest), channel_id=1, source_target_pairs={{0,8},{8,16},{16,24},{24,0},{1,9},{9,17},{17,25},{25,1},{2,10},{10... | collective-permute-start | bytes 1572872 | tf_op jit(solution)/shard_map/ppermute | solution.py:25
  17.4 3.1 %collective-permute-start.6 = (f32[1,4,64,512]{3,2,1,0:T(8,128)S(1)}, f32[1,4,64,512]{3,2,1,0:T(8,128)S(1)}, u32[]{:S(2)}, u32[]{:S(2)}) collective-permute-start(f32[1,4,64,512]{3,2,1,0:T(8,128)S(1)} %collective-permute-done.3.x.refs_2_.refs_1_), channel_id=1, source_target_pairs={{0,1},{1,0},{2,3},{3,2},{4,5},{5,4},{6,7},{7,6},{8,9},{9,8},{10,11... | collective-permute-start | bytes 1572872 | tf_op jit(solution)/shard_map/ppermute | solution.py:19
  17.5 3.0 %collective-permute-start.7 = (f32[1,4,64,512]{3,2,1,0:T(8,128)S(1)}, f32[1,4,64,512]{3,2,1,0:T(8,128)S(1)}, u32[]{:S(2)}, u32[]{:S(2)}) collective-permute-start(f32[1,4,64,512]{3,2,1,0:T(8,128)S(1)} %collective-permute-done.4.y.refs_3_.refs_2_), channel_id=1, source_target_pairs={{0,1},{1,0},{2,3},{3,2},{4,5},{5,4},{6,7},{7,6},{8,9},{9,8},{10,11... | collective-permute-start | bytes 1572872 | tf_op jit(solution)/shard_map/ppermute | solution.py:19
  18.0 9.0 %collective-permute-start.8 = (f32[1,144,512]{2,1,0:T(8,128)S(1)}, f32[1,144,512]{2,1,0:T(8,128)S(1)}, u32[]{:S(2)}, u32[]{:S(2)}) collective-permute-start(f32[1,144,512]{2,1,0:T(8,128)S(1)} %get-tuple-element.41), channel_id=1, source_target_pairs={{0,2},{1,3},{2,0},{3,1},{4,6},{5,7},{6,4},{7,5},{8,10},{9,11},{10,... | collective-permute-start | bytes 884744 | tf_op jit(solution)/shard_map/ppermute | solution.py:19
  18.6 8.7 %collective-permute-start.9 = (f32[1,144,512]{2,1,0:T(8,128)S(1)}, f32[1,144,512]{2,1,0:T(8,128)S(1)}, u32[]{:S(2)}, u32[]{:S(2)}) collective-permute-start(f32[1,144,512]{2,1,0:T(8,128)S(1)} %get-tuple-element.42), channel_id=1, source_target_pairs={{0,4},{1,5},{2,6},{3,7},{4,0},{5,1},{6,2},{7,3},{8,12},{9,13},{10,... | collective-permute-start | bytes 884744 | tf_op jit(solution)/shard_map/ppermute | solution.py:19
  20.9 8.4 %copy-start.1 = (f32[1,2,1,16,16,512]{5,4,3,2,1,0:T(8,128)S(1)}, f32[1,2,1,16,16,512]{5,4,3,2,1,0:T(8,128)}, u32[]{:S(2)}) copy-start(f32[1,2,1,16,16,512]{5,4,3,2,1,0:T(8,128)} %param.4) | copy-start | bytes 3145732
  21.1 52.2 %collective-permute-start.15 = (f32[3,1,4,64,512]{4,3,2,1,0:T(8,128)S(1)}, f32[3,1,4,64,512]{4,3,2,1,0:T(8,128)S(1)}, u32[]{:S(2)}, u32[]{:S(2)}) collective-permute-start(f32[3,1,4,64,512]{4,3,2,1,0:T(8,128)S(1)} %shard_map.53), channel_id=1, source_target_pairs={{8,0},{16,8},{24,16},{9,1},{17,9},{25,17},{10,2},{18,10},{26,18},{... | collective-permute-start | bytes 4718600 | tf_op jit(solution)/shard_map/ppermute | solution.py:29
  27.3 1.6 %collective-permute-start.10 = (f32[1,144,512]{2,1,0:T(8,128)S(1)}, f32[1,144,512]{2,1,0:T(8,128)S(1)}, u32[]{:S(2)}, u32[]{:S(2)}) collective-permute-start(f32[1,144,512]{2,1,0:T(8,128)S(1)} %collective-permute-done.8.refs_0_.one), channel_id=1, source_target_pairs={{0,1},{1,0},{2,3},{3,2},{4,5},{5,4},{6,7},{7,6},{8,9},{9,8},{10,11... | collective-permute-start | bytes 884744 | tf_op jit(solution)/shard_map/ppermute | solution.py:19
  27.3 2.0 %collective-permute-start.11 = (f32[1,144,512]{2,1,0:T(8,128)S(1)}, f32[1,144,512]{2,1,0:T(8,128)S(1)}, u32[]{:S(2)}, u32[]{:S(2)}) collective-permute-start(f32[1,144,512]{2,1,0:T(8,128)S(1)} %collective-permute-done.9.refs_2_.two), channel_id=1, source_target_pairs={{0,1},{1,0},{2,3},{3,2},{4,5},{5,4},{6,7},{7,6},{8,9},{9,8},{10,11... | collective-permute-start | bytes 884744 | tf_op jit(solution)/shard_map/ppermute | solution.py:19
  29.3 6.8 %copy-start = (f32[3,1,16,16,512]{4,3,2,1,0:T(8,128)S(1)}, f32[3,1,16,16,512]{4,3,2,1,0:T(8,128)}, u32[]{:S(2)}) copy-start(f32[3,1,16,16,512]{4,3,2,1,0:T(8,128)} %param.5) | copy-start | bytes 4718596
  32.5 15.9 %collective-permute-start.12 = (f32[16,16,512]{2,1,0:T(8,128)S(1)}, f32[16,16,512]{2,1,0:T(8,128)S(1)}, u32[]{:S(2)}, u32[]{:S(2)}) collective-permute-start(f32[16,16,512]{2,1,0:T(8,128)S(1)} %get-tuple-element.49.past), channel_id=1, source_target_pairs={{0,8},{8,16},{16,24},{1,9},{9,17},{17,25},{2,10},{10,18},{18,26},{... | collective-permute-start | bytes 1572872 | tf_op jit(solution)/shard_map/ppermute | solution.py:25
  37.0 36.2 %collective-permute-start.16 = (f32[1,320,512]{2,1,0:T(8,128)S(1)}, f32[1,320,512]{2,1,0:T(8,128)S(1)}, u32[]{:S(2)}, u32[]{:S(2)}) collective-permute-start(f32[1,320,512]{2,1,0:T(8,128)S(1)} %shard_map.54), channel_id=1, source_target_pairs={{8,0},{16,8},{24,16},{9,1},{17,9},{25,17},{10,2},{18,10},{26,18},{... | collective-permute-start | bytes 1966088 | tf_op jit(solution)/shard_map/ppermute | solution.py:29
  48.4 16.7 %collective-permute-start.14 = (f32[16,16,512]{2,1,0:T(8,128)S(1)}, f32[16,16,512]{2,1,0:T(8,128)S(1)}, u32[]{:S(2)}, u32[]{:S(2)}) collective-permute-start(f32[16,16,512]{2,1,0:T(8,128)S(1)} %collective-permute-done.12.got), channel_id=1, source_target_pairs={{8,16},{16,24},{9,17},{17,25},{10,18},{18,26},{11,19},{19,27},{12,... | collective-permute-start | bytes 1572872 | tf_op jit(solution)/shard_map/ppermute | solution.py:25
  54.2 20.4 %collective-permute-start.13 = (f32[16,16,512]{2,1,0:T(8,128)S(1)}, f32[16,16,512]{2,1,0:T(8,128)S(1)}, u32[]{:S(2)}, u32[]{:S(2)}) collective-permute-start(f32[16,16,512]{2,1,0:T(8,128)S(1)} %get-tuple-element.53.past), channel_id=1, source_target_pairs={{0,8},{8,16},{16,24},{1,9},{9,17},{17,25},{2,10},{10,18},{18,26},{... | collective-permute-start | bytes 1572872 | tf_op jit(solution)/shard_map/ppermute | solution.py:25
  73.2 4.4 %collective-permute-start.17 = (f32[3,1,4,64,512]{4,3,2,1,0:T(8,128)S(1)}, f32[3,1,4,64,512]{4,3,2,1,0:T(8,128)S(1)}, u32[]{:S(2)}, u32[]{:S(2)}) collective-permute-start(f32[3,1,4,64,512]{4,3,2,1,0:T(8,128)S(1)} %collective-permute-done.15.near), channel_id=1, source_target_pairs={{0,1},{1,0},{2,3},{3,2},{4,5},{5,4},{6,7},{7,6},{8,9},{9,8},{10,11... | collective-permute-start | bytes 4718600 | tf_op jit(solution)/shard_map/ppermute | solution.py:19
  73.2 4.3 %collective-permute-start.18 = (f32[1,320,512]{2,1,0:T(8,128)S(1)}, f32[1,320,512]{2,1,0:T(8,128)S(1)}, u32[]{:S(2)}, u32[]{:S(2)}) collective-permute-start(f32[1,320,512]{2,1,0:T(8,128)S(1)} %collective-permute-done.16.far), channel_id=1, source_target_pairs={{0,1},{1,0},{2,3},{3,2},{4,5},{5,4},{6,7},{7,6},{8,9},{9,8},{10,11... | collective-permute-start | bytes 1966088 | tf_op jit(solution)/shard_map/ppermute | solution.py:19
  81.5 15.9 %collective-permute-start.19 = (f32[16,16,512]{2,1,0:T(8,128)S(1)}, f32[16,16,512]{2,1,0:T(8,128)S(1)}, u32[]{:S(2)}, u32[]{:S(2)}) collective-permute-start(f32[16,16,512]{2,1,0:T(8,128)S(1)} %get-tuple-element.67), channel_id=1, source_target_pairs={{0,8},{8,16},{16,24},{1,9},{9,17},{17,25},{2,10},{10,18},{18,26},{... | collective-permute-start | bytes 1572872 | tf_op jit(solution)/shard_map/ppermute | solution.py:25

commit v2 on v1

--- a/solution.py
+++ b/solution.py
@@ -102,8 +102,9 @@
         low = jnp.concatenate([p[1] for p in parts], 1)
         matrix_high = highs[branch, k : k + depth, :]
         matrix_low = lows[branch, k : k + depth, :]
-        product = jnp.dot(high, matrix_high, preferred_element_type=F32)
-        product = product + jnp.dot(low, matrix_high, preferred_element_type=F32)
+        both = jnp.concatenate([high, low], 0)
+        product = jnp.dot(both, matrix_high, preferred_element_type=F32)
+        product = product[: high.shape[0]] + product[high.shape[0] :]
         product = product + jnp.dot(high, matrix_low, preferred_element_type=F32)
         total = product if total is None else total + product
     return total.reshape(source.shape)
@@ -238,31 +239,30 @@
     )
 
 
-def halves_kernel(x, y, *refs):
-    taps, (one, two, sem) = refs[:-3], refs[-3:]
-    uppers, branches, count, _ = x.shape
+def half_kernel(start, block, *refs):
+    taps, (out, sem) = refs[:-2], refs[-2:]
+    uppers, branches, count, _ = block.shape
     half = branches // 2
     copies = []
     for u in range(uppers):
         for i in range(half):
-            rows = pl.ds(i * count, count)
-            n = 2 * (u * half + i)
-            copies.append(begin(y.at[u, i], one.at[u, rows], sem.at[n]))
-            copies.append(begin(x.at[u, half + i], two.at[u, rows], sem.at[n + 1]))
-    for chip in taps:
-        for out in (one, two):
-            for n in range(branches):
-                out[0, half * count : half * count + 9, n * LANES : (n + 1) * LANES] = chip[n]
+            target = out.at[u, pl.ds(i * count, count)]
+            copies.append(begin(block.at[u, start + i], target, sem.at[u * half + i]))
+    for j, chip in enumerate(taps):
+        row = half * count + j * TAP_ROWS
+        for n in range(branches):
+            out[0, row : row + 9, n * LANES : (n + 1) * LANES] = chip[n]
     for copy in copies:
         copy.wait()
 
 
-def halves(x, y, *taps):
-    uppers, branches, count, channels = x.shape
+def half_of(block, start, *taps):
+    uppers, branches, count, channels = block.shape
     half = branches // 2
     out = jax.ShapeDtypeStruct((uppers, half * count + TAP_ROWS * len(taps), channels), F32)
-    work = pl.CostEstimate(flops=0, bytes_accessed=4 * x.size, transcendentals=0)
-    return call(halves_kernel, (out, out), (x, y, *taps), [], 2 * half * uppers, work)
+    work = pl.CostEstimate(flops=0, bytes_accessed=4 * block.size, transcendentals=0)
+    kernel = functools.partial(half_kernel, start * half)
+    return call(kernel, (out,), (block, *taps), [], half * uppers, work)[0]
 
 
 def join_far(far, lower, position, highs, lows):
@@ -294,15 +294,19 @@
     return call(stack_kernel, (out,), pieces, [], n, work, apart=range(n))[0]
 
 
+def table_rows(table):
+    return -(-table.shape[1] * table.shape[2] // 8) * 8
+
+
 def pack_kernel(one, two, table, out, sem):
     parts, branches, count, lanes = table.shape
-    rows = (out.shape[1] - branches * TAP_ROWS) // 2
+    rows = (out.shape[1] - table_rows(table)) // 2
     copies = []
     for i, piece in enumerate((one, two)):
         source = piece.at[:, pl.ds(0, rows)]
         copies.append(begin(source, out.at[:, pl.ds(i * rows, rows)], sem.at[i]))
     for n in range(branches):
-        row = 2 * rows + n * TAP_ROWS
+        row = 2 * rows + n * count
         for p in range(parts):
             out[0, row : row + count, p * lanes : (p + 1) * lanes] = table[p, n]
     for copy in copies:
@@ -311,7 +315,7 @@
 
 def pack(one, two, table, rows):
     uppers, _, channels = one.shape
-    out = jax.ShapeDtypeStruct((uppers, 2 * rows + table.shape[1] * TAP_ROWS, channels), F32)
+    out = jax.ShapeDtypeStruct((uppers, 2 * rows + table_rows(table), channels), F32)
     work = pl.CostEstimate(flops=0, bytes_accessed=16 * one.size, transcendentals=0)
     return call(pack_kernel, (out,), (one, two, table), [], 2, work)[0]
 
@@ -327,7 +331,7 @@
         join(6 + core, lower, position[0], uppers, count, range(branches), block, highs, lows)
     parts, _, taps, lanes = table.shape
     for n in range(branches):
-        row = branches * count + n * TAP_ROWS
+        row = branches * count + n * taps
         for p in range(parts):
             table[p, n] = far[0, row : row + taps, p * lanes : (p + 1) * lanes]
 
@@ -351,13 +355,13 @@
         table[...] = taps[0][...]
     else:
         chip = position[0] // 2
-        for n in range(branches):
-            table[chip, n] = taps[0][n]
-            table[chip ^ 3, n] = taps[1][n]
-            for j in (1, 2):
-                block = far[2 * j - 2]
-                row = block.shape[1] - TAP_ROWS
-                table[chip ^ j, n] = block[0, row : row + 9, n * LANES : (n + 1) * LANES]
+        below = far[2]
+        for j, part in enumerate(taps):
+            row = below.shape[1] - (n_taps - j) * TAP_ROWS
+            for n in range(branches):
+                table[chip ^ j, n] = part[n]
+                lanes = slice(n * LANES, (n + 1) * LANES)
+                table[chip ^ (j + 2), n] = below[0, row : row + 9, lanes]
     join_far(far, lower, position[0], highs, lows)
     first[...] = separable(newest, table, highs, lows, 0)
     load.wait()
@@ -398,7 +402,7 @@
     branches, count, width = taps.shape
     if size == 8 and 2 * width == LANES:
         chip = doubled(taps, axis, 1, 2)
-        return chip, swap(chip, axis, 6)
+        return chip, swap(chip, axis, 2)
     if size & (size - 1):
         taps = lax.all_gather(taps, axis, axis=2, tiled=True)
     else:
@@ -440,8 +444,9 @@
     else:
         own, x, y = from_neighbours(shard, "dp")
         near = {0: own, 1: swap(own, "dp", 1), 2: x, 4: y}
-        one, two = halves(after(x, near[1], *taps), y, *taps[: len(taps) - 1])
-        x_late, y_late, *_ = lax.optimization_barrier((x, y, one, two))
+        two = half_of(after(x, near[1]), 1, *(taps if len(taps) > 1 else ()))
+        one = half_of(y, 0)
+        x_late, y_late = after(x, two), after(y, one)
         near.update({3: swap(x_late, "dp", 1), 5: swap(y_late, "dp", 1)})
         one, two = swap(one, "dp", 2), swap(two, "dp", 4)
         partial = near_part(after(position, passed_on), near, lower)
@@ -456,7 +461,7 @@
     else:
         near = lax.optimization_barrier((own, x, y, *partial))[:3]
         next_near = from_ahead(stack(*near), "section")
-        rows = far[0].shape[1] - TAP_ROWS * (len(taps) - 1)
+        rows = far[0].shape[1]
     emitted = None
     held = (1, 0, newest)
     for tick in range(1, ticks - 1):

time: 99.2 us -> 97.8 us (0.986)
    ppermute x13, waiting for transfers between devices: 15.2 us -> 12.1 us  [swap(): return lax.ppermute(x, axis, [(i, i ^ bit) for i in range(size)])]
    ppermute x5, waiting for transfers between devices: 29.4 us -> 31.8 us  [from_behind(): lax.ppermute(x, axis, pairs + [(size - 1, 0)] * (around and size > 1))]
    pallas_call x14 -> x15, Pallas kernels: 18.7 us -> 17.9 us  [call(): pl.pallas_call(kernel, out_shape=outs, in_specs=[spec(x, i, apart) for i,...]
where the time goes in v2:
time: 97.8 us; the launch traced here: 96.8 us
  waiting for transfers between devices  51 us (52%)
  starting transfers between devices  25.7 us (26%)
  Pallas kernels  17.9 us (18%)
  local copies, waits for them, and re-layouts  1.82 us (2%)
    ppermute x5, waiting for transfers between devices, from_behind(): lax.ppermute(x, axis, pairs + [(size - 1, 0)] * (around and size > 1))  31.8 us
    pallas_call x15, Pallas kernels, call(): pl.pallas_call(kernel, out_shape=outs, in_specs=[spec(x, i, apart) for i,...  17.9 us
    ppermute x5, starting transfers between devices, from_behind(): lax.ppermute(x, axis, pairs + [(size - 1, 0)] * (around and size > 1))  13.5 us
    ppermute x13, waiting for transfers between devices, swap(): return lax.ppermute(x, axis, [(i, i ^ bit) for i in range(size)])  12.1 us
    ppermute x13, starting transfers between devices, swap(): return lax.ppermute(x, axis, [(i, i ^ bit) for i in range(size)])  7.35 us
    ppermute x2, waiting for transfers between devices, from_ahead(): lax.ppermute(x, axis, [(i + 1, i) for i in range(lax.axis_size(axis) - 1)])  7.07 us
    ppermute x2, starting transfers between devices, from_ahead(): lax.ppermute(x, axis, [(i + 1, i) for i in range(lax.axis_size(axis) - 1)])  4.85 us
  transfers between devices with their start and end apart: 20, of which 14 were waited for; matrix products, arithmetic and copies ran while one was open for 2% of the time, Pallas kernels for 14%

profile of v2, /device:TPU:16, one launch (start us, length us, event | category | flops | bytes accessed | tf_op | source)
XLA Modules:
  0.0 96.8 jit_solution(16742938492264453951)
XLA Ops:
  0.0 1.5 %collective-permute-start.4 = (f32[1,4,64,512]{3,2,1,0:T(8,128)}, f32[1,4,64,512]{3,2,1,0:T(8,128)S(1)}, u32[]{:S(2)}, u32[]{:S(2)}) collective-permute-start(f32[1,4,64,512]{3,2,1,0:T(8,128)} %refs_0_.2), channel_id=1, source_target_pairs={{0,4},{1,5},{2,6},{3,7},{4,0},{5,1},{6,2},{7,3},{8,12},{9,13},{10,... | collective-permute-start | bytes 1572872 | tf_op jit(solution)/shard_map/ppermute | solution.py:19
  1.5 1.5 %collective-permute-start.3 = (f32[1,4,64,512]{3,2,1,0:T(8,128)}, f32[1,4,64,512]{3,2,1,0:T(8,128)S(1)}, u32[]{:S(2)}, u32[]{:S(2)}) collective-permute-start(f32[1,4,64,512]{3,2,1,0:T(8,128)} %refs_0_.2), channel_id=1, source_target_pairs={{0,2},{1,3},{2,0},{3,1},{4,6},{5,7},{6,4},{7,5},{8,10},{9,11},{10,... | collective-permute-start | bytes 1572872 | tf_op jit(solution)/shard_map/ppermute | solution.py:19
  6.9 1.6 %collective-permute-start.1 = (f32[16,16,512]{2,1,0:T(8,128)S(1)}, f32[16,16,512]{2,1,0:T(8,128)S(1)}, u32[]{:S(2)}, u32[]{:S(2)}) collective-permute-start(f32[16,16,512]{2,1,0:T(8,128)S(1)} %slice_bitcast_fusion.newest), channel_id=1, source_target_pairs={{0,8},{8,16},{16,24},{24,0},{1,9},{9,17},{17,25},{25,1},{2,10},{10... | collective-permute-start | bytes 1572872 | tf_op jit(solution)/shard_map/ppermute | solution.py:25
  8.5 5.4 %collective-permute-done.4.block.refs_3_.refs_2_ = f32[1,4,64,512]{3,2,1,0:T(8,128)S(1)} collective-permute-done((f32[1,4,64,512]{3,2,1,0:T(8,128)}, f32[1,4,64,512]{3,2,1,0:T(8,128)S(1)}, u32[]{:S(2)}, u32[]{:S(2)}) %collective-permute-start.4) | collective-permute-done | bytes 524320 | tf_op jit(solution)/shard_map/ppermute | solution.py:19
  16.8 1.5 %collective-permute-start.8 = (f32[1,128,512]{2,1,0:T(8,128)S(1)}, f32[1,128,512]{2,1,0:T(8,128)S(1)}, u32[]{:S(2)}, u32[]{:S(2)}) collective-permute-start(f32[1,128,512]{2,1,0:T(8,128)S(1)} %shard_map.47), channel_id=1, source_target_pairs={{0,2},{1,3},{2,0},{3,1},{4,6},{5,7},{6,4},{7,5},{8,10},{9,11},{10,... | collective-permute-start | bytes 786440 | tf_op jit(solution)/shard_map/ppermute | solution.py:19
  18.3 2.5 %collective-permute-done.1.got = f32[16,16,512]{2,1,0:T(8,128)S(1)} collective-permute-done((f32[16,16,512]{2,1,0:T(8,128)S(1)}, f32[16,16,512]{2,1,0:T(8,128)S(1)}, u32[]{:S(2)}, u32[]{:S(2)}) %collective-permute-start.1) | collective-permute-done | bytes 524320 | tf_op jit(solution)/shard_map/ppermute | solution.py:25
  21.4 2.5 %collective-permute-start.15 = (f32[3,1,4,64,512]{4,3,2,1,0:T(8,128)S(1)}, f32[3,1,4,64,512]{4,3,2,1,0:T(8,128)S(1)}, u32[]{:S(2)}, u32[]{:S(2)}) collective-permute-start(f32[3,1,4,64,512]{4,3,2,1,0:T(8,128)S(1)} %shard_map.54), channel_id=1, source_target_pairs={{8,0},{16,8},{24,16},{9,1},{17,9},{25,17},{10,2},{18,10},{26,18},{... | collective-permute-start | bytes 4718600 | tf_op jit(solution)/shard_map/ppermute | solution.py:29
  23.9 1.3 %collective-permute-done.8.refs_0_.one = f32[1,128,512]{2,1,0:T(8,128)S(1)} collective-permute-done((f32[1,128,512]{2,1,0:T(8,128)S(1)}, f32[1,128,512]{2,1,0:T(8,128)S(1)}, u32[]{:S(2)}, u32[]{:S(2)}) %collective-permute-start.8) | collective-permute-done | bytes 262176 | tf_op jit(solution)/shard_map/ppermute | solution.py:19
  25.2 1.2 %collective-permute-done.9.refs_2_.two = f32[1,160,512]{2,1,0:T(8,128)S(1)} collective-permute-done((f32[1,160,512]{2,1,0:T(8,128)S(1)}, f32[1,160,512]{2,1,0:T(8,128)S(1)}, u32[]{:S(2)}, u32[]{:S(2)}) %collective-permute-start.9) | collective-permute-done | bytes 327712 | tf_op jit(solution)/shard_map/ppermute | solution.py:19
  26.9 1.5 %collective-permute-done.10.refs_1_ = f32[1,128,512]{2,1,0:T(8,128)S(1)} collective-permute-done((f32[1,128,512]{2,1,0:T(8,128)S(1)}, f32[1,128,512]{2,1,0:T(8,128)S(1)}, u32[]{:S(2)}, u32[]{:S(2)}) %collective-permute-start.10) | collective-permute-done | bytes 262176 | tf_op jit(solution)/shard_map/ppermute | solution.py:19
  28.4 3.0 %shard_map.49 = (f32[16,16,512]{2,1,0:T(8,128)S(1)}, bf16[4,512,512]{2,1,0:T(8,128)(2,1)S(1)}, bf16[4,512,512]{2,1,0:T(8,128)(2,1)S(1)}, f32[4,4,9,128]{3,2,1,0:T(8,128)S(1)}) custom-call(s32[1]{0:T(128)} %bitcast.2.position, f32[16,16,512]{2,1,0:T(8,128)S(1)} %slice_bitcast_fusion.newest, ...), custom_call_target="tpu_custom_call", output_to_operand_aliasing={{1}: (3, {}), {2}: (4, {})} | custom-call | flops 1610612736 | bytes 5767168 | tf_op jit(solution)/shard_map/pallas_call | solution.py:52
  31.4 3.5 %collective-permute-start.12 = (f32[16,16,512]{2,1,0:T(8,128)S(1)}, f32[16,16,512]{2,1,0:T(8,128)S(1)}, u32[]{:S(2)}, u32[]{:S(2)}) collective-permute-start(f32[16,16,512]{2,1,0:T(8,128)S(1)} %get-tuple-element.45.past), channel_id=1, source_target_pairs={{0,8},{8,16},{16,24},{1,9},{9,17},{17,25},{2,10},{10,18},{18,26},{... | collective-permute-start | bytes 1572872 | tf_op jit(solution)/shard_map/ppermute | solution.py:25
  35.9 2.4 %collective-permute-start.16 = (f32[1,296,512]{2,1,0:T(8,128)S(1)}, f32[1,296,512]{2,1,0:T(8,128)S(1)}, u32[]{:S(2)}, u32[]{:S(2)}) collective-permute-start(f32[1,296,512]{2,1,0:T(8,128)S(1)} %shard_map.55), channel_id=1, source_target_pairs={{8,0},{16,8},{24,16},{9,1},{17,9},{25,17},{10,2},{18,10},{26,18},{... | collective-permute-start | bytes 1818632 | tf_op jit(solution)/shard_map/ppermute | solution.py:29
  38.2 9.1 %collective-permute-done.12.got = f32[16,16,512]{2,1,0:T(8,128)S(1)} collective-permute-done((f32[16,16,512]{2,1,0:T(8,128)S(1)}, f32[16,16,512]{2,1,0:T(8,128)S(1)}, u32[]{:S(2)}, u32[]{:S(2)}) %collective-permute-start.12) | collective-permute-done | bytes 524320 | tf_op jit(solution)/shard_map/ppermute | solution.py:25
  47.3 3.5 %collective-permute-start.14 = (f32[16,16,512]{2,1,0:T(8,128)S(1)}, f32[16,16,512]{2,1,0:T(8,128)S(1)}, u32[]{:S(2)}, u32[]{:S(2)}) collective-permute-start(f32[16,16,512]{2,1,0:T(8,128)S(1)} %collective-permute-done.12.got), channel_id=1, source_target_pairs={{8,16},{16,24},{9,17},{17,25},{10,18},{18,26},{11,19},{19,27},{12,... | collective-permute-start | bytes 1572872 | tf_op jit(solution)/shard_map/ppermute | solution.py:25
  50.8 2.3 %shard_map.51 = (f32[4,16,16,512]{3,2,1,0:T(8,128)}, f32[16,16,512]{2,1,0:T(8,128)S(1)}) custom-call(s32[1]{0:T(128)} %bitcast.section, f32[3,16,16,512]{3,2,1,0:T(8,128)S(1)} %bitcast.13, f32[16,16,512]{2,1,0:T(8,128)S(1)} %collective-permute-done.12.got, f32[16,16,512]{2,1,0:T(8,128)S(1)} %shard_map.50.early, ...), custom_call_target="tpu_custom_call" | custom-call | flops 2415919104 | bytes 7864320 | tf_op jit(solution)/shard_map/pallas_call | solution.py:52
  53.0 1.9 %collective-permute-start.13 = (f32[16,16,512]{2,1,0:T(8,128)S(1)}, f32[16,16,512]{2,1,0:T(8,128)S(1)}, u32[]{:S(2)}, u32[]{:S(2)}) collective-permute-start(f32[16,16,512]{2,1,0:T(8,128)S(1)} %get-tuple-element.49.past), channel_id=1, source_target_pairs={{0,8},{8,16},{16,24},{1,9},{9,17},{17,25},{2,10},{10,18},{18,26},{... | collective-permute-start | bytes 1572872 | tf_op jit(solution)/shard_map/ppermute | solution.py:25
  55.0 9.1 %collective-permute-done.14.got = f32[16,16,512]{2,1,0:T(8,128)S(1)} collective-permute-done((f32[16,16,512]{2,1,0:T(8,128)S(1)}, f32[16,16,512]{2,1,0:T(8,128)S(1)}, u32[]{:S(2)}, u32[]{:S(2)}) %collective-permute-start.14) | collective-permute-done | bytes 524320 | tf_op jit(solution)/shard_map/ppermute | solution.py:25
  64.9 7.1 %collective-permute-done.16.far = f32[1,296,512]{2,1,0:T(8,128)S(1)} collective-permute-done((f32[1,296,512]{2,1,0:T(8,128)S(1)}, f32[1,296,512]{2,1,0:T(8,128)S(1)}, u32[]{:S(2)}, u32[]{:S(2)}) %collective-permute-start.16) | collective-permute-done | bytes 606240 | tf_op jit(solution)/shard_map/ppermute | solution.py:29
  73.5 2.3 %shard_map.53 = (f32[4,16,16,512]{3,2,1,0:T(8,128)}, f32[16,16,512]{2,1,0:T(8,128)S(1)}) custom-call(s32[1]{0:T(128)} %bitcast.section, f32[3,16,16,512]{3,2,1,0:T(8,128)S(1)} %bitcast.15, f32[16,16,512]{2,1,0:T(8,128)S(1)} %collective-permute-done.13.got, f32[16,16,512]{2,1,0:T(8,128)S(1)} %shard_map.52.early, ...), custom_call_target="tpu_custom_call", output_to_operand_aliasing={{0}: (8, {})} | custom-call | flops 14495514624 | bytes 39321600 | tf_op jit(solution)/shard_map/pallas_call | solution.py:52
  77.6 2.5 %shard_map.58 = (f32[4,16,16,512]{3,2,1,0:T(8,128)}, f32[16,16,512]{2,1,0:T(8,128)S(1)}) custom-call(s32[1]{0:T(128)} %bitcast.section, f32[3,16,16,512]{3,2,1,0:T(8,128)S(1)} %bitcast.17, f32[16,16,512]{2,1,0:T(8,128)S(1)} %get-tuple-element.52.got.past, f32[16,16,512]{2,1,0:T(8,128)S(1)} %shard_map.57.early, ...), custom_call_target="tpu_custom_call", output_to_operand_aliasing={{0}: (8, {})} | custom-call | flops 2415919104 | bytes 7864320 | tf_op jit(solution)/shard_map/pallas_call | solution.py:52
  80.1 3.0 %collective-permute-start.19 = (f32[16,16,512]{2,1,0:T(8,128)S(1)}, f32[16,16,512]{2,1,0:T(8,128)S(1)}, u32[]{:S(2)}, u32[]{:S(2)}) collective-permute-start(f32[16,16,512]{2,1,0:T(8,128)S(1)} %get-tuple-element.63), channel_id=1, source_target_pairs={{0,8},{8,16},{16,24},{1,9},{9,17},{17,25},{2,10},{10,18},{18,26},{... | collective-permute-start | bytes 1572872 | tf_op jit(solution)/shard_map/ppermute | solution.py:25
  83.1 2.8 %shard_map.59.own = f32[16,16,512]{2,1,0:T(8,128)S(1)} custom-call(f32[3,16,16,512]{3,2,1,0:T(8,128)S(1)} %bitcast.18, f32[4,4,9,128]{3,2,1,0:T(8,128)S(1)} %get-tuple-element.46.table, bf16[4,512,512]{2,1,0:T(8,128)(2,1)S(1)} %get-tuple-element.47.highs, bf16[4,512,512]{2,1,0:T(8,128)(2,1)S(1)} %get-tuple-element.48.lows), custom_call_target="tpu_custom_call" | custom-call | flops 1610612736 | bytes 5767168 | tf_op jit(solution)/shard_map/pallas_call | solution.py:52
  85.9 10.0 %collective-permute-done.19.got = f32[16,16,512]{2,1,0:T(8,128)S(1)} collective-permute-done((f32[16,16,512]{2,1,0:T(8,128)S(1)}, f32[16,16,512]{2,1,0:T(8,128)S(1)}, u32[]{:S(2)}, u32[]{:S(2)}) %collective-permute-start.19) | collective-permute-done | bytes 524320 | tf_op jit(solution)/shard_map/ppermute | solution.py:25
  (40 shorter events, 13.7 us)
Async XLA Ops:
  0.0 20.8 %copy-start.2 = (f32[1,4,64,512]{3,2,1,0:T(8,128)S(1)}, f32[1,4,64,512]{3,2,1,0:T(8,128)}, u32[]{:S(2)}) copy-start(f32[1,4,64,512]{3,2,1,0:T(8,128)} %refs_0_.2) | copy-start | bytes 1572868
  0.0 13.9 %collective-permute-start.4 = (f32[1,4,64,512]{3,2,1,0:T(8,128)}, f32[1,4,64,512]{3,2,1,0:T(8,128)S(1)}, u32[]{:S(2)}, u32[]{:S(2)}) collective-permute-start(f32[1,4,64,512]{3,2,1,0:T(8,128)} %refs_0_.2), channel_id=1, source_target_pairs={{0,4},{1,5},{2,6},{3,7},{4,0},{5,1},{6,2},{7,3},{8,12},{9,13},{10,... | collective-permute-start | bytes 1572872 | tf_op jit(solution)/shard_map/ppermute | solution.py:19
  1.5 13.9 %collective-permute-start.3 = (f32[1,4,64,512]{3,2,1,0:T(8,128)}, f32[1,4,64,512]{3,2,1,0:T(8,128)S(1)}, u32[]{:S(2)}, u32[]{:S(2)}) collective-permute-start(f32[1,4,64,512]{3,2,1,0:T(8,128)} %refs_0_.2), channel_id=1, source_target_pairs={{0,2},{1,3},{2,0},{3,1},{4,6},{5,7},{6,4},{7,5},{8,10},{9,11},{10,... | collective-permute-start | bytes 1572872 | tf_op jit(solution)/shard_map/ppermute | solution.py:19
  3.0 12.5 %collective-permute-start.2 = (f32[1,4,64,512]{3,2,1,0:T(8,128)}, f32[1,4,64,512]{3,2,1,0:T(8,128)S(1)}, u32[]{:S(2)}, u32[]{:S(2)}) collective-permute-start(f32[1,4,64,512]{3,2,1,0:T(8,128)} %refs_0_.2), channel_id=1, source_target_pairs={{0,1},{1,0},{2,3},{3,2},{4,5},{5,4},{6,7},{7,6},{8,9},{9,8},{10,11... | collective-permute-start | bytes 1572872 | tf_op jit(solution)/shard_map/ppermute | solution.py:19
  3.7 1.4 %collective-permute-start = (f32[4,9,64]{2,1,0:T(8,128)S(1)}, f32[4,9,64]{2,1,0:T(8,128)S(1)}, u32[]{:S(2)}, u32[]{:S(2)}) collective-permute-start(f32[4,9,64]{2,1,0:T(8,128)S(1)} %bitcast.20), channel_id=1, source_target_pairs={{0,1},{1,0},{2,3},{3,2},{4,5},{5,4},{6,7},{7,6},{8,9},{9,8},{10,11... | collective-permute-start | bytes 27656 | tf_op jit(solution)/shard_map/ppermute | solution.py:19
  5.2 10.6 %collective-permute-start.5 = (f32[4,9,128]{2,1,0:T(8,128)S(1)}, f32[4,9,128]{2,1,0:T(8,128)S(1)}, u32[]{:S(2)}, u32[]{:S(2)}) collective-permute-start(f32[4,9,128]{2,1,0:T(8,128)S(1)} %maximum_select_fusion.refs_0_.refs_4_), channel_id=1, source_target_pairs={{0,2},{1,3},{2,0},{3,1},{4,6},{5,7},{6,4},{7,5},{8,10},{9,11},{10,... | collective-permute-start | bytes 55304 | tf_op jit(solution)/shard_map/ppermute | solution.py:19
  6.9 13.9 %collective-permute-start.1 = (f32[16,16,512]{2,1,0:T(8,128)S(1)}, f32[16,16,512]{2,1,0:T(8,128)S(1)}, u32[]{:S(2)}, u32[]{:S(2)}) collective-permute-start(f32[16,16,512]{2,1,0:T(8,128)S(1)} %slice_bitcast_fusion.newest), channel_id=1, source_target_pairs={{0,8},{8,16},{16,24},{24,0},{1,9},{9,17},{17,25},{25,1},{2,10},{10... | collective-permute-start | bytes 1572872 | tf_op jit(solution)/shard_map/ppermute | solution.py:25
  14.2 6.6 %collective-permute-start.7 = (f32[1,4,64,512]{3,2,1,0:T(8,128)S(1)}, f32[1,4,64,512]{3,2,1,0:T(8,128)S(1)}, u32[]{:S(2)}, u32[]{:S(2)}) collective-permute-start(f32[1,4,64,512]{3,2,1,0:T(8,128)S(1)} %collective-permute-done.4.block.refs_3_.refs_2_), channel_id=1, source_target_pairs={{0,1},{1,0},{2,3},{3,2},{4,5},{5,4},{6,7},{7,6},{8,9},{9,8},{10,11... | collective-permute-start | bytes 1572872 | tf_op jit(solution)/shard_map/ppermute | solution.py:19
  16.2 4.7 %collective-permute-start.6 = (f32[1,4,64,512]{3,2,1,0:T(8,128)S(1)}, f32[1,4,64,512]{3,2,1,0:T(8,128)S(1)}, u32[]{:S(2)}, u32[]{:S(2)}) collective-permute-start(f32[1,4,64,512]{3,2,1,0:T(8,128)S(1)} %collective-permute-done.3.block.refs_2_.refs_1_), channel_id=1, source_target_pairs={{0,1},{1,0},{2,3},{3,2},{4,5},{5,4},{6,7},{7,6},{8,9},{9,8},{10,11... | collective-permute-start | bytes 1572872 | tf_op jit(solution)/shard_map/ppermute | solution.py:19
  16.2 10.1 %collective-permute-start.9 = (f32[1,160,512]{2,1,0:T(8,128)S(1)}, f32[1,160,512]{2,1,0:T(8,128)S(1)}, u32[]{:S(2)}, u32[]{:S(2)}) collective-permute-start(f32[1,160,512]{2,1,0:T(8,128)S(1)} %shard_map.46), channel_id=1, source_target_pairs={{0,4},{1,5},{2,6},{3,7},{4,0},{5,1},{6,2},{7,3},{8,12},{9,13},{10,... | collective-permute-start | bytes 983048 | tf_op jit(solution)/shard_map/ppermute | solution.py:19
  16.8 8.4 %collective-permute-start.8 = (f32[1,128,512]{2,1,0:T(8,128)S(1)}, f32[1,128,512]{2,1,0:T(8,128)S(1)}, u32[]{:S(2)}, u32[]{:S(2)}) collective-permute-start(f32[1,128,512]{2,1,0:T(8,128)S(1)} %shard_map.47), channel_id=1, source_target_pairs={{0,2},{1,3},{2,0},{3,1},{4,6},{5,7},{6,4},{7,5},{8,10},{9,11},{10,... | collective-permute-start | bytes 786440 | tf_op jit(solution)/shard_map/ppermute | solution.py:19
  21.2 7.1 %copy-start.1 = (f32[1,2,1,16,16,512]{5,4,3,2,1,0:T(8,128)S(1)}, f32[1,2,1,16,16,512]{5,4,3,2,1,0:T(8,128)}, u32[]{:S(2)}) copy-start(f32[1,2,1,16,16,512]{5,4,3,2,1,0:T(8,128)} %param.4) | copy-start | bytes 3145732
  21.4 50.5 %collective-permute-start.15 = (f32[3,1,4,64,512]{4,3,2,1,0:T(8,128)S(1)}, f32[3,1,4,64,512]{4,3,2,1,0:T(8,128)S(1)}, u32[]{:S(2)}, u32[]{:S(2)}) collective-permute-start(f32[3,1,4,64,512]{4,3,2,1,0:T(8,128)S(1)} %shard_map.54), channel_id=1, source_target_pairs={{8,0},{16,8},{24,16},{9,1},{17,9},{25,17},{10,2},{18,10},{26,18},{... | collective-permute-start | bytes 4718600 | tf_op jit(solution)/shard_map/ppermute | solution.py:29
  26.4 2.0 %collective-permute-start.11 = (f32[1,160,512]{2,1,0:T(8,128)S(1)}, f32[1,160,512]{2,1,0:T(8,128)S(1)}, u32[]{:S(2)}, u32[]{:S(2)}) collective-permute-start(f32[1,160,512]{2,1,0:T(8,128)S(1)} %collective-permute-done.9.refs_2_.two), channel_id=1, source_target_pairs={{0,1},{1,0},{2,3},{3,2},{4,5},{5,4},{6,7},{7,6},{8,9},{9,8},{10,11... | collective-permute-start | bytes 983048 | tf_op jit(solution)/shard_map/ppermute | solution.py:19
  26.4 2.0 %collective-permute-start.10 = (f32[1,128,512]{2,1,0:T(8,128)S(1)}, f32[1,128,512]{2,1,0:T(8,128)S(1)}, u32[]{:S(2)}, u32[]{:S(2)}) collective-permute-start(f32[1,128,512]{2,1,0:T(8,128)S(1)} %collective-permute-done.8.refs_0_.one), channel_id=1, source_target_pairs={{0,1},{1,0},{2,3},{3,2},{4,5},{5,4},{6,7},{7,6},{8,9},{9,8},{10,11... | collective-permute-start | bytes 786440 | tf_op jit(solution)/shard_map/ppermute | solution.py:19
  28.4 6.6 %copy-start = (f32[3,1,16,16,512]{4,3,2,1,0:T(8,128)S(1)}, f32[3,1,16,16,512]{4,3,2,1,0:T(8,128)}, u32[]{:S(2)}) copy-start(f32[3,1,16,16,512]{4,3,2,1,0:T(8,128)} %param.5) | copy-start | bytes 4718596
  31.4 15.9 %collective-permute-start.12 = (f32[16,16,512]{2,1,0:T(8,128)S(1)}, f32[16,16,512]{2,1,0:T(8,128)S(1)}, u32[]{:S(2)}, u32[]{:S(2)}) collective-permute-start(f32[16,16,512]{2,1,0:T(8,128)S(1)} %get-tuple-element.45.past), channel_id=1, source_target_pairs={{0,8},{8,16},{16,24},{1,9},{9,17},{17,25},{2,10},{10,18},{18,26},{... | collective-permute-start | bytes 1572872 | tf_op jit(solution)/shard_map/ppermute | solution.py:25
  35.9 36.1 %collective-permute-start.16 = (f32[1,296,512]{2,1,0:T(8,128)S(1)}, f32[1,296,512]{2,1,0:T(8,128)S(1)}, u32[]{:S(2)}, u32[]{:S(2)}) collective-permute-start(f32[1,296,512]{2,1,0:T(8,128)S(1)} %shard_map.55), channel_id=1, source_target_pairs={{8,0},{16,8},{24,16},{9,1},{17,9},{25,17},{10,2},{18,10},{26,18},{... | collective-permute-start | bytes 1818632 | tf_op jit(solution)/shard_map/ppermute | solution.py:29
  47.3 16.7 %collective-permute-start.14 = (f32[16,16,512]{2,1,0:T(8,128)S(1)}, f32[16,16,512]{2,1,0:T(8,128)S(1)}, u32[]{:S(2)}, u32[]{:S(2)}) collective-permute-start(f32[16,16,512]{2,1,0:T(8,128)S(1)} %collective-permute-done.12.got), channel_id=1, source_target_pairs={{8,16},{16,24},{9,17},{17,25},{10,18},{18,26},{11,19},{19,27},{12,... | collective-permute-start | bytes 1572872 | tf_op jit(solution)/shard_map/ppermute | solution.py:25
  53.0 20.5 %collective-permute-start.13 = (f32[16,16,512]{2,1,0:T(8,128)S(1)}, f32[16,16,512]{2,1,0:T(8,128)S(1)}, u32[]{:S(2)}, u32[]{:S(2)}) collective-permute-start(f32[16,16,512]{2,1,0:T(8,128)S(1)} %get-tuple-element.49.past), channel_id=1, source_target_pairs={{0,8},{8,16},{16,24},{1,9},{9,17},{17,25},{2,10},{10,18},{18,26},{... | collective-permute-start | bytes 1572872 | tf_op jit(solution)/shard_map/ppermute | solution.py:25
  71.9 4.3 %collective-permute-start.17 = (f32[3,1,4,64,512]{4,3,2,1,0:T(8,128)S(1)}, f32[3,1,4,64,512]{4,3,2,1,0:T(8,128)S(1)}, u32[]{:S(2)}, u32[]{:S(2)}) collective-permute-start(f32[3,1,4,64,512]{4,3,2,1,0:T(8,128)S(1)} %collective-permute-done.15.near), channel_id=1, source_target_pairs={{0,1},{1,0},{2,3},{3,2},{4,5},{5,4},{6,7},{7,6},{8,9},{9,8},{10,11... | collective-permute-start | bytes 4718600 | tf_op jit(solution)/shard_map/ppermute | solution.py:19
  71.9 4.3 %collective-permute-start.18 = (f32[1,296,512]{2,1,0:T(8,128)S(1)}, f32[1,296,512]{2,1,0:T(8,128)S(1)}, u32[]{:S(2)}, u32[]{:S(2)}) collective-permute-start(f32[1,296,512]{2,1,0:T(8,128)S(1)} %collective-permute-done.16.far), channel_id=1, source_target_pairs={{0,1},{1,0},{2,3},{3,2},{4,5},{5,4},{6,7},{7,6},{8,9},{9,8},{10,11... | collective-permute-start | bytes 1818632 | tf_op jit(solution)/shard_map/ppermute | solution.py:19
  80.1 15.8 %collective-permute-start.19 = (f32[16,16,512]{2,1,0:T(8,128)S(1)}, f32[16,16,512]{2,1,0:T(8,128)S(1)}, u32[]{:S(2)}, u32[]{:S(2)}) collective-permute-start(f32[16,16,512]{2,1,0:T(8,128)S(1)} %get-tuple-element.63), channel_id=1, source_target_pairs={{0,8},{8,16},{16,24},{1,9},{9,17},{17,25},{2,10},{10,18},{18,26},{... | collective-permute-start | bytes 1572872 | tf_op jit(solution)/shard_map/ppermute | solution.py:25

commit v3 on v2

--- a/solution.py
+++ b/solution.py
@@ -11,6 +11,7 @@
 BF16 = jnp.bfloat16
 VMEM_LIMIT = 16 * 1024 * 1024
 LANES = 128
+DEPTH = 256
 TAP_ROWS = 16
 
 
@@ -78,30 +79,37 @@
     return jnp.where(column == outside, 0.0, pltpu.roll(u, by % side, 1))
 
 
-def depthwise(source, table, branch, low, width):
-    x = jnp.maximum(source[:, :, low : low + width], 0.0)
+def depthwise(source, table, branch, part, width):
+    low = part * width
+    if not isinstance(part, int):
+        low = pl.multiple_of(low, width)
+    x = jnp.maximum(source[:, :, pl.ds(low, width)], 0.0)
     nothing = jnp.zeros((1,) + x.shape[1:], F32)
     above = jnp.concatenate([nothing, x[:-1]], 0)
     below = jnp.concatenate([x[1:], nothing], 0)
-    tap = [table[low // width, branch, k : k + 1, :].reshape(1, 1, width) for k in range(9)]
+    tap = [table[part, branch, k : k + 1, :].reshape(1, 1, width) for k in range(9)]
     by_column = [above * tap[j] + x * tap[3 + j] + below * tap[6 + j] for j in range(3)]
     return shifted(by_column[0], 1) + by_column[1] + shifted(by_column[2], -1)
 
 
-def separable(source, table, highs, lows, branch):
+def separable(source, table, highs, lows, branch, blocks=None):
     rows, columns, channels = source.shape
     width = min(LANES, channels)
-    depth = min(256, channels)
+    depth = min(DEPTH, channels)
+    each = depth // width
     total = None
-    for k in range(0, channels, depth):
-        parts = []
-        for low in range(k, k + depth, width):
-            mixed_in = depthwise(source, table, branch, low, width)
-            parts.append(split(mixed_in.reshape(rows * columns, width)))
-        high = jnp.concatenate([p[0] for p in parts], 1)
-        low = jnp.concatenate([p[1] for p in parts], 1)
-        matrix_high = highs[branch, k : k + depth, :]
-        matrix_low = lows[branch, k : k + depth, :]
+    for block in range(channels // depth) if blocks is None else blocks:
+        mixed_in = []
+        for i in range(each):
+            value = depthwise(source, table, branch, block * each + i, width)
+            mixed_in.append(split(value.reshape(rows * columns, width)))
+        high = jnp.concatenate([p[0] for p in mixed_in], 1)
+        low = jnp.concatenate([p[1] for p in mixed_in], 1)
+        k = block * depth
+        if not isinstance(block, int):
+            k = pl.multiple_of(k, depth)
+        matrix_high = highs[branch, pl.ds(k, depth), :]
+        matrix_low = lows[branch, pl.ds(k, depth), :]
         both = jnp.concatenate([high, low], 0)
         product = jnp.dot(both, matrix_high, preferred_element_type=F32)
         product = product[: high.shape[0]] + product[high.shape[0] :]
@@ -345,16 +353,42 @@
     return table, highs, lows
 
 
-def first_kernel(n_far, n_taps, lower, position, newest, pair, highs_in, lows_in, *refs):
+def ahead_kernel(position, newest, pair, highs, lows, *refs):
+    taps, (out, table, earlier, sem) = refs[:2], refs[2:]
+    load = begin(pair.at[0], earlier, sem.at[0])
+    chip = position[0] // 2
+    for j, part in enumerate(taps):
+        for n in range(part.shape[0]):
+            table[chip ^ j, n] = part[n]
+    blocks = [chip // 2]
+    total = separable(newest, table, highs, lows, 0, blocks)
+    load.wait()
+    out[...] = total + separable(earlier, table, highs, lows, 1, blocks)
+
+
+def ahead_part(position, newest, pair, matrices, taps):
+    shape, channels = newest.shape, newest.shape[-1]
+    table = (channels // LANES,) + taps[0].shape
+    return call(
+        ahead_kernel,
+        (jax.ShapeDtypeStruct(shape, F32),),
+        (position, newest, pair, *matrices, *taps),
+        [(table, F32), (shape, F32)],
+        1,
+        cost(shape, 1),
+        apart=(2,),
+    )[0]
+
+
+def first_kernel(n_far, n_taps, n_sums, lower, position, newest, pair, highs_in, lows_in, *refs):
     far, taps, refs = refs[:n_far], refs[n_far : n_far + n_taps], refs[n_far + n_taps :]
-    out, highs, lows, table, earlier, first, second, sem = refs
+    sums, (out, highs, lows, table, earlier, first, second, sem) = refs[:n_sums], refs[n_sums:]
     load = begin(pair.at[0], earlier, sem.at[0])
     branches, channels, _ = highs.shape
-    half = branches // 2
+    chip = position[0] // 2
     if n_taps == 1:
         table[...] = taps[0][...]
     else:
-        chip = position[0] // 2
         below = far[2]
         for j, part in enumerate(taps):
             row = below.shape[1] - (n_taps - j) * TAP_ROWS
@@ -363,26 +397,30 @@
                 lanes = slice(n * LANES, (n + 1) * LANES)
                 table[chip ^ (j + 2), n] = below[0, row : row + 9, lanes]
     join_far(far, lower, position[0], highs, lows)
-    first[...] = separable(newest, table, highs, lows, 0)
+    blocks = [1 - chip // 2] if sums else None
+    total = separable(newest, table, highs, lows, 0, blocks)
+    for part in sums:
+        total = total + part[...]
+    first[...] = total
     load.wait()
-    first[...] += separable(earlier, table, highs, lows, 1)
+    first[...] += separable(earlier, table, highs, lows, 1, blocks)
     second[...] = separable(first, table, highs, lows, 2) + newest[...]
     out[...] = separable(second, table, highs, lows, 3) + first[...]
 
 
-def first_part(position, newest, pair, matrices, far, lower, taps):
+def first_part(position, newest, pair, matrices, far, lower, taps, sums):
     shape, channels = newest.shape, newest.shape[-1]
     branches = matrices[0].shape[0]
     lanes = min(LANES, channels)
     like = [jax.ShapeDtypeStruct(m.shape, m.dtype) for m in matrices]
     return call(
-        functools.partial(first_kernel, len(far), len(taps), lower),
+        functools.partial(first_kernel, len(far), len(taps), len(sums), lower),
         (
             jax.ShapeDtypeStruct(shape, F32),
             *like,
             jax.ShapeDtypeStruct((channels // lanes, branches, 9, lanes), F32),
         ),
-        (position, newest, pair, *matrices, *far, *taps),
+        (position, newest, pair, *matrices, *far, *taps, *sums),
         [(shape, F32)] * 3,
         1,
         cost(shape, 4),
@@ -401,8 +439,7 @@
     size = lax.axis_size(axis)
     branches, count, width = taps.shape
     if size == 8 and 2 * width == LANES:
-        chip = doubled(taps, axis, 1, 2)
-        return chip, swap(chip, axis, 2)
+        return doubled(taps, axis, 1, 2)
     if size & (size - 1):
         taps = lax.all_gather(taps, axis, axis=2, tiled=True)
     else:
@@ -413,7 +450,7 @@
     channels = taps.shape[-1]
     lanes = min(LANES, channels)
     taps = taps.reshape(branches, count, channels // lanes, lanes)
-    return (taps.transpose(2, 0, 1, 3),)
+    return taps.transpose(2, 0, 1, 3)
 
 
 def from_neighbours(shard, axis):
@@ -437,8 +474,11 @@
     simple = size & (size - 1) or size < 8
     lower = 1 if simple else 8
     taps = near_taps(after(taps[0], section, position), "dp")
-    passed_on = from_behind(after(newest, taps[0]), "section", around=True)
-    far = ()
+    newest, taps = lax.optimization_barrier((newest, taps))
+    taps = (taps, swap(taps, "dp", 2)) if taps.ndim == 3 else (taps,)
+    passed_on = from_behind(newest, "section", around=True)
+    far = sums = ()
+    channels = newest.shape[-1]
     if simple:
         partial = near_part(position, {0: lax.all_gather(shard, "dp")}, lower)
     else:
@@ -449,10 +489,14 @@
         x_late, y_late = after(x, two), after(y, one)
         near.update({3: swap(x_late, "dp", 1), 5: swap(y_late, "dp", 1)})
         one, two = swap(one, "dp", 2), swap(two, "dp", 4)
-        partial = near_part(after(position, passed_on), near, lower)
-        one, two, *_ = lax.optimization_barrier((one, two, *partial))
+        partial = near_part(position, near, lower)
+        if len(taps) > 1 and channels == 2 * DEPTH:
+            sums = (ahead_part(after(position, passed_on), newest, pair, partial, taps),)
+        one, two, *_ = lax.optimization_barrier((one, two, passed_on, *partial, *sums))
         far = (one, swap(one, "dp", 1), two, swap(two, "dp", 1))
-    output, *weights, table = first_part(position, newest, pair, partial, far, lower, taps)
+    output, *weights, table = first_part(
+        position, newest, pair, partial, far, lower, taps, sums
+    )
     weights = (table, *weights)
 
     if simple:

time: 97.8 us -> 96.4 us (0.986)
  waiting for transfers between devices: 51 us -> 48.7 us
    ppermute x5, waiting for transfers between devices: 31.8 us -> 30.6 us  [from_behind(): lax.ppermute(x, axis, pairs + [(size - 1, 0)] * (around and size > 1))]
    pallas_call x15 -> x16, Pallas kernels: 17.9 us -> 18.2 us  [call(): pl.pallas_call(kernel, out_shape=outs, in_specs=[spec(x, i, apart) for i,...]
  transfers between devices with their start and end apart: 20 -> 20, of which waited for: 14 -> 12; matrix products, arithmetic and copies ran while one was open for 2% -> 2% of each run, Pallas kernels for 14% -> 14%
where the time goes in v3:
time: 96.4 us; the launch traced here: 95.4 us
  waiting for transfers between devices  48.7 us (51%)
  starting transfers between devices  26.1 us (27%)
  Pallas kernels  18.2 us (19%)
  local copies, waits for them, and re-layouts  1.82 us (2%)
    ppermute x5, waiting for transfers between devices, from_behind(): lax.ppermute(x, axis, pairs + [(size - 1, 0)] * (around and size > 1))  30.6 us
    pallas_call x16, Pallas kernels, call(): pl.pallas_call(kernel, out_shape=outs, in_specs=[spec(x, i, apart) for i,...  18.2 us
    ppermute x5, starting transfers between devices, from_behind(): lax.ppermute(x, axis, pairs + [(size - 1, 0)] * (around and size > 1))  14 us
    ppermute x13, waiting for transfers between devices, swap(): return lax.ppermute(x, axis, [(i, i ^ bit) for i in range(size)])  11.9 us
    ppermute x13, starting transfers between devices, swap(): return lax.ppermute(x, axis, [(i, i ^ bit) for i in range(size)])  7.35 us
    ppermute x2, waiting for transfers between devices, from_ahead(): lax.ppermute(x, axis, [(i + 1, i) for i in range(lax.axis_size(axis) - 1)])  6.21 us
    ppermute x2, starting transfers between devices, from_ahead(): lax.ppermute(x, axis, [(i + 1, i) for i in range(lax.axis_size(axis) - 1)])  4.82 us
  transfers between devices with their start and end apart: 20, of which 12 were waited for; matrix products, arithmetic and copies ran while one was open for 2% of the time, Pallas kernels for 14%

profile of v3, /device:TPU:16, one launch (start us, length us, event | category | flops | bytes accessed | tf_op | source)
XLA Modules:
  0.0 95.4 jit_solution(1889769602750597491)
XLA Ops:
  0.0 1.5 %collective-permute-start.3 = (f32[1,4,64,512]{3,2,1,0:T(8,128)}, f32[1,4,64,512]{3,2,1,0:T(8,128)S(1)}, u32[]{:S(2)}, u32[]{:S(2)}) collective-permute-start(f32[1,4,64,512]{3,2,1,0:T(8,128)} %refs_0_.2), channel_id=1, source_target_pairs={{0,4},{1,5},{2,6},{3,7},{4,0},{5,1},{6,2},{7,3},{8,12},{9,13},{10,... | collective-permute-start | bytes 1572872 | tf_op jit(solution)/shard_map/ppermute | solution.py:20
  1.5 1.5 %collective-permute-start.2 = (f32[1,4,64,512]{3,2,1,0:T(8,128)}, f32[1,4,64,512]{3,2,1,0:T(8,128)S(1)}, u32[]{:S(2)}, u32[]{:S(2)}) collective-permute-start(f32[1,4,64,512]{3,2,1,0:T(8,128)} %refs_0_.2), channel_id=1, source_target_pairs={{0,2},{1,3},{2,0},{3,1},{4,6},{5,7},{6,4},{7,5},{8,10},{9,11},{10,... | collective-permute-start | bytes 1572872 | tf_op jit(solution)/shard_map/ppermute | solution.py:20
  6.0 1.6 %collective-permute-start.9 = (f32[16,16,512]{2,1,0:T(8,128)S(1)}, f32[16,16,512]{2,1,0:T(8,128)S(1)}, u32[]{:S(2)}, u32[]{:S(2)}) collective-permute-start(f32[16,16,512]{2,1,0:T(8,128)S(1)} %slice_bitcast_fusion.newest), channel_id=1, source_target_pairs={{0,8},{8,16},{16,24},{24,0},{1,9},{9,17},{17,25},{25,1},{2,10},{10... | collective-permute-start | bytes 1572872 | tf_op jit(solution)/shard_map/ppermute | solution.py:26
  7.6 6.3 %collective-permute-done.3.block.refs_3_.refs_2_ = f32[1,4,64,512]{3,2,1,0:T(8,128)S(1)} collective-permute-done((f32[1,4,64,512]{3,2,1,0:T(8,128)}, f32[1,4,64,512]{3,2,1,0:T(8,128)S(1)}, u32[]{:S(2)}, u32[]{:S(2)}) %collective-permute-start.3) | collective-permute-done | bytes 524320 | tf_op jit(solution)/shard_map/ppermute | solution.py:20
  16.8 1.5 %collective-permute-start.7 = (f32[1,128,512]{2,1,0:T(8,128)S(1)}, f32[1,128,512]{2,1,0:T(8,128)S(1)}, u32[]{:S(2)}, u32[]{:S(2)}) collective-permute-start(f32[1,128,512]{2,1,0:T(8,128)S(1)} %shard_map.47), channel_id=1, source_target_pairs={{0,2},{1,3},{2,0},{3,1},{4,6},{5,7},{6,4},{7,5},{8,10},{9,11},{10,... | collective-permute-start | bytes 786440 | tf_op jit(solution)/shard_map/ppermute | solution.py:20
  18.3 1.4 %collective-permute-done.9.got = f32[16,16,512]{2,1,0:T(8,128)S(1)} collective-permute-done((f32[16,16,512]{2,1,0:T(8,128)S(1)}, f32[16,16,512]{2,1,0:T(8,128)S(1)}, u32[]{:S(2)}, u32[]{:S(2)}) %collective-permute-start.9) | collective-permute-done | bytes 524320 | tf_op jit(solution)/shard_map/ppermute | solution.py:26
  20.3 2.5 %collective-permute-start.15 = (f32[3,1,4,64,512]{4,3,2,1,0:T(8,128)S(1)}, f32[3,1,4,64,512]{4,3,2,1,0:T(8,128)S(1)}, u32[]{:S(2)}, u32[]{:S(2)}) collective-permute-start(f32[3,1,4,64,512]{4,3,2,1,0:T(8,128)S(1)} %shard_map.55), channel_id=1, source_target_pairs={{8,0},{16,8},{24,16},{9,1},{17,9},{25,17},{10,2},{18,10},{26,18},{... | collective-permute-start | bytes 4718600 | tf_op jit(solution)/shard_map/ppermute | solution.py:30
  23.7 1.5 %collective-permute-done.7.refs_0_.one = f32[1,128,512]{2,1,0:T(8,128)S(1)} collective-permute-done((f32[1,128,512]{2,1,0:T(8,128)S(1)}, f32[1,128,512]{2,1,0:T(8,128)S(1)}, u32[]{:S(2)}, u32[]{:S(2)}) %collective-permute-start.7) | collective-permute-done | bytes 262176 | tf_op jit(solution)/shard_map/ppermute | solution.py:20
  26.9 1.5 %collective-permute-done.10.refs_1_ = f32[1,128,512]{2,1,0:T(8,128)S(1)} collective-permute-done((f32[1,128,512]{2,1,0:T(8,128)S(1)}, f32[1,128,512]{2,1,0:T(8,128)S(1)}, u32[]{:S(2)}, u32[]{:S(2)}) %collective-permute-start.10) | collective-permute-done | bytes 262176 | tf_op jit(solution)/shard_map/ppermute | solution.py:20
  28.4 2.5 %shard_map.50 = (f32[16,16,512]{2,1,0:T(8,128)S(1)}, bf16[4,512,512]{2,1,0:T(8,128)(2,1)S(1)}, bf16[4,512,512]{2,1,0:T(8,128)(2,1)S(1)}, f32[4,4,9,128]{3,2,1,0:T(8,128)S(1)}) custom-call(s32[1]{0:T(128)} %bitcast.2.position, f32[16,16,512]{2,1,0:T(8,128)S(1)} %slice_bitcast_fusion.newest, ...), custom_call_target="tpu_custom_call", output_to_operand_aliasing={{1}: (3, {}), {2}: (4, {})} | custom-call | flops 1610612736 | bytes 5767168 | tf_op jit(solution)/shard_map/pallas_call | solution.py:53
  30.9 3.5 %collective-permute-start.12 = (f32[16,16,512]{2,1,0:T(8,128)S(1)}, f32[16,16,512]{2,1,0:T(8,128)S(1)}, u32[]{:S(2)}, u32[]{:S(2)}) collective-permute-start(f32[16,16,512]{2,1,0:T(8,128)S(1)} %get-tuple-element.47.past), channel_id=1, source_target_pairs={{0,8},{8,16},{16,24},{1,9},{9,17},{17,25},{2,10},{10,18},{18,26},{... | collective-permute-start | bytes 1572872 | tf_op jit(solution)/shard_map/ppermute | solution.py:26
  35.3 2.3 %collective-permute-start.16 = (f32[1,296,512]{2,1,0:T(8,128)S(1)}, f32[1,296,512]{2,1,0:T(8,128)S(1)}, u32[]{:S(2)}, u32[]{:S(2)}) collective-permute-start(f32[1,296,512]{2,1,0:T(8,128)S(1)} %shard_map.56), channel_id=1, source_target_pairs={{8,0},{16,8},{24,16},{9,1},{17,9},{25,17},{10,2},{18,10},{26,18},{... | collective-permute-start | bytes 1818632 | tf_op jit(solution)/shard_map/ppermute | solution.py:30
  37.7 9.1 %collective-permute-done.12.got = f32[16,16,512]{2,1,0:T(8,128)S(1)} collective-permute-done((f32[16,16,512]{2,1,0:T(8,128)S(1)}, f32[16,16,512]{2,1,0:T(8,128)S(1)}, u32[]{:S(2)}, u32[]{:S(2)}) %collective-permute-start.12) | collective-permute-done | bytes 524320 | tf_op jit(solution)/shard_map/ppermute | solution.py:26
  46.7 3.5 %collective-permute-start.14 = (f32[16,16,512]{2,1,0:T(8,128)S(1)}, f32[16,16,512]{2,1,0:T(8,128)S(1)}, u32[]{:S(2)}, u32[]{:S(2)}) collective-permute-start(f32[16,16,512]{2,1,0:T(8,128)S(1)} %collective-permute-done.12.got), channel_id=1, source_target_pairs={{8,16},{16,24},{9,17},{17,25},{10,18},{18,26},{11,19},{19,27},{12,... | collective-permute-start | bytes 1572872 | tf_op jit(solution)/shard_map/ppermute | solution.py:26
  50.2 2.3 %shard_map.52 = (f32[4,16,16,512]{3,2,1,0:T(8,128)}, f32[16,16,512]{2,1,0:T(8,128)S(1)}) custom-call(s32[1]{0:T(128)} %bitcast.section, f32[3,16,16,512]{3,2,1,0:T(8,128)S(1)} %bitcast.13, f32[16,16,512]{2,1,0:T(8,128)S(1)} %collective-permute-done.12.got, f32[16,16,512]{2,1,0:T(8,128)S(1)} %shard_map.51.early, ...), custom_call_target="tpu_custom_call" | custom-call | flops 2415919104 | bytes 7864320 | tf_op jit(solution)/shard_map/pallas_call | solution.py:53
  52.5 1.9 %collective-permute-start.13 = (f32[16,16,512]{2,1,0:T(8,128)S(1)}, f32[16,16,512]{2,1,0:T(8,128)S(1)}, u32[]{:S(2)}, u32[]{:S(2)}) collective-permute-start(f32[16,16,512]{2,1,0:T(8,128)S(1)} %get-tuple-element.51.past), channel_id=1, source_target_pairs={{0,8},{8,16},{16,24},{1,9},{9,17},{17,25},{2,10},{10,18},{18,26},{... | collective-permute-start | bytes 1572872 | tf_op jit(solution)/shard_map/ppermute | solution.py:26
  54.4 9.1 %collective-permute-done.14.got = f32[16,16,512]{2,1,0:T(8,128)S(1)} collective-permute-done((f32[16,16,512]{2,1,0:T(8,128)S(1)}, f32[16,16,512]{2,1,0:T(8,128)S(1)}, u32[]{:S(2)}, u32[]{:S(2)}) %collective-permute-start.14) | collective-permute-done | bytes 524320 | tf_op jit(solution)/shard_map/ppermute | solution.py:26
  64.3 6.2 %collective-permute-done.16.far = f32[1,296,512]{2,1,0:T(8,128)S(1)} collective-permute-done((f32[1,296,512]{2,1,0:T(8,128)S(1)}, f32[1,296,512]{2,1,0:T(8,128)S(1)}, u32[]{:S(2)}, u32[]{:S(2)}) %collective-permute-start.16) | collective-permute-done | bytes 606240 | tf_op jit(solution)/shard_map/ppermute | solution.py:30
  71.0 2.0 %collective-permute-done.13.got = f32[16,16,512]{2,1,0:T(8,128)S(1)} collective-permute-done((f32[16,16,512]{2,1,0:T(8,128)S(1)}, f32[16,16,512]{2,1,0:T(8,128)S(1)}, u32[]{:S(2)}, u32[]{:S(2)}) %collective-permute-start.13) | collective-permute-done | bytes 524320 | tf_op jit(solution)/shard_map/ppermute | solution.py:26
  73.0 2.3 %shard_map.54 = (f32[4,16,16,512]{3,2,1,0:T(8,128)}, f32[16,16,512]{2,1,0:T(8,128)S(1)}) custom-call(s32[1]{0:T(128)} %bitcast.section, f32[3,16,16,512]{3,2,1,0:T(8,128)S(1)} %bitcast.15, f32[16,16,512]{2,1,0:T(8,128)S(1)} %collective-permute-done.13.got, f32[16,16,512]{2,1,0:T(8,128)S(1)} %shard_map.53.early, ...), custom_call_target="tpu_custom_call", output_to_operand_aliasing={{0}: (8, {})} | custom-call | flops 14495514624 | bytes 39321600 | tf_op jit(solution)/shard_map/pallas_call | solution.py:53
  76.6 2.4 %shard_map.59 = (f32[4,16,16,512]{3,2,1,0:T(8,128)}, f32[16,16,512]{2,1,0:T(8,128)S(1)}) custom-call(s32[1]{0:T(128)} %bitcast.section, f32[3,16,16,512]{3,2,1,0:T(8,128)S(1)} %bitcast.17, f32[16,16,512]{2,1,0:T(8,128)S(1)} %get-tuple-element.54.got.past, f32[16,16,512]{2,1,0:T(8,128)S(1)} %shard_map.58.early, ...), custom_call_target="tpu_custom_call", output_to_operand_aliasing={{0}: (8, {})} | custom-call | flops 2415919104 | bytes 7864320 | tf_op jit(solution)/shard_map/pallas_call | solution.py:53
  79.1 3.5 %collective-permute-start.19 = (f32[16,16,512]{2,1,0:T(8,128)S(1)}, f32[16,16,512]{2,1,0:T(8,128)S(1)}, u32[]{:S(2)}, u32[]{:S(2)}) collective-permute-start(f32[16,16,512]{2,1,0:T(8,128)S(1)} %get-tuple-element.65), channel_id=1, source_target_pairs={{0,8},{8,16},{16,24},{1,9},{9,17},{17,25},{2,10},{10,18},{18,26},{... | collective-permute-start | bytes 1572872 | tf_op jit(solution)/shard_map/ppermute | solution.py:26
  82.6 2.8 %shard_map.60.own = f32[16,16,512]{2,1,0:T(8,128)S(1)} custom-call(f32[3,16,16,512]{3,2,1,0:T(8,128)S(1)} %bitcast.18, f32[4,4,9,128]{3,2,1,0:T(8,128)S(1)} %get-tuple-element.48.table, bf16[4,512,512]{2,1,0:T(8,128)(2,1)S(1)} %get-tuple-element.49.highs, bf16[4,512,512]{2,1,0:T(8,128)(2,1)S(1)} %get-tuple-element.50.lows), custom_call_target="tpu_custom_call" | custom-call | flops 1610612736 | bytes 5767168 | tf_op jit(solution)/shard_map/pallas_call | solution.py:53
  85.4 9.1 %collective-permute-done.19.got = f32[16,16,512]{2,1,0:T(8,128)S(1)} collective-permute-done((f32[16,16,512]{2,1,0:T(8,128)S(1)}, f32[16,16,512]{2,1,0:T(8,128)S(1)}, u32[]{:S(2)}, u32[]{:S(2)}) %collective-permute-start.19) | collective-permute-done | bytes 524320 | tf_op jit(solution)/shard_map/ppermute | solution.py:26
  (41 shorter events, 13.5 us)
Async XLA Ops:
  0.0 19.7 %copy-start.2 = (f32[1,4,64,512]{3,2,1,0:T(8,128)S(1)}, f32[1,4,64,512]{3,2,1,0:T(8,128)}, u32[]{:S(2)}) copy-start(f32[1,4,64,512]{3,2,1,0:T(8,128)} %refs_0_.2) | copy-start | bytes 1572868
  0.0 13.9 %collective-permute-start.3 = (f32[1,4,64,512]{3,2,1,0:T(8,128)}, f32[1,4,64,512]{3,2,1,0:T(8,128)S(1)}, u32[]{:S(2)}, u32[]{:S(2)}) collective-permute-start(f32[1,4,64,512]{3,2,1,0:T(8,128)} %refs_0_.2), channel_id=1, source_target_pairs={{0,4},{1,5},{2,6},{3,7},{4,0},{5,1},{6,2},{7,3},{8,12},{9,13},{10,... | collective-permute-start | bytes 1572872 | tf_op jit(solution)/shard_map/ppermute | solution.py:20
  1.5 13.9 %collective-permute-start.2 = (f32[1,4,64,512]{3,2,1,0:T(8,128)}, f32[1,4,64,512]{3,2,1,0:T(8,128)S(1)}, u32[]{:S(2)}, u32[]{:S(2)}) collective-permute-start(f32[1,4,64,512]{3,2,1,0:T(8,128)} %refs_0_.2), channel_id=1, source_target_pairs={{0,2},{1,3},{2,0},{3,1},{4,6},{5,7},{6,4},{7,5},{8,10},{9,11},{10,... | collective-permute-start | bytes 1572872 | tf_op jit(solution)/shard_map/ppermute | solution.py:20
  3.0 12.5 %collective-permute-start.1 = (f32[1,4,64,512]{3,2,1,0:T(8,128)}, f32[1,4,64,512]{3,2,1,0:T(8,128)S(1)}, u32[]{:S(2)}, u32[]{:S(2)}) collective-permute-start(f32[1,4,64,512]{3,2,1,0:T(8,128)} %refs_0_.2), channel_id=1, source_target_pairs={{0,1},{1,0},{2,3},{3,2},{4,5},{5,4},{6,7},{7,6},{8,9},{9,8},{10,11... | collective-permute-start | bytes 1572872 | tf_op jit(solution)/shard_map/ppermute | solution.py:20
  3.7 1.6 %collective-permute-start = (f32[4,9,64]{2,1,0:T(8,128)S(1)}, f32[4,9,64]{2,1,0:T(8,128)S(1)}, u32[]{:S(2)}, u32[]{:S(2)}) collective-permute-start(f32[4,9,64]{2,1,0:T(8,128)S(1)} %bitcast.21), channel_id=1, source_target_pairs={{0,1},{1,0},{2,3},{3,2},{4,5},{5,4},{6,7},{7,6},{8,9},{9,8},{10,11... | collective-permute-start | bytes 27656 | tf_op jit(solution)/shard_map/ppermute | solution.py:20
  5.4 10.4 %collective-permute-start.4 = (f32[4,9,128]{2,1,0:T(8,128)S(1)}, f32[4,9,128]{2,1,0:T(8,128)S(1)}, u32[]{:S(2)}, u32[]{:S(2)}) collective-permute-start(f32[4,9,128]{2,1,0:T(8,128)S(1)} %maximum_select_fusion.refs_0_.refs_4_), channel_id=1, source_target_pairs={{0,2},{1,3},{2,0},{3,1},{4,6},{5,7},{6,4},{7,5},{8,10},{9,11},{10,... | collective-permute-start | bytes 55304 | tf_op jit(solution)/shard_map/ppermute | solution.py:20
  6.0 13.7 %collective-permute-start.9 = (f32[16,16,512]{2,1,0:T(8,128)S(1)}, f32[16,16,512]{2,1,0:T(8,128)S(1)}, u32[]{:S(2)}, u32[]{:S(2)}) collective-permute-start(f32[16,16,512]{2,1,0:T(8,128)S(1)} %slice_bitcast_fusion.newest), channel_id=1, source_target_pairs={{0,8},{8,16},{16,24},{24,0},{1,9},{9,17},{17,25},{25,1},{2,10},{10... | collective-permute-start | bytes 1572872 | tf_op jit(solution)/shard_map/ppermute | solution.py:26
  14.2 5.5 %collective-permute-start.6 = (f32[1,4,64,512]{3,2,1,0:T(8,128)S(1)}, f32[1,4,64,512]{3,2,1,0:T(8,128)S(1)}, u32[]{:S(2)}, u32[]{:S(2)}) collective-permute-start(f32[1,4,64,512]{3,2,1,0:T(8,128)S(1)} %collective-permute-done.3.block.refs_3_.refs_2_), channel_id=1, source_target_pairs={{0,1},{1,0},{2,3},{3,2},{4,5},{5,4},{6,7},{7,6},{8,9},{9,8},{10,11... | collective-permute-start | bytes 1572872 | tf_op jit(solution)/shard_map/ppermute | solution.py:20
  16.2 3.5 %collective-permute-start.5 = (f32[1,4,64,512]{3,2,1,0:T(8,128)S(1)}, f32[1,4,64,512]{3,2,1,0:T(8,128)S(1)}, u32[]{:S(2)}, u32[]{:S(2)}) collective-permute-start(f32[1,4,64,512]{3,2,1,0:T(8,128)S(1)} %collective-permute-done.2.block.refs_2_.refs_1_), channel_id=1, source_target_pairs={{0,1},{1,0},{2,3},{3,2},{4,5},{5,4},{6,7},{7,6},{8,9},{9,8},{10,11... | collective-permute-start | bytes 1572872 | tf_op jit(solution)/shard_map/ppermute | solution.py:20
  16.2 10.1 %collective-permute-start.8 = (f32[1,160,512]{2,1,0:T(8,128)S(1)}, f32[1,160,512]{2,1,0:T(8,128)S(1)}, u32[]{:S(2)}, u32[]{:S(2)}) collective-permute-start(f32[1,160,512]{2,1,0:T(8,128)S(1)} %shard_map.46), channel_id=1, source_target_pairs={{0,4},{1,5},{2,6},{3,7},{4,0},{5,1},{6,2},{7,3},{8,12},{9,13},{10,... | collective-permute-start | bytes 983048 | tf_op jit(solution)/shard_map/ppermute | solution.py:20
  16.8 8.4 %collective-permute-start.7 = (f32[1,128,512]{2,1,0:T(8,128)S(1)}, f32[1,128,512]{2,1,0:T(8,128)S(1)}, u32[]{:S(2)}, u32[]{:S(2)}) collective-permute-start(f32[1,128,512]{2,1,0:T(8,128)S(1)} %shard_map.47), channel_id=1, source_target_pairs={{0,2},{1,3},{2,0},{3,1},{4,6},{5,7},{6,4},{7,5},{8,10},{9,11},{10,... | collective-permute-start | bytes 786440 | tf_op jit(solution)/shard_map/ppermute | solution.py:20
  20.1 2.7 %copy-start.1 = (f32[1,2,1,16,16,512]{5,4,3,2,1,0:T(8,128)S(1)}, f32[1,2,1,16,16,512]{5,4,3,2,1,0:T(8,128)}, u32[]{:S(2)}) copy-start(f32[1,2,1,16,16,512]{5,4,3,2,1,0:T(8,128)} %param.4) | copy-start | bytes 3145732
  20.3 50.3 %collective-permute-start.15 = (f32[3,1,4,64,512]{4,3,2,1,0:T(8,128)S(1)}, f32[3,1,4,64,512]{4,3,2,1,0:T(8,128)S(1)}, u32[]{:S(2)}, u32[]{:S(2)}) collective-permute-start(f32[3,1,4,64,512]{4,3,2,1,0:T(8,128)S(1)} %shard_map.55), channel_id=1, source_target_pairs={{8,0},{16,8},{24,16},{9,1},{17,9},{25,17},{10,2},{18,10},{26,18},{... | collective-permute-start | bytes 4718600 | tf_op jit(solution)/shard_map/ppermute | solution.py:30
  23.7 10.7 %copy-start = (f32[3,1,16,16,512]{4,3,2,1,0:T(8,128)S(1)}, f32[3,1,16,16,512]{4,3,2,1,0:T(8,128)}, u32[]{:S(2)}) copy-start(f32[3,1,16,16,512]{4,3,2,1,0:T(8,128)} %param.5) | copy-start | bytes 4718596
  26.4 2.0 %collective-permute-start.11 = (f32[1,160,512]{2,1,0:T(8,128)S(1)}, f32[1,160,512]{2,1,0:T(8,128)S(1)}, u32[]{:S(2)}, u32[]{:S(2)}) collective-permute-start(f32[1,160,512]{2,1,0:T(8,128)S(1)} %collective-permute-done.8.refs_2_.two), channel_id=1, source_target_pairs={{0,1},{1,0},{2,3},{3,2},{4,5},{5,4},{6,7},{7,6},{8,9},{9,8},{10,11... | collective-permute-start | bytes 983048 | tf_op jit(solution)/shard_map/ppermute | solution.py:20
  26.4 2.0 %collective-permute-start.10 = (f32[1,128,512]{2,1,0:T(8,128)S(1)}, f32[1,128,512]{2,1,0:T(8,128)S(1)}, u32[]{:S(2)}, u32[]{:S(2)}) collective-permute-start(f32[1,128,512]{2,1,0:T(8,128)S(1)} %collective-permute-done.7.refs_0_.one), channel_id=1, source_target_pairs={{0,1},{1,0},{2,3},{3,2},{4,5},{5,4},{6,7},{7,6},{8,9},{9,8},{10,11... | collective-permute-start | bytes 786440 | tf_op jit(solution)/shard_map/ppermute | solution.py:20
  30.9 15.9 %collective-permute-start.12 = (f32[16,16,512]{2,1,0:T(8,128)S(1)}, f32[16,16,512]{2,1,0:T(8,128)S(1)}, u32[]{:S(2)}, u32[]{:S(2)}) collective-permute-start(f32[16,16,512]{2,1,0:T(8,128)S(1)} %get-tuple-element.47.past), channel_id=1, source_target_pairs={{0,8},{8,16},{16,24},{1,9},{9,17},{17,25},{2,10},{10,18},{18,26},{... | collective-permute-start | bytes 1572872 | tf_op jit(solution)/shard_map/ppermute | solution.py:26
  35.3 35.2 %collective-permute-start.16 = (f32[1,296,512]{2,1,0:T(8,128)S(1)}, f32[1,296,512]{2,1,0:T(8,128)S(1)}, u32[]{:S(2)}, u32[]{:S(2)}) collective-permute-start(f32[1,296,512]{2,1,0:T(8,128)S(1)} %shard_map.56), channel_id=1, source_target_pairs={{8,0},{16,8},{24,16},{9,1},{17,9},{25,17},{10,2},{18,10},{26,18},{... | collective-permute-start | bytes 1818632 | tf_op jit(solution)/shard_map/ppermute | solution.py:30
  46.7 16.7 %collective-permute-start.14 = (f32[16,16,512]{2,1,0:T(8,128)S(1)}, f32[16,16,512]{2,1,0:T(8,128)S(1)}, u32[]{:S(2)}, u32[]{:S(2)}) collective-permute-start(f32[16,16,512]{2,1,0:T(8,128)S(1)} %collective-permute-done.12.got), channel_id=1, source_target_pairs={{8,16},{16,24},{9,17},{17,25},{10,18},{18,26},{11,19},{19,27},{12,... | collective-permute-start | bytes 1572872 | tf_op jit(solution)/shard_map/ppermute | solution.py:26
  52.5 20.5 %collective-permute-start.13 = (f32[16,16,512]{2,1,0:T(8,128)S(1)}, f32[16,16,512]{2,1,0:T(8,128)S(1)}, u32[]{:S(2)}, u32[]{:S(2)}) collective-permute-start(f32[16,16,512]{2,1,0:T(8,128)S(1)} %get-tuple-element.51.past), channel_id=1, source_target_pairs={{0,8},{8,16},{16,24},{1,9},{9,17},{17,25},{2,10},{10,18},{18,26},{... | collective-permute-start | bytes 1572872 | tf_op jit(solution)/shard_map/ppermute | solution.py:26
  70.5 4.7 %collective-permute-start.17 = (f32[3,1,4,64,512]{4,3,2,1,0:T(8,128)S(1)}, f32[3,1,4,64,512]{4,3,2,1,0:T(8,128)S(1)}, u32[]{:S(2)}, u32[]{:S(2)}) collective-permute-start(f32[3,1,4,64,512]{4,3,2,1,0:T(8,128)S(1)} %collective-permute-done.15.near), channel_id=1, source_target_pairs={{0,1},{1,0},{2,3},{3,2},{4,5},{5,4},{6,7},{7,6},{8,9},{9,8},{10,11... | collective-permute-start | bytes 4718600 | tf_op jit(solution)/shard_map/ppermute | solution.py:20
  70.5 4.7 %collective-permute-start.18 = (f32[1,296,512]{2,1,0:T(8,128)S(1)}, f32[1,296,512]{2,1,0:T(8,128)S(1)}, u32[]{:S(2)}, u32[]{:S(2)}) collective-permute-start(f32[1,296,512]{2,1,0:T(8,128)S(1)} %collective-permute-done.16.far), channel_id=1, source_target_pairs={{0,1},{1,0},{2,3},{3,2},{4,5},{5,4},{6,7},{7,6},{8,9},{9,8},{10,11... | collective-permute-start | bytes 1818632 | tf_op jit(solution)/shard_map/ppermute | solution.py:20
  79.1 15.4 %collective-permute-start.19 = (f32[16,16,512]{2,1,0:T(8,128)S(1)}, f32[16,16,512]{2,1,0:T(8,128)S(1)}, u32[]{:S(2)}, u32[]{:S(2)}) collective-permute-start(f32[16,16,512]{2,1,0:T(8,128)S(1)} %get-tuple-element.65), channel_id=1, source_target_pairs={{0,8},{8,16},{16,24},{1,9},{9,17},{17,25},{2,10},{10,18},{18,26},{... | collective-permute-start | bytes 1572872 | tf_op jit(solution)/shard_map/ppermute | solution.py:26

commit v4 on v3

--- a/solution.py
+++ b/solution.py
@@ -12,7 +12,6 @@
 VMEM_LIMIT = 16 * 1024 * 1024
 LANES = 128
 DEPTH = 256
-TAP_ROWS = 16
 
 
 def swap(x, axis, bit):
@@ -257,7 +256,7 @@
             target = out.at[u, pl.ds(i * count, count)]
             copies.append(begin(block.at[u, start + i], target, sem.at[u * half + i]))
     for j, chip in enumerate(taps):
-        row = half * count + j * TAP_ROWS
+        row = half * count + j * chip.shape[1]
         for n in range(branches):
             out[0, row : row + 9, n * LANES : (n + 1) * LANES] = chip[n]
     for copy in copies:
@@ -267,7 +266,8 @@
 def half_of(block, start, *taps):
     uppers, branches, count, channels = block.shape
     half = branches // 2
-    out = jax.ShapeDtypeStruct((uppers, half * count + TAP_ROWS * len(taps), channels), F32)
+    extra = -(-sum(chip.shape[1] for chip in taps) // 8) * 8
+    out = jax.ShapeDtypeStruct((uppers, half * count + extra, channels), F32)
     work = pl.CostEstimate(flops=0, bytes_accessed=4 * block.size, transcendentals=0)
     kernel = functools.partial(half_kernel, start * half)
     return call(kernel, (out,), (block, *taps), [], half * uppers, work)[0]
@@ -391,7 +391,7 @@
     else:
         below = far[2]
         for j, part in enumerate(taps):
-            row = below.shape[1] - (n_taps - j) * TAP_ROWS
+            row = far[0].shape[1] + j * part.shape[1]
             for n in range(branches):
                 table[chip ^ j, n] = part[n]
                 lanes = slice(n * LANES, (n + 1) * LANES)

time: 96.4 us -> 96.4 us (level)
  no operation moved by 1% of the time
where the time goes in v4:
time: 96.4 us; the launch traced here: 95.4 us
  waiting for transfers between devices  48.8 us (51%)
  starting transfers between devices  26.1 us (27%)
  Pallas kernels  18.2 us (19%)
  local copies, waits for them, and re-layouts  1.82 us (2%)
    ppermute x5, waiting for transfers between devices, from_behind(): lax.ppermute(x, axis, pairs + [(size - 1, 0)] * (around and size > 1))  30.6 us
    pallas_call x16, Pallas kernels, call(): pl.pallas_call(kernel, out_shape=outs, in_specs=[spec(x, i, apart) for i,...  18.2 us
    ppermute x5, starting transfers between devices, from_behind(): lax.ppermute(x, axis, pairs + [(size - 1, 0)] * (around and size > 1))  13.9 us
    ppermute x13, waiting for transfers between devices, swap(): return lax.ppermute(x, axis, [(i, i ^ bit) for i in range(size)])  11.6 us
    ppermute x13, starting transfers between devices, swap(): return lax.ppermute(x, axis, [(i, i ^ bit) for i in range(size)])  7.35 us
    ppermute x2, waiting for transfers between devices, from_ahead(): lax.ppermute(x, axis, [(i + 1, i) for i in range(lax.axis_size(axis) - 1)])  6.58 us
    ppermute x2, starting transfers between devices, from_ahead(): lax.ppermute(x, axis, [(i + 1, i) for i in range(lax.axis_size(axis) - 1)])  4.85 us
  transfers between devices with their start and end apart: 20, of which 12 were waited for; matrix products, arithmetic and copies ran while one was open for 2% of the time, Pallas kernels for 14%

profile of v4, /device:TPU:16, one launch (start us, length us, event | category | flops | bytes accessed | tf_op | source)
XLA Modules:
  0.0 95.4 jit_solution(5311995298064347257)
XLA Ops:
  0.0 1.5 %collective-permute-start.3 = (f32[1,4,64,512]{3,2,1,0:T(8,128)}, f32[1,4,64,512]{3,2,1,0:T(8,128)S(1)}, u32[]{:S(2)}, u32[]{:S(2)}) collective-permute-start(f32[1,4,64,512]{3,2,1,0:T(8,128)} %refs_0_.2), channel_id=1, source_target_pairs={{0,4},{1,5},{2,6},{3,7},{4,0},{5,1},{6,2},{7,3},{8,12},{9,13},{10,... | collective-permute-start | bytes 1572872 | tf_op jit(solution)/shard_map/ppermute | solution.py:19
  1.5 1.5 %collective-permute-start.2 = (f32[1,4,64,512]{3,2,1,0:T(8,128)}, f32[1,4,64,512]{3,2,1,0:T(8,128)S(1)}, u32[]{:S(2)}, u32[]{:S(2)}) collective-permute-start(f32[1,4,64,512]{3,2,1,0:T(8,128)} %refs_0_.2), channel_id=1, source_target_pairs={{0,2},{1,3},{2,0},{3,1},{4,6},{5,7},{6,4},{7,5},{8,10},{9,11},{10,... | collective-permute-start | bytes 1572872 | tf_op jit(solution)/shard_map/ppermute | solution.py:19
  6.0 1.6 %collective-permute-start.9 = (f32[16,16,512]{2,1,0:T(8,128)S(1)}, f32[16,16,512]{2,1,0:T(8,128)S(1)}, u32[]{:S(2)}, u32[]{:S(2)}) collective-permute-start(f32[16,16,512]{2,1,0:T(8,128)S(1)} %slice_bitcast_fusion.newest), channel_id=1, source_target_pairs={{0,8},{8,16},{16,24},{24,0},{1,9},{9,17},{17,25},{25,1},{2,10},{10... | collective-permute-start | bytes 1572872 | tf_op jit(solution)/shard_map/ppermute | solution.py:25
  7.6 6.3 %collective-permute-done.3.block.refs_3_.refs_2_ = f32[1,4,64,512]{3,2,1,0:T(8,128)S(1)} collective-permute-done((f32[1,4,64,512]{3,2,1,0:T(8,128)}, f32[1,4,64,512]{3,2,1,0:T(8,128)S(1)}, u32[]{:S(2)}, u32[]{:S(2)}) %collective-permute-start.3) | collective-permute-done | bytes 524320 | tf_op jit(solution)/shard_map/ppermute | solution.py:19
  16.8 1.5 %collective-permute-start.7 = (f32[1,128,512]{2,1,0:T(8,128)S(1)}, f32[1,128,512]{2,1,0:T(8,128)S(1)}, u32[]{:S(2)}, u32[]{:S(2)}) collective-permute-start(f32[1,128,512]{2,1,0:T(8,128)S(1)} %shard_map.47), channel_id=1, source_target_pairs={{0,2},{1,3},{2,0},{3,1},{4,6},{5,7},{6,4},{7,5},{8,10},{9,11},{10,... | collective-permute-start | bytes 786440 | tf_op jit(solution)/shard_map/ppermute | solution.py:19
  18.3 1.4 %collective-permute-done.9.got = f32[16,16,512]{2,1,0:T(8,128)S(1)} collective-permute-done((f32[16,16,512]{2,1,0:T(8,128)S(1)}, f32[16,16,512]{2,1,0:T(8,128)S(1)}, u32[]{:S(2)}, u32[]{:S(2)}) %collective-permute-start.9) | collective-permute-done | bytes 524320 | tf_op jit(solution)/shard_map/ppermute | solution.py:25
  20.3 2.5 %collective-permute-start.15 = (f32[3,1,4,64,512]{4,3,2,1,0:T(8,128)S(1)}, f32[3,1,4,64,512]{4,3,2,1,0:T(8,128)S(1)}, u32[]{:S(2)}, u32[]{:S(2)}) collective-permute-start(f32[3,1,4,64,512]{4,3,2,1,0:T(8,128)S(1)} %shard_map.55), channel_id=1, source_target_pairs={{8,0},{16,8},{24,16},{9,1},{17,9},{25,17},{10,2},{18,10},{26,18},{... | collective-permute-start | bytes 4718600 | tf_op jit(solution)/shard_map/ppermute | solution.py:29
  23.7 1.5 %collective-permute-done.7.refs_0_.one = f32[1,128,512]{2,1,0:T(8,128)S(1)} collective-permute-done((f32[1,128,512]{2,1,0:T(8,128)S(1)}, f32[1,128,512]{2,1,0:T(8,128)S(1)}, u32[]{:S(2)}, u32[]{:S(2)}) %collective-permute-start.7) | collective-permute-done | bytes 262176 | tf_op jit(solution)/shard_map/ppermute | solution.py:19
  26.5 1.5 %collective-permute-done.10.refs_1_ = f32[1,128,512]{2,1,0:T(8,128)S(1)} collective-permute-done((f32[1,128,512]{2,1,0:T(8,128)S(1)}, f32[1,128,512]{2,1,0:T(8,128)S(1)}, u32[]{:S(2)}, u32[]{:S(2)}) %collective-permute-start.10) | collective-permute-done | bytes 262176 | tf_op jit(solution)/shard_map/ppermute | solution.py:19
  28.0 2.5 %shard_map.50 = (f32[16,16,512]{2,1,0:T(8,128)S(1)}, bf16[4,512,512]{2,1,0:T(8,128)(2,1)S(1)}, bf16[4,512,512]{2,1,0:T(8,128)(2,1)S(1)}, f32[4,4,9,128]{3,2,1,0:T(8,128)S(1)}) custom-call(s32[1]{0:T(128)} %bitcast.2.position, f32[16,16,512]{2,1,0:T(8,128)S(1)} %slice_bitcast_fusion.newest, ...), custom_call_target="tpu_custom_call", output_to_operand_aliasing={{1}: (3, {}), {2}: (4, {})} | custom-call | flops 1610612736 | bytes 5767168 | tf_op jit(solution)/shard_map/pallas_call | solution.py:52
  30.5 3.5 %collective-permute-start.12 = (f32[16,16,512]{2,1,0:T(8,128)S(1)}, f32[16,16,512]{2,1,0:T(8,128)S(1)}, u32[]{:S(2)}, u32[]{:S(2)}) collective-permute-start(f32[16,16,512]{2,1,0:T(8,128)S(1)} %get-tuple-element.47.past), channel_id=1, source_target_pairs={{0,8},{8,16},{16,24},{1,9},{9,17},{17,25},{2,10},{10,18},{18,26},{... | collective-permute-start | bytes 1572872 | tf_op jit(solution)/shard_map/ppermute | solution.py:25
  34.9 2.4 %collective-permute-start.16 = (f32[1,296,512]{2,1,0:T(8,128)S(1)}, f32[1,296,512]{2,1,0:T(8,128)S(1)}, u32[]{:S(2)}, u32[]{:S(2)}) collective-permute-start(f32[1,296,512]{2,1,0:T(8,128)S(1)} %shard_map.56), channel_id=1, source_target_pairs={{8,0},{16,8},{24,16},{9,1},{17,9},{25,17},{10,2},{18,10},{26,18},{... | collective-permute-start | bytes 1818632 | tf_op jit(solution)/shard_map/ppermute | solution.py:29
  37.3 9.1 %collective-permute-done.12.got = f32[16,16,512]{2,1,0:T(8,128)S(1)} collective-permute-done((f32[16,16,512]{2,1,0:T(8,128)S(1)}, f32[16,16,512]{2,1,0:T(8,128)S(1)}, u32[]{:S(2)}, u32[]{:S(2)}) %collective-permute-start.12) | collective-permute-done | bytes 524320 | tf_op jit(solution)/shard_map/ppermute | solution.py:25
  46.4 3.5 %collective-permute-start.14 = (f32[16,16,512]{2,1,0:T(8,128)S(1)}, f32[16,16,512]{2,1,0:T(8,128)S(1)}, u32[]{:S(2)}, u32[]{:S(2)}) collective-permute-start(f32[16,16,512]{2,1,0:T(8,128)S(1)} %collective-permute-done.12.got), channel_id=1, source_target_pairs={{8,16},{16,24},{9,17},{17,25},{10,18},{18,26},{11,19},{19,27},{12,... | collective-permute-start | bytes 1572872 | tf_op jit(solution)/shard_map/ppermute | solution.py:25
  49.8 2.3 %shard_map.52 = (f32[4,16,16,512]{3,2,1,0:T(8,128)}, f32[16,16,512]{2,1,0:T(8,128)S(1)}) custom-call(s32[1]{0:T(128)} %bitcast.section, f32[3,16,16,512]{3,2,1,0:T(8,128)S(1)} %bitcast.13, f32[16,16,512]{2,1,0:T(8,128)S(1)} %collective-permute-done.12.got, f32[16,16,512]{2,1,0:T(8,128)S(1)} %shard_map.51.early, ...), custom_call_target="tpu_custom_call" | custom-call | flops 2415919104 | bytes 7864320 | tf_op jit(solution)/shard_map/pallas_call | solution.py:52
  52.1 1.9 %collective-permute-start.13 = (f32[16,16,512]{2,1,0:T(8,128)S(1)}, f32[16,16,512]{2,1,0:T(8,128)S(1)}, u32[]{:S(2)}, u32[]{:S(2)}) collective-permute-start(f32[16,16,512]{2,1,0:T(8,128)S(1)} %get-tuple-element.51.past), channel_id=1, source_target_pairs={{0,8},{8,16},{16,24},{1,9},{9,17},{17,25},{2,10},{10,18},{18,26},{... | collective-permute-start | bytes 1572872 | tf_op jit(solution)/shard_map/ppermute | solution.py:25
  54.0 9.1 %collective-permute-done.14.got = f32[16,16,512]{2,1,0:T(8,128)S(1)} collective-permute-done((f32[16,16,512]{2,1,0:T(8,128)S(1)}, f32[16,16,512]{2,1,0:T(8,128)S(1)}, u32[]{:S(2)}, u32[]{:S(2)}) %collective-permute-start.14) | collective-permute-done | bytes 524320 | tf_op jit(solution)/shard_map/ppermute | solution.py:25
  64.0 6.6 %collective-permute-done.16.far = f32[1,296,512]{2,1,0:T(8,128)S(1)} collective-permute-done((f32[1,296,512]{2,1,0:T(8,128)S(1)}, f32[1,296,512]{2,1,0:T(8,128)S(1)}, u32[]{:S(2)}, u32[]{:S(2)}) %collective-permute-start.16) | collective-permute-done | bytes 606240 | tf_op jit(solution)/shard_map/ppermute | solution.py:29
  71.0 1.6 %collective-permute-done.13.got = f32[16,16,512]{2,1,0:T(8,128)S(1)} collective-permute-done((f32[16,16,512]{2,1,0:T(8,128)S(1)}, f32[16,16,512]{2,1,0:T(8,128)S(1)}, u32[]{:S(2)}, u32[]{:S(2)}) %collective-permute-start.13) | collective-permute-done | bytes 524320 | tf_op jit(solution)/shard_map/ppermute | solution.py:25
  72.6 2.3 %shard_map.54 = (f32[4,16,16,512]{3,2,1,0:T(8,128)}, f32[16,16,512]{2,1,0:T(8,128)S(1)}) custom-call(s32[1]{0:T(128)} %bitcast.section, f32[3,16,16,512]{3,2,1,0:T(8,128)S(1)} %bitcast.15, f32[16,16,512]{2,1,0:T(8,128)S(1)} %collective-permute-done.13.got, f32[16,16,512]{2,1,0:T(8,128)S(1)} %shard_map.53.early, ...), custom_call_target="tpu_custom_call", output_to_operand_aliasing={{0}: (8, {})} | custom-call | flops 14495514624 | bytes 39321600 | tf_op jit(solution)/shard_map/pallas_call | solution.py:52
  76.3 2.4 %shard_map.59 = (f32[4,16,16,512]{3,2,1,0:T(8,128)}, f32[16,16,512]{2,1,0:T(8,128)S(1)}) custom-call(s32[1]{0:T(128)} %bitcast.section, f32[3,16,16,512]{3,2,1,0:T(8,128)S(1)} %bitcast.17, f32[16,16,512]{2,1,0:T(8,128)S(1)} %get-tuple-element.54.got.past, f32[16,16,512]{2,1,0:T(8,128)S(1)} %shard_map.58.early, ...), custom_call_target="tpu_custom_call", output_to_operand_aliasing={{0}: (8, {})} | custom-call | flops 2415919104 | bytes 7864320 | tf_op jit(solution)/shard_map/pallas_call | solution.py:52
  78.7 3.5 %collective-permute-start.19 = (f32[16,16,512]{2,1,0:T(8,128)S(1)}, f32[16,16,512]{2,1,0:T(8,128)S(1)}, u32[]{:S(2)}, u32[]{:S(2)}) collective-permute-start(f32[16,16,512]{2,1,0:T(8,128)S(1)} %get-tuple-element.65), channel_id=1, source_target_pairs={{0,8},{8,16},{16,24},{1,9},{9,17},{17,25},{2,10},{10,18},{18,26},{... | collective-permute-start | bytes 1572872 | tf_op jit(solution)/shard_map/ppermute | solution.py:25
  82.2 2.8 %shard_map.60.own = f32[16,16,512]{2,1,0:T(8,128)S(1)} custom-call(f32[3,16,16,512]{3,2,1,0:T(8,128)S(1)} %bitcast.18, f32[4,4,9,128]{3,2,1,0:T(8,128)S(1)} %get-tuple-element.48.table, bf16[4,512,512]{2,1,0:T(8,128)(2,1)S(1)} %get-tuple-element.49.highs, bf16[4,512,512]{2,1,0:T(8,128)(2,1)S(1)} %get-tuple-element.50.lows), custom_call_target="tpu_custom_call" | custom-call | flops 1610612736 | bytes 5767168 | tf_op jit(solution)/shard_map/pallas_call | solution.py:52
  85.0 9.5 %collective-permute-done.19.got = f32[16,16,512]{2,1,0:T(8,128)S(1)} collective-permute-done((f32[16,16,512]{2,1,0:T(8,128)S(1)}, f32[16,16,512]{2,1,0:T(8,128)S(1)}, u32[]{:S(2)}, u32[]{:S(2)}) %collective-permute-start.19) | collective-permute-done | bytes 524320 | tf_op jit(solution)/shard_map/ppermute | solution.py:25
  (41 shorter events, 13.1 us)
Async XLA Ops:
  0.0 19.7 %copy-start.2 = (f32[1,4,64,512]{3,2,1,0:T(8,128)S(1)}, f32[1,4,64,512]{3,2,1,0:T(8,128)}, u32[]{:S(2)}) copy-start(f32[1,4,64,512]{3,2,1,0:T(8,128)} %refs_0_.2) | copy-start | bytes 1572868
  0.0 13.9 %collective-permute-start.3 = (f32[1,4,64,512]{3,2,1,0:T(8,128)}, f32[1,4,64,512]{3,2,1,0:T(8,128)S(1)}, u32[]{:S(2)}, u32[]{:S(2)}) collective-permute-start(f32[1,4,64,512]{3,2,1,0:T(8,128)} %refs_0_.2), channel_id=1, source_target_pairs={{0,4},{1,5},{2,6},{3,7},{4,0},{5,1},{6,2},{7,3},{8,12},{9,13},{10,... | collective-permute-start | bytes 1572872 | tf_op jit(solution)/shard_map/ppermute | solution.py:19
  1.5 13.9 %collective-permute-start.2 = (f32[1,4,64,512]{3,2,1,0:T(8,128)}, f32[1,4,64,512]{3,2,1,0:T(8,128)S(1)}, u32[]{:S(2)}, u32[]{:S(2)}) collective-permute-start(f32[1,4,64,512]{3,2,1,0:T(8,128)} %refs_0_.2), channel_id=1, source_target_pairs={{0,2},{1,3},{2,0},{3,1},{4,6},{5,7},{6,4},{7,5},{8,10},{9,11},{10,... | collective-permute-start | bytes 1572872 | tf_op jit(solution)/shard_map/ppermute | solution.py:19
  3.0 12.5 %collective-permute-start.1 = (f32[1,4,64,512]{3,2,1,0:T(8,128)}, f32[1,4,64,512]{3,2,1,0:T(8,128)S(1)}, u32[]{:S(2)}, u32[]{:S(2)}) collective-permute-start(f32[1,4,64,512]{3,2,1,0:T(8,128)} %refs_0_.2), channel_id=1, source_target_pairs={{0,1},{1,0},{2,3},{3,2},{4,5},{5,4},{6,7},{7,6},{8,9},{9,8},{10,11... | collective-permute-start | bytes 1572872 | tf_op jit(solution)/shard_map/ppermute | solution.py:19
  3.7 1.6 %collective-permute-start = (f32[4,9,64]{2,1,0:T(8,128)S(1)}, f32[4,9,64]{2,1,0:T(8,128)S(1)}, u32[]{:S(2)}, u32[]{:S(2)}) collective-permute-start(f32[4,9,64]{2,1,0:T(8,128)S(1)} %bitcast.21), channel_id=1, source_target_pairs={{0,1},{1,0},{2,3},{3,2},{4,5},{5,4},{6,7},{7,6},{8,9},{9,8},{10,11... | collective-permute-start | bytes 27656 | tf_op jit(solution)/shard_map/ppermute | solution.py:19
  5.4 10.4 %collective-permute-start.4 = (f32[4,9,128]{2,1,0:T(8,128)S(1)}, f32[4,9,128]{2,1,0:T(8,128)S(1)}, u32[]{:S(2)}, u32[]{:S(2)}) collective-permute-start(f32[4,9,128]{2,1,0:T(8,128)S(1)} %maximum_select_fusion.refs_0_.refs_4_), channel_id=1, source_target_pairs={{0,2},{1,3},{2,0},{3,1},{4,6},{5,7},{6,4},{7,5},{8,10},{9,11},{10,... | collective-permute-start | bytes 55304 | tf_op jit(solution)/shard_map/ppermute | solution.py:19
  6.0 13.7 %collective-permute-start.9 = (f32[16,16,512]{2,1,0:T(8,128)S(1)}, f32[16,16,512]{2,1,0:T(8,128)S(1)}, u32[]{:S(2)}, u32[]{:S(2)}) collective-permute-start(f32[16,16,512]{2,1,0:T(8,128)S(1)} %slice_bitcast_fusion.newest), channel_id=1, source_target_pairs={{0,8},{8,16},{16,24},{24,0},{1,9},{9,17},{17,25},{25,1},{2,10},{10... | collective-permute-start | bytes 1572872 | tf_op jit(solution)/shard_map/ppermute | solution.py:25
  14.2 5.5 %collective-permute-start.6 = (f32[1,4,64,512]{3,2,1,0:T(8,128)S(1)}, f32[1,4,64,512]{3,2,1,0:T(8,128)S(1)}, u32[]{:S(2)}, u32[]{:S(2)}) collective-permute-start(f32[1,4,64,512]{3,2,1,0:T(8,128)S(1)} %collective-permute-done.3.block.refs_3_.refs_2_), channel_id=1, source_target_pairs={{0,1},{1,0},{2,3},{3,2},{4,5},{5,4},{6,7},{7,6},{8,9},{9,8},{10,11... | collective-permute-start | bytes 1572872 | tf_op jit(solution)/shard_map/ppermute | solution.py:19
  16.2 3.5 %collective-permute-start.5 = (f32[1,4,64,512]{3,2,1,0:T(8,128)S(1)}, f32[1,4,64,512]{3,2,1,0:T(8,128)S(1)}, u32[]{:S(2)}, u32[]{:S(2)}) collective-permute-start(f32[1,4,64,512]{3,2,1,0:T(8,128)S(1)} %collective-permute-done.2.block.refs_2_.refs_1_), channel_id=1, source_target_pairs={{0,1},{1,0},{2,3},{3,2},{4,5},{5,4},{6,7},{7,6},{8,9},{9,8},{10,11... | collective-permute-start | bytes 1572872 | tf_op jit(solution)/shard_map/ppermute | solution.py:19
  16.2 9.8 %collective-permute-start.8 = (f32[1,152,512]{2,1,0:T(8,128)S(1)}, f32[1,152,512]{2,1,0:T(8,128)S(1)}, u32[]{:S(2)}, u32[]{:S(2)}) collective-permute-start(f32[1,152,512]{2,1,0:T(8,128)S(1)} %shard_map.46), channel_id=1, source_target_pairs={{0,4},{1,5},{2,6},{3,7},{4,0},{5,1},{6,2},{7,3},{8,12},{9,13},{10,... | collective-permute-start | bytes 933896 | tf_op jit(solution)/shard_map/ppermute | solution.py:19
  16.8 8.4 %collective-permute-start.7 = (f32[1,128,512]{2,1,0:T(8,128)S(1)}, f32[1,128,512]{2,1,0:T(8,128)S(1)}, u32[]{:S(2)}, u32[]{:S(2)}) collective-permute-start(f32[1,128,512]{2,1,0:T(8,128)S(1)} %shard_map.47), channel_id=1, source_target_pairs={{0,2},{1,3},{2,0},{3,1},{4,6},{5,7},{6,4},{7,5},{8,10},{9,11},{10,... | collective-permute-start | bytes 786440 | tf_op jit(solution)/shard_map/ppermute | solution.py:19
  20.1 2.7 %copy-start.1 = (f32[1,2,1,16,16,512]{5,4,3,2,1,0:T(8,128)S(1)}, f32[1,2,1,16,16,512]{5,4,3,2,1,0:T(8,128)}, u32[]{:S(2)}) copy-start(f32[1,2,1,16,16,512]{5,4,3,2,1,0:T(8,128)} %param.4) | copy-start | bytes 3145732
  20.3 50.3 %collective-permute-start.15 = (f32[3,1,4,64,512]{4,3,2,1,0:T(8,128)S(1)}, f32[3,1,4,64,512]{4,3,2,1,0:T(8,128)S(1)}, u32[]{:S(2)}, u32[]{:S(2)}) collective-permute-start(f32[3,1,4,64,512]{4,3,2,1,0:T(8,128)S(1)} %shard_map.55), channel_id=1, source_target_pairs={{8,0},{16,8},{24,16},{9,1},{17,9},{25,17},{10,2},{18,10},{26,18},{... | collective-permute-start | bytes 4718600 | tf_op jit(solution)/shard_map/ppermute | solution.py:29
  23.7 10.3 %copy-start = (f32[3,1,16,16,512]{4,3,2,1,0:T(8,128)S(1)}, f32[3,1,16,16,512]{4,3,2,1,0:T(8,128)}, u32[]{:S(2)}) copy-start(f32[3,1,16,16,512]{4,3,2,1,0:T(8,128)} %param.5) | copy-start | bytes 4718596
  26.0 2.0 %collective-permute-start.11 = (f32[1,152,512]{2,1,0:T(8,128)S(1)}, f32[1,152,512]{2,1,0:T(8,128)S(1)}, u32[]{:S(2)}, u32[]{:S(2)}) collective-permute-start(f32[1,152,512]{2,1,0:T(8,128)S(1)} %collective-permute-done.8.refs_2_.two), channel_id=1, source_target_pairs={{0,1},{1,0},{2,3},{3,2},{4,5},{5,4},{6,7},{7,6},{8,9},{9,8},{10,11... | collective-permute-start | bytes 933896 | tf_op jit(solution)/shard_map/ppermute | solution.py:19
  26.0 2.0 %collective-permute-start.10 = (f32[1,128,512]{2,1,0:T(8,128)S(1)}, f32[1,128,512]{2,1,0:T(8,128)S(1)}, u32[]{:S(2)}, u32[]{:S(2)}) collective-permute-start(f32[1,128,512]{2,1,0:T(8,128)S(1)} %collective-permute-done.7.refs_0_.one), channel_id=1, source_target_pairs={{0,1},{1,0},{2,3},{3,2},{4,5},{5,4},{6,7},{7,6},{8,9},{9,8},{10,11... | collective-permute-start | bytes 786440 | tf_op jit(solution)/shard_map/ppermute | solution.py:19
  30.5 15.9 %collective-permute-start.12 = (f32[16,16,512]{2,1,0:T(8,128)S(1)}, f32[16,16,512]{2,1,0:T(8,128)S(1)}, u32[]{:S(2)}, u32[]{:S(2)}) collective-permute-start(f32[16,16,512]{2,1,0:T(8,128)S(1)} %get-tuple-element.47.past), channel_id=1, source_target_pairs={{0,8},{8,16},{16,24},{1,9},{9,17},{17,25},{2,10},{10,18},{18,26},{... | collective-permute-start | bytes 1572872 | tf_op jit(solution)/shard_map/ppermute | solution.py:25
  34.9 35.6 %collective-permute-start.16 = (f32[1,296,512]{2,1,0:T(8,128)S(1)}, f32[1,296,512]{2,1,0:T(8,128)S(1)}, u32[]{:S(2)}, u32[]{:S(2)}) collective-permute-start(f32[1,296,512]{2,1,0:T(8,128)S(1)} %shard_map.56), channel_id=1, source_target_pairs={{8,0},{16,8},{24,16},{9,1},{17,9},{25,17},{10,2},{18,10},{26,18},{... | collective-permute-start | bytes 1818632 | tf_op jit(solution)/shard_map/ppermute | solution.py:29
  46.4 16.7 %collective-permute-start.14 = (f32[16,16,512]{2,1,0:T(8,128)S(1)}, f32[16,16,512]{2,1,0:T(8,128)S(1)}, u32[]{:S(2)}, u32[]{:S(2)}) collective-permute-start(f32[16,16,512]{2,1,0:T(8,128)S(1)} %collective-permute-done.12.got), channel_id=1, source_target_pairs={{8,16},{16,24},{9,17},{17,25},{10,18},{18,26},{11,19},{19,27},{12,... | collective-permute-start | bytes 1572872 | tf_op jit(solution)/shard_map/ppermute | solution.py:25
  52.1 20.5 %collective-permute-start.13 = (f32[16,16,512]{2,1,0:T(8,128)S(1)}, f32[16,16,512]{2,1,0:T(8,128)S(1)}, u32[]{:S(2)}, u32[]{:S(2)}) collective-permute-start(f32[16,16,512]{2,1,0:T(8,128)S(1)} %get-tuple-element.51.past), channel_id=1, source_target_pairs={{0,8},{8,16},{16,24},{1,9},{9,17},{17,25},{2,10},{10,18},{18,26},{... | collective-permute-start | bytes 1572872 | tf_op jit(solution)/shard_map/ppermute | solution.py:25
  70.5 4.4 %collective-permute-start.17 = (f32[3,1,4,64,512]{4,3,2,1,0:T(8,128)S(1)}, f32[3,1,4,64,512]{4,3,2,1,0:T(8,128)S(1)}, u32[]{:S(2)}, u32[]{:S(2)}) collective-permute-start(f32[3,1,4,64,512]{4,3,2,1,0:T(8,128)S(1)} %collective-permute-done.15.near), channel_id=1, source_target_pairs={{0,1},{1,0},{2,3},{3,2},{4,5},{5,4},{6,7},{7,6},{8,9},{9,8},{10,11... | collective-permute-start | bytes 4718600 | tf_op jit(solution)/shard_map/ppermute | solution.py:19
  70.5 4.4 %collective-permute-start.18 = (f32[1,296,512]{2,1,0:T(8,128)S(1)}, f32[1,296,512]{2,1,0:T(8,128)S(1)}, u32[]{:S(2)}, u32[]{:S(2)}) collective-permute-start(f32[1,296,512]{2,1,0:T(8,128)S(1)} %collective-permute-done.16.far), channel_id=1, source_target_pairs={{0,1},{1,0},{2,3},{3,2},{4,5},{5,4},{6,7},{7,6},{8,9},{9,8},{10,11... | collective-permute-start | bytes 1818632 | tf_op jit(solution)/shard_map/ppermute | solution.py:19
  78.7 15.7 %collective-permute-start.19 = (f32[16,16,512]{2,1,0:T(8,128)S(1)}, f32[16,16,512]{2,1,0:T(8,128)S(1)}, u32[]{:S(2)}, u32[]{:S(2)}) collective-permute-start(f32[16,16,512]{2,1,0:T(8,128)S(1)} %get-tuple-element.65), channel_id=1, source_target_pairs={{0,8},{8,16},{16,24},{1,9},{9,17},{17,25},{2,10},{10,18},{18,26},{... | collective-permute-start | bytes 1572872 | tf_op jit(solution)/shard_map/ppermute | solution.py:25

commit v5 on v3

--- a/solution.py
+++ b/solution.py
@@ -174,6 +174,34 @@
         apart=(1, 2, 8),
         outs_apart=(0,),
         aliases=None if emitted is None else {8: 0},
+    )
+
+
+def last_cell_kernel(tick, at, section, stems, got, newest, table, highs, lows, _, *rest):
+    emitted, out, earlier, first, second, sem = rest
+    load = fetch(tick, at, section[0], stems, got, earlier, sem.at[0])
+    store = begin(newest, emitted.at[tick], sem.at[1])
+    first[...] = separable(newest, table, highs, lows, 0)
+    load.wait()
+    first[...] += separable(earlier, table, highs, lows, 1)
+    second[...] = separable(first, table, highs, lows, 2) + newest[...]
+    out[...] = separable(second, table, highs, lows, 3) + first[...]
+    store.wait()
+
+
+def last_cell(tick, at, section, stems, got, newest, weights, emitted):
+    shape = got.shape
+    whole = jax.ShapeDtypeStruct(emitted.shape, F32)
+    return call(
+        functools.partial(last_cell_kernel, tick, at),
+        (whole, jax.ShapeDtypeStruct(shape, F32)),
+        (section, stems, got, newest, *weights, emitted),
+        [(shape, F32)] * 3,
+        2,
+        cost(shape, 7),
+        apart=(1, 2, 7),
+        outs_apart=(0,),
+        aliases={7: 0},
     )
 
 
@@ -526,9 +554,8 @@
         next_near, next_far, _ = lax.optimization_barrier((next_near, next_far, last_early))
         blocks = next_near, swap(next_near, "dp", 1), next_far, swap(next_far, "dp", 1)
         next_weights = next_part(position, *blocks, weights, lower)
-    early = early_part(held[0], held[1], section, stems, held[2], next_weights)
-    emitted, ahead = late_part(
-        ticks - 1, 0, section, stems, output, early, next_weights, output, emitted
+    emitted, ahead = last_cell(
+        held[0], held[1], section, stems, held[2], output, next_weights, emitted
     )
     got = from_behind(ahead, "section")
     emitted = last_part(section, got, stem_part(stems, weights), emitted)

time: 96.4 us -> 96.1 us (level)
    pallas_call x16 -> x15, Pallas kernels: 18.2 us -> 18 us  [call(): pl.pallas_call(kernel, out_shape=outs, in_specs=[spec(x, i, apart) for i,...]
where the time goes in v5:
time: 96.1 us; the launch traced here: 95.2 us
  waiting for transfers between devices  48.7 us (51%)
  starting transfers between devices  26.2 us (27%)
  Pallas kernels  18 us (19%)
  local copies, waits for them, and re-layouts  1.82 us (2%)
    ppermute x5, waiting for transfers between devices, from_behind(): lax.ppermute(x, axis, pairs + [(size - 1, 0)] * (around and size > 1))  30.6 us
    pallas_call x15, Pallas kernels, call(): pl.pallas_call(kernel, out_shape=outs, in_specs=[spec(x, i, apart) for i,...  18 us
    ppermute x5, starting transfers between devices, from_behind(): lax.ppermute(x, axis, pairs + [(size - 1, 0)] * (around and size > 1))  14 us
    ppermute x13, waiting for transfers between devices, swap(): return lax.ppermute(x, axis, [(i, i ^ bit) for i in range(size)])  11.9 us
    ppermute x13, starting transfers between devices, swap(): return lax.ppermute(x, axis, [(i, i ^ bit) for i in range(size)])  7.35 us
    ppermute x2, waiting for transfers between devices, from_ahead(): lax.ppermute(x, axis, [(i + 1, i) for i in range(lax.axis_size(axis) - 1)])  6.21 us
    ppermute x2, starting transfers between devices, from_ahead(): lax.ppermute(x, axis, [(i + 1, i) for i in range(lax.axis_size(axis) - 1)])  4.82 us
  transfers between devices with their start and end apart: 20, of which 12 were waited for; matrix products, arithmetic and copies ran while one was open for 2% of the time, Pallas kernels for 14%

profile of v5, /device:TPU:16, one launch (start us, length us, event | category | flops | bytes accessed | tf_op | source)
XLA Modules:
  0.0 95.2 jit_solution(3778666686475586594)
XLA Ops:
  0.0 1.5 %collective-permute-start.3 = (f32[1,4,64,512]{3,2,1,0:T(8,128)}, f32[1,4,64,512]{3,2,1,0:T(8,128)S(1)}, u32[]{:S(2)}, u32[]{:S(2)}) collective-permute-start(f32[1,4,64,512]{3,2,1,0:T(8,128)} %refs_0_.2), channel_id=1, source_target_pairs={{0,4},{1,5},{2,6},{3,7},{4,0},{5,1},{6,2},{7,3},{8,12},{9,13},{10,... | collective-permute-start | bytes 1572872 | tf_op jit(solution)/shard_map/ppermute | solution.py:20
  1.5 1.5 %collective-permute-start.2 = (f32[1,4,64,512]{3,2,1,0:T(8,128)}, f32[1,4,64,512]{3,2,1,0:T(8,128)S(1)}, u32[]{:S(2)}, u32[]{:S(2)}) collective-permute-start(f32[1,4,64,512]{3,2,1,0:T(8,128)} %refs_0_.2), channel_id=1, source_target_pairs={{0,2},{1,3},{2,0},{3,1},{4,6},{5,7},{6,4},{7,5},{8,10},{9,11},{10,... | collective-permute-start | bytes 1572872 | tf_op jit(solution)/shard_map/ppermute | solution.py:20
  6.0 1.6 %collective-permute-start.9 = (f32[16,16,512]{2,1,0:T(8,128)S(1)}, f32[16,16,512]{2,1,0:T(8,128)S(1)}, u32[]{:S(2)}, u32[]{:S(2)}) collective-permute-start(f32[16,16,512]{2,1,0:T(8,128)S(1)} %slice_bitcast_fusion.newest), channel_id=1, source_target_pairs={{0,8},{8,16},{16,24},{24,0},{1,9},{9,17},{17,25},{25,1},{2,10},{10... | collective-permute-start | bytes 1572872 | tf_op jit(solution)/shard_map/ppermute | solution.py:26
  7.6 6.3 %collective-permute-done.3.block.refs_3_.refs_2_ = f32[1,4,64,512]{3,2,1,0:T(8,128)S(1)} collective-permute-done((f32[1,4,64,512]{3,2,1,0:T(8,128)}, f32[1,4,64,512]{3,2,1,0:T(8,128)S(1)}, u32[]{:S(2)}, u32[]{:S(2)}) %collective-permute-start.3) | collective-permute-done | bytes 524320 | tf_op jit(solution)/shard_map/ppermute | solution.py:20
  16.8 1.5 %collective-permute-start.7 = (f32[1,128,512]{2,1,0:T(8,128)S(1)}, f32[1,128,512]{2,1,0:T(8,128)S(1)}, u32[]{:S(2)}, u32[]{:S(2)}) collective-permute-start(f32[1,128,512]{2,1,0:T(8,128)S(1)} %shard_map.47), channel_id=1, source_target_pairs={{0,2},{1,3},{2,0},{3,1},{4,6},{5,7},{6,4},{7,5},{8,10},{9,11},{10,... | collective-permute-start | bytes 786440 | tf_op jit(solution)/shard_map/ppermute | solution.py:20
  18.3 1.4 %collective-permute-done.9.got = f32[16,16,512]{2,1,0:T(8,128)S(1)} collective-permute-done((f32[16,16,512]{2,1,0:T(8,128)S(1)}, f32[16,16,512]{2,1,0:T(8,128)S(1)}, u32[]{:S(2)}, u32[]{:S(2)}) %collective-permute-start.9) | collective-permute-done | bytes 524320 | tf_op jit(solution)/shard_map/ppermute | solution.py:26
  20.3 2.5 %collective-permute-start.15 = (f32[3,1,4,64,512]{4,3,2,1,0:T(8,128)S(1)}, f32[3,1,4,64,512]{4,3,2,1,0:T(8,128)S(1)}, u32[]{:S(2)}, u32[]{:S(2)}) collective-permute-start(f32[3,1,4,64,512]{4,3,2,1,0:T(8,128)S(1)} %shard_map.55), channel_id=1, source_target_pairs={{8,0},{16,8},{24,16},{9,1},{17,9},{25,17},{10,2},{18,10},{26,18},{... | collective-permute-start | bytes 4718600 | tf_op jit(solution)/shard_map/ppermute | solution.py:30
  23.7 1.5 %collective-permute-done.7.refs_0_.one = f32[1,128,512]{2,1,0:T(8,128)S(1)} collective-permute-done((f32[1,128,512]{2,1,0:T(8,128)S(1)}, f32[1,128,512]{2,1,0:T(8,128)S(1)}, u32[]{:S(2)}, u32[]{:S(2)}) %collective-permute-start.7) | collective-permute-done | bytes 262176 | tf_op jit(solution)/shard_map/ppermute | solution.py:20
  26.9 1.5 %collective-permute-done.10.refs_1_ = f32[1,128,512]{2,1,0:T(8,128)S(1)} collective-permute-done((f32[1,128,512]{2,1,0:T(8,128)S(1)}, f32[1,128,512]{2,1,0:T(8,128)S(1)}, u32[]{:S(2)}, u32[]{:S(2)}) %collective-permute-start.10) | collective-permute-done | bytes 262176 | tf_op jit(solution)/shard_map/ppermute | solution.py:20
  28.4 2.5 %shard_map.50 = (f32[16,16,512]{2,1,0:T(8,128)S(1)}, bf16[4,512,512]{2,1,0:T(8,128)(2,1)S(1)}, bf16[4,512,512]{2,1,0:T(8,128)(2,1)S(1)}, f32[4,4,9,128]{3,2,1,0:T(8,128)S(1)}) custom-call(s32[1]{0:T(128)} %bitcast.2.position, f32[16,16,512]{2,1,0:T(8,128)S(1)} %slice_bitcast_fusion.newest, ...), custom_call_target="tpu_custom_call", output_to_operand_aliasing={{1}: (3, {}), {2}: (4, {})} | custom-call | flops 1610612736 | bytes 5767168 | tf_op jit(solution)/shard_map/pallas_call | solution.py:53
  30.9 3.5 %collective-permute-start.12 = (f32[16,16,512]{2,1,0:T(8,128)S(1)}, f32[16,16,512]{2,1,0:T(8,128)S(1)}, u32[]{:S(2)}, u32[]{:S(2)}) collective-permute-start(f32[16,16,512]{2,1,0:T(8,128)S(1)} %get-tuple-element.47.past), channel_id=1, source_target_pairs={{0,8},{8,16},{16,24},{1,9},{9,17},{17,25},{2,10},{10,18},{18,26},{... | collective-permute-start | bytes 1572872 | tf_op jit(solution)/shard_map/ppermute | solution.py:26
  35.3 2.3 %collective-permute-start.16 = (f32[1,296,512]{2,1,0:T(8,128)S(1)}, f32[1,296,512]{2,1,0:T(8,128)S(1)}, u32[]{:S(2)}, u32[]{:S(2)}) collective-permute-start(f32[1,296,512]{2,1,0:T(8,128)S(1)} %shard_map.56), channel_id=1, source_target_pairs={{8,0},{16,8},{24,16},{9,1},{17,9},{25,17},{10,2},{18,10},{26,18},{... | collective-permute-start | bytes 1818632 | tf_op jit(solution)/shard_map/ppermute | solution.py:30
  37.7 9.1 %collective-permute-done.12.got = f32[16,16,512]{2,1,0:T(8,128)S(1)} collective-permute-done((f32[16,16,512]{2,1,0:T(8,128)S(1)}, f32[16,16,512]{2,1,0:T(8,128)S(1)}, u32[]{:S(2)}, u32[]{:S(2)}) %collective-permute-start.12) | collective-permute-done | bytes 524320 | tf_op jit(solution)/shard_map/ppermute | solution.py:26
  46.7 3.5 %collective-permute-start.14 = (f32[16,16,512]{2,1,0:T(8,128)S(1)}, f32[16,16,512]{2,1,0:T(8,128)S(1)}, u32[]{:S(2)}, u32[]{:S(2)}) collective-permute-start(f32[16,16,512]{2,1,0:T(8,128)S(1)} %collective-permute-done.12.got), channel_id=1, source_target_pairs={{8,16},{16,24},{9,17},{17,25},{10,18},{18,26},{11,19},{19,27},{12,... | collective-permute-start | bytes 1572872 | tf_op jit(solution)/shard_map/ppermute | solution.py:26
  50.2 2.3 %shard_map.52 = (f32[4,16,16,512]{3,2,1,0:T(8,128)}, f32[16,16,512]{2,1,0:T(8,128)S(1)}) custom-call(s32[1]{0:T(128)} %bitcast.section, f32[3,16,16,512]{3,2,1,0:T(8,128)S(1)} %bitcast.13, f32[16,16,512]{2,1,0:T(8,128)S(1)} %collective-permute-done.12.got, f32[16,16,512]{2,1,0:T(8,128)S(1)} %shard_map.51.early, ...), custom_call_target="tpu_custom_call" | custom-call | flops 2415919104 | bytes 7864320 | tf_op jit(solution)/shard_map/pallas_call | solution.py:53
  52.5 1.9 %collective-permute-start.13 = (f32[16,16,512]{2,1,0:T(8,128)S(1)}, f32[16,16,512]{2,1,0:T(8,128)S(1)}, u32[]{:S(2)}, u32[]{:S(2)}) collective-permute-start(f32[16,16,512]{2,1,0:T(8,128)S(1)} %get-tuple-element.51.past), channel_id=1, source_target_pairs={{0,8},{8,16},{16,24},{1,9},{9,17},{17,25},{2,10},{10,18},{18,26},{... | collective-permute-start | bytes 1572872 | tf_op jit(solution)/shard_map/ppermute | solution.py:26
  54.4 9.1 %collective-permute-done.14.got = f32[16,16,512]{2,1,0:T(8,128)S(1)} collective-permute-done((f32[16,16,512]{2,1,0:T(8,128)S(1)}, f32[16,16,512]{2,1,0:T(8,128)S(1)}, u32[]{:S(2)}, u32[]{:S(2)}) %collective-permute-start.14) | collective-permute-done | bytes 524320 | tf_op jit(solution)/shard_map/ppermute | solution.py:26
  64.3 6.2 %collective-permute-done.16.far = f32[1,296,512]{2,1,0:T(8,128)S(1)} collective-permute-done((f32[1,296,512]{2,1,0:T(8,128)S(1)}, f32[1,296,512]{2,1,0:T(8,128)S(1)}, u32[]{:S(2)}, u32[]{:S(2)}) %collective-permute-start.16) | collective-permute-done | bytes 606240 | tf_op jit(solution)/shard_map/ppermute | solution.py:30
  71.0 2.0 %collective-permute-done.13.got = f32[16,16,512]{2,1,0:T(8,128)S(1)} collective-permute-done((f32[16,16,512]{2,1,0:T(8,128)S(1)}, f32[16,16,512]{2,1,0:T(8,128)S(1)}, u32[]{:S(2)}, u32[]{:S(2)}) %collective-permute-start.13) | collective-permute-done | bytes 524320 | tf_op jit(solution)/shard_map/ppermute | solution.py:26
  73.0 2.3 %shard_map.54 = (f32[4,16,16,512]{3,2,1,0:T(8,128)}, f32[16,16,512]{2,1,0:T(8,128)S(1)}) custom-call(s32[1]{0:T(128)} %bitcast.section, f32[3,16,16,512]{3,2,1,0:T(8,128)S(1)} %bitcast.15, f32[16,16,512]{2,1,0:T(8,128)S(1)} %collective-permute-done.13.got, f32[16,16,512]{2,1,0:T(8,128)S(1)} %shard_map.53.early, ...), custom_call_target="tpu_custom_call", output_to_operand_aliasing={{0}: (8, {})} | custom-call | flops 14495514624 | bytes 39321600 | tf_op jit(solution)/shard_map/pallas_call | solution.py:53
  75.8 3.0 %shard_map.58 = (f32[4,16,16,512]{3,2,1,0:T(8,128)}, f32[16,16,512]{2,1,0:T(8,128)S(1)}) custom-call(s32[1]{0:T(128)} %bitcast.section, f32[3,16,16,512]{3,2,1,0:T(8,128)S(1)} %bitcast.16, f32[16,16,512]{2,1,0:T(8,128)S(1)} %collective-permute-done.13.got, f32[16,16,512]{2,1,0:T(8,128)S(1)} %get-tuple-element.54.newest, ...), custom_call_target="tpu_custom_call", output_to_operand_aliasing={{0}: (7, {})} | custom-call | flops 2818572288 | bytes 8912896 | tf_op jit(solution)/shard_map/pallas_call | solution.py:53
  78.8 3.5 %collective-permute-start.19 = (f32[16,16,512]{2,1,0:T(8,128)S(1)}, f32[16,16,512]{2,1,0:T(8,128)S(1)}, u32[]{:S(2)}, u32[]{:S(2)}) collective-permute-start(f32[16,16,512]{2,1,0:T(8,128)S(1)} %get-tuple-element.65), channel_id=1, source_target_pairs={{0,8},{8,16},{16,24},{1,9},{9,17},{17,25},{2,10},{10,18},{18,26},{... | collective-permute-start | bytes 1572872 | tf_op jit(solution)/shard_map/ppermute | solution.py:26
  82.4 2.8 %shard_map.59.own = f32[16,16,512]{2,1,0:T(8,128)S(1)} custom-call(f32[3,16,16,512]{3,2,1,0:T(8,128)S(1)} %bitcast.17, f32[4,4,9,128]{3,2,1,0:T(8,128)S(1)} %get-tuple-element.48.table, bf16[4,512,512]{2,1,0:T(8,128)(2,1)S(1)} %get-tuple-element.49.highs, bf16[4,512,512]{2,1,0:T(8,128)(2,1)S(1)} %get-tuple-element.50.lows), custom_call_target="tpu_custom_call" | custom-call | flops 1610612736 | bytes 5767168 | tf_op jit(solution)/shard_map/pallas_call | solution.py:53
  85.1 9.1 %collective-permute-done.19.got = f32[16,16,512]{2,1,0:T(8,128)S(1)} collective-permute-done((f32[16,16,512]{2,1,0:T(8,128)S(1)}, f32[16,16,512]{2,1,0:T(8,128)S(1)}, u32[]{:S(2)}, u32[]{:S(2)}) %collective-permute-start.19) | collective-permute-done | bytes 524320 | tf_op jit(solution)/shard_map/ppermute | solution.py:26
  (40 shorter events, 12.6 us)
Async XLA Ops:
  0.0 19.7 %copy-start.2 = (f32[1,4,64,512]{3,2,1,0:T(8,128)S(1)}, f32[1,4,64,512]{3,2,1,0:T(8,128)}, u32[]{:S(2)}) copy-start(f32[1,4,64,512]{3,2,1,0:T(8,128)} %refs_0_.2) | copy-start | bytes 1572868
  0.0 13.9 %collective-permute-start.3 = (f32[1,4,64,512]{3,2,1,0:T(8,128)}, f32[1,4,64,512]{3,2,1,0:T(8,128)S(1)}, u32[]{:S(2)}, u32[]{:S(2)}) collective-permute-start(f32[1,4,64,512]{3,2,1,0:T(8,128)} %refs_0_.2), channel_id=1, source_target_pairs={{0,4},{1,5},{2,6},{3,7},{4,0},{5,1},{6,2},{7,3},{8,12},{9,13},{10,... | collective-permute-start | bytes 1572872 | tf_op jit(solution)/shard_map/ppermute | solution.py:20
  1.5 13.9 %collective-permute-start.2 = (f32[1,4,64,512]{3,2,1,0:T(8,128)}, f32[1,4,64,512]{3,2,1,0:T(8,128)S(1)}, u32[]{:S(2)}, u32[]{:S(2)}) collective-permute-start(f32[1,4,64,512]{3,2,1,0:T(8,128)} %refs_0_.2), channel_id=1, source_target_pairs={{0,2},{1,3},{2,0},{3,1},{4,6},{5,7},{6,4},{7,5},{8,10},{9,11},{10,... | collective-permute-start | bytes 1572872 | tf_op jit(solution)/shard_map/ppermute | solution.py:20
  3.0 12.5 %collective-permute-start.1 = (f32[1,4,64,512]{3,2,1,0:T(8,128)}, f32[1,4,64,512]{3,2,1,0:T(8,128)S(1)}, u32[]{:S(2)}, u32[]{:S(2)}) collective-permute-start(f32[1,4,64,512]{3,2,1,0:T(8,128)} %refs_0_.2), channel_id=1, source_target_pairs={{0,1},{1,0},{2,3},{3,2},{4,5},{5,4},{6,7},{7,6},{8,9},{9,8},{10,11... | collective-permute-start | bytes 1572872 | tf_op jit(solution)/shard_map/ppermute | solution.py:20
  3.7 1.6 %collective-permute-start = (f32[4,9,64]{2,1,0:T(8,128)S(1)}, f32[4,9,64]{2,1,0:T(8,128)S(1)}, u32[]{:S(2)}, u32[]{:S(2)}) collective-permute-start(f32[4,9,64]{2,1,0:T(8,128)S(1)} %bitcast.20), channel_id=1, source_target_pairs={{0,1},{1,0},{2,3},{3,2},{4,5},{5,4},{6,7},{7,6},{8,9},{9,8},{10,11... | collective-permute-start | bytes 27656 | tf_op jit(solution)/shard_map/ppermute | solution.py:20
  5.4 10.4 %collective-permute-start.4 = (f32[4,9,128]{2,1,0:T(8,128)S(1)}, f32[4,9,128]{2,1,0:T(8,128)S(1)}, u32[]{:S(2)}, u32[]{:S(2)}) collective-permute-start(f32[4,9,128]{2,1,0:T(8,128)S(1)} %maximum_select_fusion.refs_0_.refs_4_), channel_id=1, source_target_pairs={{0,2},{1,3},{2,0},{3,1},{4,6},{5,7},{6,4},{7,5},{8,10},{9,11},{10,... | collective-permute-start | bytes 55304 | tf_op jit(solution)/shard_map/ppermute | solution.py:20
  6.0 13.7 %collective-permute-start.9 = (f32[16,16,512]{2,1,0:T(8,128)S(1)}, f32[16,16,512]{2,1,0:T(8,128)S(1)}, u32[]{:S(2)}, u32[]{:S(2)}) collective-permute-start(f32[16,16,512]{2,1,0:T(8,128)S(1)} %slice_bitcast_fusion.newest), channel_id=1, source_target_pairs={{0,8},{8,16},{16,24},{24,0},{1,9},{9,17},{17,25},{25,1},{2,10},{10... | collective-permute-start | bytes 1572872 | tf_op jit(solution)/shard_map/ppermute | solution.py:26
  14.2 5.5 %collective-permute-start.6 = (f32[1,4,64,512]{3,2,1,0:T(8,128)S(1)}, f32[1,4,64,512]{3,2,1,0:T(8,128)S(1)}, u32[]{:S(2)}, u32[]{:S(2)}) collective-permute-start(f32[1,4,64,512]{3,2,1,0:T(8,128)S(1)} %collective-permute-done.3.block.refs_3_.refs_2_), channel_id=1, source_target_pairs={{0,1},{1,0},{2,3},{3,2},{4,5},{5,4},{6,7},{7,6},{8,9},{9,8},{10,11... | collective-permute-start | bytes 1572872 | tf_op jit(solution)/shard_map/ppermute | solution.py:20
  16.2 3.5 %collective-permute-start.5 = (f32[1,4,64,512]{3,2,1,0:T(8,128)S(1)}, f32[1,4,64,512]{3,2,1,0:T(8,128)S(1)}, u32[]{:S(2)}, u32[]{:S(2)}) collective-permute-start(f32[1,4,64,512]{3,2,1,0:T(8,128)S(1)} %collective-permute-done.2.block.refs_2_.refs_1_), channel_id=1, source_target_pairs={{0,1},{1,0},{2,3},{3,2},{4,5},{5,4},{6,7},{7,6},{8,9},{9,8},{10,11... | collective-permute-start | bytes 1572872 | tf_op jit(solution)/shard_map/ppermute | solution.py:20
  16.2 10.1 %collective-permute-start.8 = (f32[1,160,512]{2,1,0:T(8,128)S(1)}, f32[1,160,512]{2,1,0:T(8,128)S(1)}, u32[]{:S(2)}, u32[]{:S(2)}) collective-permute-start(f32[1,160,512]{2,1,0:T(8,128)S(1)} %shard_map.46), channel_id=1, source_target_pairs={{0,4},{1,5},{2,6},{3,7},{4,0},{5,1},{6,2},{7,3},{8,12},{9,13},{10,... | collective-permute-start | bytes 983048 | tf_op jit(solution)/shard_map/ppermute | solution.py:20
  16.8 8.4 %collective-permute-start.7 = (f32[1,128,512]{2,1,0:T(8,128)S(1)}, f32[1,128,512]{2,1,0:T(8,128)S(1)}, u32[]{:S(2)}, u32[]{:S(2)}) collective-permute-start(f32[1,128,512]{2,1,0:T(8,128)S(1)} %shard_map.47), channel_id=1, source_target_pairs={{0,2},{1,3},{2,0},{3,1},{4,6},{5,7},{6,4},{7,5},{8,10},{9,11},{10,... | collective-permute-start | bytes 786440 | tf_op jit(solution)/shard_map/ppermute | solution.py:20
  20.1 2.7 %copy-start.1 = (f32[1,2,1,16,16,512]{5,4,3,2,1,0:T(8,128)S(1)}, f32[1,2,1,16,16,512]{5,4,3,2,1,0:T(8,128)}, u32[]{:S(2)}) copy-start(f32[1,2,1,16,16,512]{5,4,3,2,1,0:T(8,128)} %param.4) | copy-start | bytes 3145732
  20.3 50.3 %collective-permute-start.15 = (f32[3,1,4,64,512]{4,3,2,1,0:T(8,128)S(1)}, f32[3,1,4,64,512]{4,3,2,1,0:T(8,128)S(1)}, u32[]{:S(2)}, u32[]{:S(2)}) collective-permute-start(f32[3,1,4,64,512]{4,3,2,1,0:T(8,128)S(1)} %shard_map.55), channel_id=1, source_target_pairs={{8,0},{16,8},{24,16},{9,1},{17,9},{25,17},{10,2},{18,10},{26,18},{... | collective-permute-start | bytes 4718600 | tf_op jit(solution)/shard_map/ppermute | solution.py:30
  23.7 10.7 %copy-start = (f32[3,1,16,16,512]{4,3,2,1,0:T(8,128)S(1)}, f32[3,1,16,16,512]{4,3,2,1,0:T(8,128)}, u32[]{:S(2)}) copy-start(f32[3,1,16,16,512]{4,3,2,1,0:T(8,128)} %param.5) | copy-start | bytes 4718596
  26.4 2.0 %collective-permute-start.11 = (f32[1,160,512]{2,1,0:T(8,128)S(1)}, f32[1,160,512]{2,1,0:T(8,128)S(1)}, u32[]{:S(2)}, u32[]{:S(2)}) collective-permute-start(f32[1,160,512]{2,1,0:T(8,128)S(1)} %collective-permute-done.8.refs_2_.two), channel_id=1, source_target_pairs={{0,1},{1,0},{2,3},{3,2},{4,5},{5,4},{6,7},{7,6},{8,9},{9,8},{10,11... | collective-permute-start | bytes 983048 | tf_op jit(solution)/shard_map/ppermute | solution.py:20
  26.4 2.0 %collective-permute-start.10 = (f32[1,128,512]{2,1,0:T(8,128)S(1)}, f32[1,128,512]{2,1,0:T(8,128)S(1)}, u32[]{:S(2)}, u32[]{:S(2)}) collective-permute-start(f32[1,128,512]{2,1,0:T(8,128)S(1)} %collective-permute-done.7.refs_0_.one), channel_id=1, source_target_pairs={{0,1},{1,0},{2,3},{3,2},{4,5},{5,4},{6,7},{7,6},{8,9},{9,8},{10,11... | collective-permute-start | bytes 786440 | tf_op jit(solution)/shard_map/ppermute | solution.py:20
  30.9 15.9 %collective-permute-start.12 = (f32[16,16,512]{2,1,0:T(8,128)S(1)}, f32[16,16,512]{2,1,0:T(8,128)S(1)}, u32[]{:S(2)}, u32[]{:S(2)}) collective-permute-start(f32[16,16,512]{2,1,0:T(8,128)S(1)} %get-tuple-element.47.past), channel_id=1, source_target_pairs={{0,8},{8,16},{16,24},{1,9},{9,17},{17,25},{2,10},{10,18},{18,26},{... | collective-permute-start | bytes 1572872 | tf_op jit(solution)/shard_map/ppermute | solution.py:26
  35.3 35.2 %collective-permute-start.16 = (f32[1,296,512]{2,1,0:T(8,128)S(1)}, f32[1,296,512]{2,1,0:T(8,128)S(1)}, u32[]{:S(2)}, u32[]{:S(2)}) collective-permute-start(f32[1,296,512]{2,1,0:T(8,128)S(1)} %shard_map.56), channel_id=1, source_target_pairs={{8,0},{16,8},{24,16},{9,1},{17,9},{25,17},{10,2},{18,10},{26,18},{... | collective-permute-start | bytes 1818632 | tf_op jit(solution)/shard_map/ppermute | solution.py:30
  46.7 16.7 %collective-permute-start.14 = (f32[16,16,512]{2,1,0:T(8,128)S(1)}, f32[16,16,512]{2,1,0:T(8,128)S(1)}, u32[]{:S(2)}, u32[]{:S(2)}) collective-permute-start(f32[16,16,512]{2,1,0:T(8,128)S(1)} %collective-permute-done.12.got), channel_id=1, source_target_pairs={{8,16},{16,24},{9,17},{17,25},{10,18},{18,26},{11,19},{19,27},{12,... | collective-permute-start | bytes 1572872 | tf_op jit(solution)/shard_map/ppermute | solution.py:26
  52.5 20.5 %collective-permute-start.13 = (f32[16,16,512]{2,1,0:T(8,128)S(1)}, f32[16,16,512]{2,1,0:T(8,128)S(1)}, u32[]{:S(2)}, u32[]{:S(2)}) collective-permute-start(f32[16,16,512]{2,1,0:T(8,128)S(1)} %get-tuple-element.51.past), channel_id=1, source_target_pairs={{0,8},{8,16},{16,24},{1,9},{9,17},{17,25},{2,10},{10,18},{18,26},{... | collective-permute-start | bytes 1572872 | tf_op jit(solution)/shard_map/ppermute | solution.py:26
  70.5 4.7 %collective-permute-start.17 = (f32[3,1,4,64,512]{4,3,2,1,0:T(8,128)S(1)}, f32[3,1,4,64,512]{4,3,2,1,0:T(8,128)S(1)}, u32[]{:S(2)}, u32[]{:S(2)}) collective-permute-start(f32[3,1,4,64,512]{4,3,2,1,0:T(8,128)S(1)} %collective-permute-done.15.near), channel_id=1, source_target_pairs={{0,1},{1,0},{2,3},{3,2},{4,5},{5,4},{6,7},{7,6},{8,9},{9,8},{10,11... | collective-permute-start | bytes 4718600 | tf_op jit(solution)/shard_map/ppermute | solution.py:20
  70.5 4.7 %collective-permute-start.18 = (f32[1,296,512]{2,1,0:T(8,128)S(1)}, f32[1,296,512]{2,1,0:T(8,128)S(1)}, u32[]{:S(2)}, u32[]{:S(2)}) collective-permute-start(f32[1,296,512]{2,1,0:T(8,128)S(1)} %collective-permute-done.16.far), channel_id=1, source_target_pairs={{0,1},{1,0},{2,3},{3,2},{4,5},{5,4},{6,7},{7,6},{8,9},{9,8},{10,11... | collective-permute-start | bytes 1818632 | tf_op jit(solution)/shard_map/ppermute | solution.py:20
  78.8 15.4 %collective-permute-start.19 = (f32[16,16,512]{2,1,0:T(8,128)S(1)}, f32[16,16,512]{2,1,0:T(8,128)S(1)}, u32[]{:S(2)}, u32[]{:S(2)}) collective-permute-start(f32[16,16,512]{2,1,0:T(8,128)S(1)} %get-tuple-element.65), channel_id=1, source_target_pairs={{0,8},{8,16},{16,24},{1,9},{9,17},{17,25},{2,10},{10,18},{18,26},{... | collective-permute-start | bytes 1572872 | tf_op jit(solution)/shard_map/ppermute | solution.py:26

commit v6 on v5

--- a/solution.py
+++ b/solution.py
@@ -12,7 +12,6 @@
 VMEM_LIMIT = 16 * 1024 * 1024
 LANES = 128
 DEPTH = 256
-TAP_ROWS = 16
 
 
 def swap(x, axis, bit):
@@ -285,7 +284,7 @@
             target = out.at[u, pl.ds(i * count, count)]
             copies.append(begin(block.at[u, start + i], target, sem.at[u * half + i]))
     for j, chip in enumerate(taps):
-        row = half * count + j * TAP_ROWS
+        row = half * count + j * chip.shape[1]
         for n in range(branches):
             out[0, row : row + 9, n * LANES : (n + 1) * LANES] = chip[n]
     for copy in copies:
@@ -295,7 +294,8 @@
 def half_of(block, start, *taps):
     uppers, branches, count, channels = block.shape
     half = branches // 2
-    out = jax.ShapeDtypeStruct((uppers, half * count + TAP_ROWS * len(taps), channels), F32)
+    extra = -(-sum(chip.shape[1] for chip in taps) // 8) * 8
+    out = jax.ShapeDtypeStruct((uppers, half * count + extra, channels), F32)
     work = pl.CostEstimate(flops=0, bytes_accessed=4 * block.size, transcendentals=0)
     kernel = functools.partial(half_kernel, start * half)
     return call(kernel, (out,), (block, *taps), [], half * uppers, work)[0]
@@ -419,7 +419,7 @@
     else:
         below = far[2]
         for j, part in enumerate(taps):
-            row = below.shape[1] - (n_taps - j) * TAP_ROWS
+            row = far[0].shape[1] + j * part.shape[1]
             for n in range(branches):
                 table[chip ^ j, n] = part[n]
                 lanes = slice(n * LANES, (n + 1) * LANES)

time: 96.1 us -> 96.1 us (level)
  no operation moved by 1% of the time
where the time goes in v6:
time: 96.1 us; the launch traced here: 95.2 us
  waiting for transfers between devices  48.8 us (51%)
  starting transfers between devices  26.1 us (27%)
  Pallas kernels  18 us (19%)
  local copies, waits for them, and re-layouts  1.82 us (2%)
    ppermute x5, waiting for transfers between devices, from_behind(): lax.ppermute(x, axis, pairs + [(size - 1, 0)] * (around and size > 1))  30.6 us
    pallas_call x15, Pallas kernels, call(): pl.pallas_call(kernel, out_shape=outs, in_specs=[spec(x, i, apart) for i,...  18 us
    ppermute x5, starting transfers between devices, from_behind(): lax.ppermute(x, axis, pairs + [(size - 1, 0)] * (around and size > 1))  13.9 us
    ppermute x13, waiting for transfers between devices, swap(): return lax.ppermute(x, axis, [(i, i ^ bit) for i in range(size)])  11.6 us
    ppermute x13, starting transfers between devices, swap(): return lax.ppermute(x, axis, [(i, i ^ bit) for i in range(size)])  7.35 us
    ppermute x2, waiting for transfers between devices, from_ahead(): lax.ppermute(x, axis, [(i + 1, i) for i in range(lax.axis_size(axis) - 1)])  6.58 us
    ppermute x2, starting transfers between devices, from_ahead(): lax.ppermute(x, axis, [(i + 1, i) for i in range(lax.axis_size(axis) - 1)])  4.85 us
  transfers between devices with their start and end apart: 20, of which 12 were waited for; matrix products, arithmetic and copies ran while one was open for 2% of the time, Pallas kernels for 14%

profile of v6, /device:TPU:16, one launch (start us, length us, event | category | flops | bytes accessed | tf_op | source)
XLA Modules:
  0.0 95.2 jit_solution(18024137121502232692)
XLA Ops:
  0.0 1.5 %collective-permute-start.3 = (f32[1,4,64,512]{3,2,1,0:T(8,128)}, f32[1,4,64,512]{3,2,1,0:T(8,128)S(1)}, u32[]{:S(2)}, u32[]{:S(2)}) collective-permute-start(f32[1,4,64,512]{3,2,1,0:T(8,128)} %refs_0_.2), channel_id=1, source_target_pairs={{0,4},{1,5},{2,6},{3,7},{4,0},{5,1},{6,2},{7,3},{8,12},{9,13},{10,... | collective-permute-start | bytes 1572872 | tf_op jit(solution)/shard_map/ppermute | solution.py:19
  1.5 1.5 %collective-permute-start.2 = (f32[1,4,64,512]{3,2,1,0:T(8,128)}, f32[1,4,64,512]{3,2,1,0:T(8,128)S(1)}, u32[]{:S(2)}, u32[]{:S(2)}) collective-permute-start(f32[1,4,64,512]{3,2,1,0:T(8,128)} %refs_0_.2), channel_id=1, source_target_pairs={{0,2},{1,3},{2,0},{3,1},{4,6},{5,7},{6,4},{7,5},{8,10},{9,11},{10,... | collective-permute-start | bytes 1572872 | tf_op jit(solution)/shard_map/ppermute | solution.py:19
  6.0 1.6 %collective-permute-start.9 = (f32[16,16,512]{2,1,0:T(8,128)S(1)}, f32[16,16,512]{2,1,0:T(8,128)S(1)}, u32[]{:S(2)}, u32[]{:S(2)}) collective-permute-start(f32[16,16,512]{2,1,0:T(8,128)S(1)} %slice_bitcast_fusion.newest), channel_id=1, source_target_pairs={{0,8},{8,16},{16,24},{24,0},{1,9},{9,17},{17,25},{25,1},{2,10},{10... | collective-permute-start | bytes 1572872 | tf_op jit(solution)/shard_map/ppermute | solution.py:25
  7.6 6.3 %collective-permute-done.3.block.refs_3_.refs_2_ = f32[1,4,64,512]{3,2,1,0:T(8,128)S(1)} collective-permute-done((f32[1,4,64,512]{3,2,1,0:T(8,128)}, f32[1,4,64,512]{3,2,1,0:T(8,128)S(1)}, u32[]{:S(2)}, u32[]{:S(2)}) %collective-permute-start.3) | collective-permute-done | bytes 524320 | tf_op jit(solution)/shard_map/ppermute | solution.py:19
  16.8 1.5 %collective-permute-start.7 = (f32[1,128,512]{2,1,0:T(8,128)S(1)}, f32[1,128,512]{2,1,0:T(8,128)S(1)}, u32[]{:S(2)}, u32[]{:S(2)}) collective-permute-start(f32[1,128,512]{2,1,0:T(8,128)S(1)} %shard_map.47), channel_id=1, source_target_pairs={{0,2},{1,3},{2,0},{3,1},{4,6},{5,7},{6,4},{7,5},{8,10},{9,11},{10,... | collective-permute-start | bytes 786440 | tf_op jit(solution)/shard_map/ppermute | solution.py:19
  18.3 1.4 %collective-permute-done.9.got = f32[16,16,512]{2,1,0:T(8,128)S(1)} collective-permute-done((f32[16,16,512]{2,1,0:T(8,128)S(1)}, f32[16,16,512]{2,1,0:T(8,128)S(1)}, u32[]{:S(2)}, u32[]{:S(2)}) %collective-permute-start.9) | collective-permute-done | bytes 524320 | tf_op jit(solution)/shard_map/ppermute | solution.py:25
  20.3 2.5 %collective-permute-start.15 = (f32[3,1,4,64,512]{4,3,2,1,0:T(8,128)S(1)}, f32[3,1,4,64,512]{4,3,2,1,0:T(8,128)S(1)}, u32[]{:S(2)}, u32[]{:S(2)}) collective-permute-start(f32[3,1,4,64,512]{4,3,2,1,0:T(8,128)S(1)} %shard_map.55), channel_id=1, source_target_pairs={{8,0},{16,8},{24,16},{9,1},{17,9},{25,17},{10,2},{18,10},{26,18},{... | collective-permute-start | bytes 4718600 | tf_op jit(solution)/shard_map/ppermute | solution.py:29
  23.7 1.5 %collective-permute-done.7.refs_0_.one = f32[1,128,512]{2,1,0:T(8,128)S(1)} collective-permute-done((f32[1,128,512]{2,1,0:T(8,128)S(1)}, f32[1,128,512]{2,1,0:T(8,128)S(1)}, u32[]{:S(2)}, u32[]{:S(2)}) %collective-permute-start.7) | collective-permute-done | bytes 262176 | tf_op jit(solution)/shard_map/ppermute | solution.py:19
  26.5 1.5 %collective-permute-done.10.refs_1_ = f32[1,128,512]{2,1,0:T(8,128)S(1)} collective-permute-done((f32[1,128,512]{2,1,0:T(8,128)S(1)}, f32[1,128,512]{2,1,0:T(8,128)S(1)}, u32[]{:S(2)}, u32[]{:S(2)}) %collective-permute-start.10) | collective-permute-done | bytes 262176 | tf_op jit(solution)/shard_map/ppermute | solution.py:19
  28.0 2.5 %shard_map.50 = (f32[16,16,512]{2,1,0:T(8,128)S(1)}, bf16[4,512,512]{2,1,0:T(8,128)(2,1)S(1)}, bf16[4,512,512]{2,1,0:T(8,128)(2,1)S(1)}, f32[4,4,9,128]{3,2,1,0:T(8,128)S(1)}) custom-call(s32[1]{0:T(128)} %bitcast.2.position, f32[16,16,512]{2,1,0:T(8,128)S(1)} %slice_bitcast_fusion.newest, ...), custom_call_target="tpu_custom_call", output_to_operand_aliasing={{1}: (3, {}), {2}: (4, {})} | custom-call | flops 1610612736 | bytes 5767168 | tf_op jit(solution)/shard_map/pallas_call | solution.py:52
  30.5 3.5 %collective-permute-start.12 = (f32[16,16,512]{2,1,0:T(8,128)S(1)}, f32[16,16,512]{2,1,0:T(8,128)S(1)}, u32[]{:S(2)}, u32[]{:S(2)}) collective-permute-start(f32[16,16,512]{2,1,0:T(8,128)S(1)} %get-tuple-element.47.past), channel_id=1, source_target_pairs={{0,8},{8,16},{16,24},{1,9},{9,17},{17,25},{2,10},{10,18},{18,26},{... | collective-permute-start | bytes 1572872 | tf_op jit(solution)/shard_map/ppermute | solution.py:25
  34.9 2.4 %collective-permute-start.16 = (f32[1,296,512]{2,1,0:T(8,128)S(1)}, f32[1,296,512]{2,1,0:T(8,128)S(1)}, u32[]{:S(2)}, u32[]{:S(2)}) collective-permute-start(f32[1,296,512]{2,1,0:T(8,128)S(1)} %shard_map.56), channel_id=1, source_target_pairs={{8,0},{16,8},{24,16},{9,1},{17,9},{25,17},{10,2},{18,10},{26,18},{... | collective-permute-start | bytes 1818632 | tf_op jit(solution)/shard_map/ppermute | solution.py:29
  37.3 9.1 %collective-permute-done.12.got = f32[16,16,512]{2,1,0:T(8,128)S(1)} collective-permute-done((f32[16,16,512]{2,1,0:T(8,128)S(1)}, f32[16,16,512]{2,1,0:T(8,128)S(1)}, u32[]{:S(2)}, u32[]{:S(2)}) %collective-permute-start.12) | collective-permute-done | bytes 524320 | tf_op jit(solution)/shard_map/ppermute | solution.py:25
  46.4 3.5 %collective-permute-start.14 = (f32[16,16,512]{2,1,0:T(8,128)S(1)}, f32[16,16,512]{2,1,0:T(8,128)S(1)}, u32[]{:S(2)}, u32[]{:S(2)}) collective-permute-start(f32[16,16,512]{2,1,0:T(8,128)S(1)} %collective-permute-done.12.got), channel_id=1, source_target_pairs={{8,16},{16,24},{9,17},{17,25},{10,18},{18,26},{11,19},{19,27},{12,... | collective-permute-start | bytes 1572872 | tf_op jit(solution)/shard_map/ppermute | solution.py:25
  49.8 2.3 %shard_map.52 = (f32[4,16,16,512]{3,2,1,0:T(8,128)}, f32[16,16,512]{2,1,0:T(8,128)S(1)}) custom-call(s32[1]{0:T(128)} %bitcast.section, f32[3,16,16,512]{3,2,1,0:T(8,128)S(1)} %bitcast.13, f32[16,16,512]{2,1,0:T(8,128)S(1)} %collective-permute-done.12.got, f32[16,16,512]{2,1,0:T(8,128)S(1)} %shard_map.51.early, ...), custom_call_target="tpu_custom_call" | custom-call | flops 2415919104 | bytes 7864320 | tf_op jit(solution)/shard_map/pallas_call | solution.py:52
  52.1 1.9 %collective-permute-start.13 = (f32[16,16,512]{2,1,0:T(8,128)S(1)}, f32[16,16,512]{2,1,0:T(8,128)S(1)}, u32[]{:S(2)}, u32[]{:S(2)}) collective-permute-start(f32[16,16,512]{2,1,0:T(8,128)S(1)} %get-tuple-element.51.past), channel_id=1, source_target_pairs={{0,8},{8,16},{16,24},{1,9},{9,17},{17,25},{2,10},{10,18},{18,26},{... | collective-permute-start | bytes 1572872 | tf_op jit(solution)/shard_map/ppermute | solution.py:25
  54.0 9.1 %collective-permute-done.14.got = f32[16,16,512]{2,1,0:T(8,128)S(1)} collective-permute-done((f32[16,16,512]{2,1,0:T(8,128)S(1)}, f32[16,16,512]{2,1,0:T(8,128)S(1)}, u32[]{:S(2)}, u32[]{:S(2)}) %collective-permute-start.14) | collective-permute-done | bytes 524320 | tf_op jit(solution)/shard_map/ppermute | solution.py:25
  64.0 6.6 %collective-permute-done.16.far = f32[1,296,512]{2,1,0:T(8,128)S(1)} collective-permute-done((f32[1,296,512]{2,1,0:T(8,128)S(1)}, f32[1,296,512]{2,1,0:T(8,128)S(1)}, u32[]{:S(2)}, u32[]{:S(2)}) %collective-permute-start.16) | collective-permute-done | bytes 606240 | tf_op jit(solution)/shard_map/ppermute | solution.py:29
  71.0 1.6 %collective-permute-done.13.got = f32[16,16,512]{2,1,0:T(8,128)S(1)} collective-permute-done((f32[16,16,512]{2,1,0:T(8,128)S(1)}, f32[16,16,512]{2,1,0:T(8,128)S(1)}, u32[]{:S(2)}, u32[]{:S(2)}) %collective-permute-start.13) | collective-permute-done | bytes 524320 | tf_op jit(solution)/shard_map/ppermute | solution.py:25
  72.6 2.3 %shard_map.54 = (f32[4,16,16,512]{3,2,1,0:T(8,128)}, f32[16,16,512]{2,1,0:T(8,128)S(1)}) custom-call(s32[1]{0:T(128)} %bitcast.section, f32[3,16,16,512]{3,2,1,0:T(8,128)S(1)} %bitcast.15, f32[16,16,512]{2,1,0:T(8,128)S(1)} %collective-permute-done.13.got, f32[16,16,512]{2,1,0:T(8,128)S(1)} %shard_map.53.early, ...), custom_call_target="tpu_custom_call", output_to_operand_aliasing={{0}: (8, {})} | custom-call | flops 14495514624 | bytes 39321600 | tf_op jit(solution)/shard_map/pallas_call | solution.py:52
  75.4 3.1 %shard_map.58 = (f32[4,16,16,512]{3,2,1,0:T(8,128)}, f32[16,16,512]{2,1,0:T(8,128)S(1)}) custom-call(s32[1]{0:T(128)} %bitcast.section, f32[3,16,16,512]{3,2,1,0:T(8,128)S(1)} %bitcast.16, f32[16,16,512]{2,1,0:T(8,128)S(1)} %collective-permute-done.13.got, f32[16,16,512]{2,1,0:T(8,128)S(1)} %get-tuple-element.54.newest, ...), custom_call_target="tpu_custom_call", output_to_operand_aliasing={{0}: (7, {})} | custom-call | flops 2818572288 | bytes 8912896 | tf_op jit(solution)/shard_map/pallas_call | solution.py:52
  78.5 3.4 %collective-permute-start.19 = (f32[16,16,512]{2,1,0:T(8,128)S(1)}, f32[16,16,512]{2,1,0:T(8,128)S(1)}, u32[]{:S(2)}, u32[]{:S(2)}) collective-permute-start(f32[16,16,512]{2,1,0:T(8,128)S(1)} %get-tuple-element.65), channel_id=1, source_target_pairs={{0,8},{8,16},{16,24},{1,9},{9,17},{17,25},{2,10},{10,18},{18,26},{... | collective-permute-start | bytes 1572872 | tf_op jit(solution)/shard_map/ppermute | solution.py:25
  81.9 2.8 %shard_map.59.own = f32[16,16,512]{2,1,0:T(8,128)S(1)} custom-call(f32[3,16,16,512]{3,2,1,0:T(8,128)S(1)} %bitcast.17, f32[4,4,9,128]{3,2,1,0:T(8,128)S(1)} %get-tuple-element.48.table, bf16[4,512,512]{2,1,0:T(8,128)(2,1)S(1)} %get-tuple-element.49.highs, bf16[4,512,512]{2,1,0:T(8,128)(2,1)S(1)} %get-tuple-element.50.lows), custom_call_target="tpu_custom_call" | custom-call | flops 1610612736 | bytes 5767168 | tf_op jit(solution)/shard_map/pallas_call | solution.py:52
  84.7 9.5 %collective-permute-done.19.got = f32[16,16,512]{2,1,0:T(8,128)S(1)} collective-permute-done((f32[16,16,512]{2,1,0:T(8,128)S(1)}, f32[16,16,512]{2,1,0:T(8,128)S(1)}, u32[]{:S(2)}, u32[]{:S(2)}) %collective-permute-start.19) | collective-permute-done | bytes 524320 | tf_op jit(solution)/shard_map/ppermute | solution.py:25
  (40 shorter events, 12.3 us)
Async XLA Ops:
  0.0 19.7 %copy-start.2 = (f32[1,4,64,512]{3,2,1,0:T(8,128)S(1)}, f32[1,4,64,512]{3,2,1,0:T(8,128)}, u32[]{:S(2)}) copy-start(f32[1,4,64,512]{3,2,1,0:T(8,128)} %refs_0_.2) | copy-start | bytes 1572868
  0.0 13.9 %collective-permute-start.3 = (f32[1,4,64,512]{3,2,1,0:T(8,128)}, f32[1,4,64,512]{3,2,1,0:T(8,128)S(1)}, u32[]{:S(2)}, u32[]{:S(2)}) collective-permute-start(f32[1,4,64,512]{3,2,1,0:T(8,128)} %refs_0_.2), channel_id=1, source_target_pairs={{0,4},{1,5},{2,6},{3,7},{4,0},{5,1},{6,2},{7,3},{8,12},{9,13},{10,... | collective-permute-start | bytes 1572872 | tf_op jit(solution)/shard_map/ppermute | solution.py:19
  1.5 13.9 %collective-permute-start.2 = (f32[1,4,64,512]{3,2,1,0:T(8,128)}, f32[1,4,64,512]{3,2,1,0:T(8,128)S(1)}, u32[]{:S(2)}, u32[]{:S(2)}) collective-permute-start(f32[1,4,64,512]{3,2,1,0:T(8,128)} %refs_0_.2), channel_id=1, source_target_pairs={{0,2},{1,3},{2,0},{3,1},{4,6},{5,7},{6,4},{7,5},{8,10},{9,11},{10,... | collective-permute-start | bytes 1572872 | tf_op jit(solution)/shard_map/ppermute | solution.py:19
  3.0 12.5 %collective-permute-start.1 = (f32[1,4,64,512]{3,2,1,0:T(8,128)}, f32[1,4,64,512]{3,2,1,0:T(8,128)S(1)}, u32[]{:S(2)}, u32[]{:S(2)}) collective-permute-start(f32[1,4,64,512]{3,2,1,0:T(8,128)} %refs_0_.2), channel_id=1, source_target_pairs={{0,1},{1,0},{2,3},{3,2},{4,5},{5,4},{6,7},{7,6},{8,9},{9,8},{10,11... | collective-permute-start | bytes 1572872 | tf_op jit(solution)/shard_map/ppermute | solution.py:19
  3.7 1.6 %collective-permute-start = (f32[4,9,64]{2,1,0:T(8,128)S(1)}, f32[4,9,64]{2,1,0:T(8,128)S(1)}, u32[]{:S(2)}, u32[]{:S(2)}) collective-permute-start(f32[4,9,64]{2,1,0:T(8,128)S(1)} %bitcast.20), channel_id=1, source_target_pairs={{0,1},{1,0},{2,3},{3,2},{4,5},{5,4},{6,7},{7,6},{8,9},{9,8},{10,11... | collective-permute-start | bytes 27656 | tf_op jit(solution)/shard_map/ppermute | solution.py:19
  5.4 10.4 %collective-permute-start.4 = (f32[4,9,128]{2,1,0:T(8,128)S(1)}, f32[4,9,128]{2,1,0:T(8,128)S(1)}, u32[]{:S(2)}, u32[]{:S(2)}) collective-permute-start(f32[4,9,128]{2,1,0:T(8,128)S(1)} %maximum_select_fusion.refs_0_.refs_4_), channel_id=1, source_target_pairs={{0,2},{1,3},{2,0},{3,1},{4,6},{5,7},{6,4},{7,5},{8,10},{9,11},{10,... | collective-permute-start | bytes 55304 | tf_op jit(solution)/shard_map/ppermute | solution.py:19
  6.0 13.7 %collective-permute-start.9 = (f32[16,16,512]{2,1,0:T(8,128)S(1)}, f32[16,16,512]{2,1,0:T(8,128)S(1)}, u32[]{:S(2)}, u32[]{:S(2)}) collective-permute-start(f32[16,16,512]{2,1,0:T(8,128)S(1)} %slice_bitcast_fusion.newest), channel_id=1, source_target_pairs={{0,8},{8,16},{16,24},{24,0},{1,9},{9,17},{17,25},{25,1},{2,10},{10... | collective-permute-start | bytes 1572872 | tf_op jit(solution)/shard_map/ppermute | solution.py:25
  14.2 5.5 %collective-permute-start.6 = (f32[1,4,64,512]{3,2,1,0:T(8,128)S(1)}, f32[1,4,64,512]{3,2,1,0:T(8,128)S(1)}, u32[]{:S(2)}, u32[]{:S(2)}) collective-permute-start(f32[1,4,64,512]{3,2,1,0:T(8,128)S(1)} %collective-permute-done.3.block.refs_3_.refs_2_), channel_id=1, source_target_pairs={{0,1},{1,0},{2,3},{3,2},{4,5},{5,4},{6,7},{7,6},{8,9},{9,8},{10,11... | collective-permute-start | bytes 1572872 | tf_op jit(solution)/shard_map/ppermute | solution.py:19
  16.2 3.5 %collective-permute-start.5 = (f32[1,4,64,512]{3,2,1,0:T(8,128)S(1)}, f32[1,4,64,512]{3,2,1,0:T(8,128)S(1)}, u32[]{:S(2)}, u32[]{:S(2)}) collective-permute-start(f32[1,4,64,512]{3,2,1,0:T(8,128)S(1)} %collective-permute-done.2.block.refs_2_.refs_1_), channel_id=1, source_target_pairs={{0,1},{1,0},{2,3},{3,2},{4,5},{5,4},{6,7},{7,6},{8,9},{9,8},{10,11... | collective-permute-start | bytes 1572872 | tf_op jit(solution)/shard_map/ppermute | solution.py:19
  16.2 9.8 %collective-permute-start.8 = (f32[1,152,512]{2,1,0:T(8,128)S(1)}, f32[1,152,512]{2,1,0:T(8,128)S(1)}, u32[]{:S(2)}, u32[]{:S(2)}) collective-permute-start(f32[1,152,512]{2,1,0:T(8,128)S(1)} %shard_map.46), channel_id=1, source_target_pairs={{0,4},{1,5},{2,6},{3,7},{4,0},{5,1},{6,2},{7,3},{8,12},{9,13},{10,... | collective-permute-start | bytes 933896 | tf_op jit(solution)/shard_map/ppermute | solution.py:19
  16.8 8.4 %collective-permute-start.7 = (f32[1,128,512]{2,1,0:T(8,128)S(1)}, f32[1,128,512]{2,1,0:T(8,128)S(1)}, u32[]{:S(2)}, u32[]{:S(2)}) collective-permute-start(f32[1,128,512]{2,1,0:T(8,128)S(1)} %shard_map.47), channel_id=1, source_target_pairs={{0,2},{1,3},{2,0},{3,1},{4,6},{5,7},{6,4},{7,5},{8,10},{9,11},{10,... | collective-permute-start | bytes 786440 | tf_op jit(solution)/shard_map/ppermute | solution.py:19
  20.1 2.7 %copy-start.1 = (f32[1,2,1,16,16,512]{5,4,3,2,1,0:T(8,128)S(1)}, f32[1,2,1,16,16,512]{5,4,3,2,1,0:T(8,128)}, u32[]{:S(2)}) copy-start(f32[1,2,1,16,16,512]{5,4,3,2,1,0:T(8,128)} %param.4) | copy-start | bytes 3145732
  20.3 50.3 %collective-permute-start.15 = (f32[3,1,4,64,512]{4,3,2,1,0:T(8,128)S(1)}, f32[3,1,4,64,512]{4,3,2,1,0:T(8,128)S(1)}, u32[]{:S(2)}, u32[]{:S(2)}) collective-permute-start(f32[3,1,4,64,512]{4,3,2,1,0:T(8,128)S(1)} %shard_map.55), channel_id=1, source_target_pairs={{8,0},{16,8},{24,16},{9,1},{17,9},{25,17},{10,2},{18,10},{26,18},{... | collective-permute-start | bytes 4718600 | tf_op jit(solution)/shard_map/ppermute | solution.py:29
  23.7 10.3 %copy-start = (f32[3,1,16,16,512]{4,3,2,1,0:T(8,128)S(1)}, f32[3,1,16,16,512]{4,3,2,1,0:T(8,128)}, u32[]{:S(2)}) copy-start(f32[3,1,16,16,512]{4,3,2,1,0:T(8,128)} %param.5) | copy-start | bytes 4718596
  26.0 2.0 %collective-permute-start.11 = (f32[1,152,512]{2,1,0:T(8,128)S(1)}, f32[1,152,512]{2,1,0:T(8,128)S(1)}, u32[]{:S(2)}, u32[]{:S(2)}) collective-permute-start(f32[1,152,512]{2,1,0:T(8,128)S(1)} %collective-permute-done.8.refs_2_.two), channel_id=1, source_target_pairs={{0,1},{1,0},{2,3},{3,2},{4,5},{5,4},{6,7},{7,6},{8,9},{9,8},{10,11... | collective-permute-start | bytes 933896 | tf_op jit(solution)/shard_map/ppermute | solution.py:19
  26.0 2.0 %collective-permute-start.10 = (f32[1,128,512]{2,1,0:T(8,128)S(1)}, f32[1,128,512]{2,1,0:T(8,128)S(1)}, u32[]{:S(2)}, u32[]{:S(2)}) collective-permute-start(f32[1,128,512]{2,1,0:T(8,128)S(1)} %collective-permute-done.7.refs_0_.one), channel_id=1, source_target_pairs={{0,1},{1,0},{2,3},{3,2},{4,5},{5,4},{6,7},{7,6},{8,9},{9,8},{10,11... | collective-permute-start | bytes 786440 | tf_op jit(solution)/shard_map/ppermute | solution.py:19
  30.5 15.9 %collective-permute-start.12 = (f32[16,16,512]{2,1,0:T(8,128)S(1)}, f32[16,16,512]{2,1,0:T(8,128)S(1)}, u32[]{:S(2)}, u32[]{:S(2)}) collective-permute-start(f32[16,16,512]{2,1,0:T(8,128)S(1)} %get-tuple-element.47.past), channel_id=1, source_target_pairs={{0,8},{8,16},{16,24},{1,9},{9,17},{17,25},{2,10},{10,18},{18,26},{... | collective-permute-start | bytes 1572872 | tf_op jit(solution)/shard_map/ppermute | solution.py:25
  34.9 35.6 %collective-permute-start.16 = (f32[1,296,512]{2,1,0:T(8,128)S(1)}, f32[1,296,512]{2,1,0:T(8,128)S(1)}, u32[]{:S(2)}, u32[]{:S(2)}) collective-permute-start(f32[1,296,512]{2,1,0:T(8,128)S(1)} %shard_map.56), channel_id=1, source_target_pairs={{8,0},{16,8},{24,16},{9,1},{17,9},{25,17},{10,2},{18,10},{26,18},{... | collective-permute-start | bytes 1818632 | tf_op jit(solution)/shard_map/ppermute | solution.py:29
  46.4 16.7 %collective-permute-start.14 = (f32[16,16,512]{2,1,0:T(8,128)S(1)}, f32[16,16,512]{2,1,0:T(8,128)S(1)}, u32[]{:S(2)}, u32[]{:S(2)}) collective-permute-start(f32[16,16,512]{2,1,0:T(8,128)S(1)} %collective-permute-done.12.got), channel_id=1, source_target_pairs={{8,16},{16,24},{9,17},{17,25},{10,18},{18,26},{11,19},{19,27},{12,... | collective-permute-start | bytes 1572872 | tf_op jit(solution)/shard_map/ppermute | solution.py:25
  52.1 20.5 %collective-permute-start.13 = (f32[16,16,512]{2,1,0:T(8,128)S(1)}, f32[16,16,512]{2,1,0:T(8,128)S(1)}, u32[]{:S(2)}, u32[]{:S(2)}) collective-permute-start(f32[16,16,512]{2,1,0:T(8,128)S(1)} %get-tuple-element.51.past), channel_id=1, source_target_pairs={{0,8},{8,16},{16,24},{1,9},{9,17},{17,25},{2,10},{10,18},{18,26},{... | collective-permute-start | bytes 1572872 | tf_op jit(solution)/shard_map/ppermute | solution.py:25
  70.5 4.4 %collective-permute-start.17 = (f32[3,1,4,64,512]{4,3,2,1,0:T(8,128)S(1)}, f32[3,1,4,64,512]{4,3,2,1,0:T(8,128)S(1)}, u32[]{:S(2)}, u32[]{:S(2)}) collective-permute-start(f32[3,1,4,64,512]{4,3,2,1,0:T(8,128)S(1)} %collective-permute-done.15.near), channel_id=1, source_target_pairs={{0,1},{1,0},{2,3},{3,2},{4,5},{5,4},{6,7},{7,6},{8,9},{9,8},{10,11... | collective-permute-start | bytes 4718600 | tf_op jit(solution)/shard_map/ppermute | solution.py:19
  70.5 4.4 %collective-permute-start.18 = (f32[1,296,512]{2,1,0:T(8,128)S(1)}, f32[1,296,512]{2,1,0:T(8,128)S(1)}, u32[]{:S(2)}, u32[]{:S(2)}) collective-permute-start(f32[1,296,512]{2,1,0:T(8,128)S(1)} %collective-permute-done.16.far), channel_id=1, source_target_pairs={{0,1},{1,0},{2,3},{3,2},{4,5},{5,4},{6,7},{7,6},{8,9},{9,8},{10,11... | collective-permute-start | bytes 1818632 | tf_op jit(solution)/shard_map/ppermute | solution.py:19
  78.5 15.7 %collective-permute-start.19 = (f32[16,16,512]{2,1,0:T(8,128)S(1)}, f32[16,16,512]{2,1,0:T(8,128)S(1)}, u32[]{:S(2)}, u32[]{:S(2)}) collective-permute-start(f32[16,16,512]{2,1,0:T(8,128)S(1)} %get-tuple-element.65), channel_id=1, source_target_pairs={{0,8},{8,16},{16,24},{1,9},{9,17},{17,25},{2,10},{10,18},{18,26},{... | collective-permute-start | bytes 1572872 | tf_op jit(solution)/shard_map/ppermute | solution.py:25

commit v7 on v5

--- a/solution.py
+++ b/solution.py
@@ -92,13 +92,15 @@
     return shifted(by_column[0], 1) + by_column[1] + shifted(by_column[2], -1)
 
 
-def separable(source, table, highs, lows, branch, blocks=None):
+def separable(source, table, highs, lows, branch, blocks=None, loads=()):
     rows, columns, channels = source.shape
     width = min(LANES, channels)
     depth = min(DEPTH, channels)
     each = depth // width
     total = None
     for block in range(channels // depth) if blocks is None else blocks:
+        if loads:
+            loads[block].wait()
         mixed_in = []
         for i in range(each):
             value = depthwise(source, table, branch, block * each + i, width)
@@ -118,18 +120,18 @@
     return total.reshape(source.shape)
 
 
-def fetch(tick, at, section, stems, got, held, sem):
+def fetch(tick, at, section, stems, got, held, sem, lanes=slice(None)):
     for s in range(at):
 
         @pl.when(section == s)
         def _(s=s):
-            begin(stems.at[tick - 1 - s], held, sem)
+            begin(stems.at[tick - 1 - s, :, :, lanes], held.at[:, :, lanes], sem)
 
     @pl.when(section >= at)
     def _():
-        begin(got, held, sem)
-
-    return pltpu.make_async_copy(got, held, sem)
+        begin(got.at[:, :, lanes], held.at[:, :, lanes], sem)
+
+    return pltpu.make_async_copy(got.at[:, :, lanes], held.at[:, :, lanes], sem)
 
 
 def early_kernel(tick, at, section, stems, got, table, highs, lows, out, held, sem):
@@ -139,9 +141,14 @@
 
 def late_kernel(tick, at, section, stems, got, early, table, highs, lows, past, *rest):
     emitted, out, newest, first, second, sem = rest[-6:]
-    store = begin(past, emitted.at[tick - 1], sem.at[1])
-    fetch(tick, at, section[0], stems, got, newest, sem.at[0]).wait()
-    first[...] = separable(newest, table, highs, lows, 0) + early[...]
+    store = begin(past, emitted.at[tick - 1], sem.at[sem.shape[0] - 1])
+    channels = newest.shape[-1]
+    depth = min(DEPTH, channels)
+    loads = [
+        fetch(tick, at, section[0], stems, got, newest, sem.at[i], pl.ds(i * depth, depth))
+        for i in range(channels // depth)
+    ]
+    first[...] = separable(newest, table, highs, lows, 0, loads=loads) + early[...]
     second[...] = separable(first, table, highs, lows, 2) + newest[...]
     out[...] = separable(second, table, highs, lows, 3) + first[...]
     store.wait()
@@ -169,7 +176,7 @@
         (whole, jax.ShapeDtypeStruct(shape, F32)),
         operands if emitted is None else operands + (emitted,),
         [(shape, F32)] * 3,
-        2,
+        1 + shape[-1] // min(DEPTH, shape[-1]),
         cost(shape, 3 * weight),
         apart=(1, 2, 8),
         outs_apart=(0,),

time: 96.1 us -> 96.1 us (level)
  transfers between devices with their start and end apart: 20 -> 20, of which waited for: 12 -> 12; matrix products, arithmetic and copies ran while one was open for 2% -> 2% of each run, Pallas kernels for 14% -> 15%
where the time goes in v7:
time: 96.1 us; the launch traced here: 95.2 us
  waiting for transfers between devices  48.6 us (51%)
  starting transfers between devices  26.1 us (27%)
  Pallas kernels  18.2 us (19%)
  local copies, waits for them, and re-layouts  1.82 us (2%)
    ppermute x5, waiting for transfers between devices, from_behind(): lax.ppermute(x, axis, pairs + [(size - 1, 0)] * (around and size > 1))  30.4 us
    pallas_call x15, Pallas kernels, call(): pl.pallas_call(kernel, out_shape=outs, in_specs=[spec(x, i, apart) for i,...  18.2 us
    ppermute x5, starting transfers between devices, from_behind(): lax.ppermute(x, axis, pairs + [(size - 1, 0)] * (around and size > 1))  13.9 us
    ppermute x13, waiting for transfers between devices, swap(): return lax.ppermute(x, axis, [(i, i ^ bit) for i in range(size)])  11.9 us
    ppermute x13, starting transfers between devices, swap(): return lax.ppermute(x, axis, [(i, i ^ bit) for i in range(size)])  7.35 us
    ppermute x2, waiting for transfers between devices, from_ahead(): lax.ppermute(x, axis, [(i + 1, i) for i in range(lax.axis_size(axis) - 1)])  6.21 us
    ppermute x2, starting transfers between devices, from_ahead(): lax.ppermute(x, axis, [(i + 1, i) for i in range(lax.axis_size(axis) - 1)])  4.82 us
  transfers between devices with their start and end apart: 20, of which 12 were waited for; matrix products, arithmetic and copies ran while one was open for 2% of the time, Pallas kernels for 15%

profile of v7, /device:TPU:16, one launch (start us, length us, event | category | flops | bytes accessed | tf_op | source)
XLA Modules:
  0.0 95.2 jit_solution(15176396861119686589)
XLA Ops:
  0.0 1.5 %collective-permute-start.3 = (f32[1,4,64,512]{3,2,1,0:T(8,128)}, f32[1,4,64,512]{3,2,1,0:T(8,128)S(1)}, u32[]{:S(2)}, u32[]{:S(2)}) collective-permute-start(f32[1,4,64,512]{3,2,1,0:T(8,128)} %refs_0_.2), channel_id=1, source_target_pairs={{0,4},{1,5},{2,6},{3,7},{4,0},{5,1},{6,2},{7,3},{8,12},{9,13},{10,... | collective-permute-start | bytes 1572872 | tf_op jit(solution)/shard_map/ppermute | solution.py:20
  1.5 1.5 %collective-permute-start.2 = (f32[1,4,64,512]{3,2,1,0:T(8,128)}, f32[1,4,64,512]{3,2,1,0:T(8,128)S(1)}, u32[]{:S(2)}, u32[]{:S(2)}) collective-permute-start(f32[1,4,64,512]{3,2,1,0:T(8,128)} %refs_0_.2), channel_id=1, source_target_pairs={{0,2},{1,3},{2,0},{3,1},{4,6},{5,7},{6,4},{7,5},{8,10},{9,11},{10,... | collective-permute-start | bytes 1572872 | tf_op jit(solution)/shard_map/ppermute | solution.py:20
  6.0 1.6 %collective-permute-start.9 = (f32[16,16,512]{2,1,0:T(8,128)S(1)}, f32[16,16,512]{2,1,0:T(8,128)S(1)}, u32[]{:S(2)}, u32[]{:S(2)}) collective-permute-start(f32[16,16,512]{2,1,0:T(8,128)S(1)} %slice_bitcast_fusion.newest), channel_id=1, source_target_pairs={{0,8},{8,16},{16,24},{24,0},{1,9},{9,17},{17,25},{25,1},{2,10},{10... | collective-permute-start | bytes 1572872 | tf_op jit(solution)/shard_map/ppermute | solution.py:26
  7.6 6.3 %collective-permute-done.3.block.refs_3_.refs_2_ = f32[1,4,64,512]{3,2,1,0:T(8,128)S(1)} collective-permute-done((f32[1,4,64,512]{3,2,1,0:T(8,128)}, f32[1,4,64,512]{3,2,1,0:T(8,128)S(1)}, u32[]{:S(2)}, u32[]{:S(2)}) %collective-permute-start.3) | collective-permute-done | bytes 524320 | tf_op jit(solution)/shard_map/ppermute | solution.py:20
  16.8 1.5 %collective-permute-start.7 = (f32[1,128,512]{2,1,0:T(8,128)S(1)}, f32[1,128,512]{2,1,0:T(8,128)S(1)}, u32[]{:S(2)}, u32[]{:S(2)}) collective-permute-start(f32[1,128,512]{2,1,0:T(8,128)S(1)} %shard_map.47), channel_id=1, source_target_pairs={{0,2},{1,3},{2,0},{3,1},{4,6},{5,7},{6,4},{7,5},{8,10},{9,11},{10,... | collective-permute-start | bytes 786440 | tf_op jit(solution)/shard_map/ppermute | solution.py:20
  18.3 1.4 %collective-permute-done.9.got = f32[16,16,512]{2,1,0:T(8,128)S(1)} collective-permute-done((f32[16,16,512]{2,1,0:T(8,128)S(1)}, f32[16,16,512]{2,1,0:T(8,128)S(1)}, u32[]{:S(2)}, u32[]{:S(2)}) %collective-permute-start.9) | collective-permute-done | bytes 524320 | tf_op jit(solution)/shard_map/ppermute | solution.py:26
  20.3 2.5 %collective-permute-start.15 = (f32[3,1,4,64,512]{4,3,2,1,0:T(8,128)S(1)}, f32[3,1,4,64,512]{4,3,2,1,0:T(8,128)S(1)}, u32[]{:S(2)}, u32[]{:S(2)}) collective-permute-start(f32[3,1,4,64,512]{4,3,2,1,0:T(8,128)S(1)} %shard_map.55), channel_id=1, source_target_pairs={{8,0},{16,8},{24,16},{9,1},{17,9},{25,17},{10,2},{18,10},{26,18},{... | collective-permute-start | bytes 4718600 | tf_op jit(solution)/shard_map/ppermute | solution.py:30
  23.7 1.5 %collective-permute-done.7.refs_0_.one = f32[1,128,512]{2,1,0:T(8,128)S(1)} collective-permute-done((f32[1,128,512]{2,1,0:T(8,128)S(1)}, f32[1,128,512]{2,1,0:T(8,128)S(1)}, u32[]{:S(2)}, u32[]{:S(2)}) %collective-permute-start.7) | collective-permute-done | bytes 262176 | tf_op jit(solution)/shard_map/ppermute | solution.py:20
  26.9 1.5 %collective-permute-done.10.refs_1_ = f32[1,128,512]{2,1,0:T(8,128)S(1)} collective-permute-done((f32[1,128,512]{2,1,0:T(8,128)S(1)}, f32[1,128,512]{2,1,0:T(8,128)S(1)}, u32[]{:S(2)}, u32[]{:S(2)}) %collective-permute-start.10) | collective-permute-done | bytes 262176 | tf_op jit(solution)/shard_map/ppermute | solution.py:20
  28.4 2.5 %shard_map.50 = (f32[16,16,512]{2,1,0:T(8,128)S(1)}, bf16[4,512,512]{2,1,0:T(8,128)(2,1)S(1)}, bf16[4,512,512]{2,1,0:T(8,128)(2,1)S(1)}, f32[4,4,9,128]{3,2,1,0:T(8,128)S(1)}) custom-call(s32[1]{0:T(128)} %bitcast.2.position, f32[16,16,512]{2,1,0:T(8,128)S(1)} %slice_bitcast_fusion.newest, ...), custom_call_target="tpu_custom_call", output_to_operand_aliasing={{1}: (3, {}), {2}: (4, {})} | custom-call | flops 1610612736 | bytes 5767168 | tf_op jit(solution)/shard_map/pallas_call | solution.py:53
  30.9 3.5 %collective-permute-start.12 = (f32[16,16,512]{2,1,0:T(8,128)S(1)}, f32[16,16,512]{2,1,0:T(8,128)S(1)}, u32[]{:S(2)}, u32[]{:S(2)}) collective-permute-start(f32[16,16,512]{2,1,0:T(8,128)S(1)} %get-tuple-element.47.past), channel_id=1, source_target_pairs={{0,8},{8,16},{16,24},{1,9},{9,17},{17,25},{2,10},{10,18},{18,26},{... | collective-permute-start | bytes 1572872 | tf_op jit(solution)/shard_map/ppermute | solution.py:26
  35.3 2.3 %collective-permute-start.16 = (f32[1,296,512]{2,1,0:T(8,128)S(1)}, f32[1,296,512]{2,1,0:T(8,128)S(1)}, u32[]{:S(2)}, u32[]{:S(2)}) collective-permute-start(f32[1,296,512]{2,1,0:T(8,128)S(1)} %shard_map.56), channel_id=1, source_target_pairs={{8,0},{16,8},{24,16},{9,1},{17,9},{25,17},{10,2},{18,10},{26,18},{... | collective-permute-start | bytes 1818632 | tf_op jit(solution)/shard_map/ppermute | solution.py:30
  37.7 9.1 %collective-permute-done.12.got = f32[16,16,512]{2,1,0:T(8,128)S(1)} collective-permute-done((f32[16,16,512]{2,1,0:T(8,128)S(1)}, f32[16,16,512]{2,1,0:T(8,128)S(1)}, u32[]{:S(2)}, u32[]{:S(2)}) %collective-permute-start.12) | collective-permute-done | bytes 524320 | tf_op jit(solution)/shard_map/ppermute | solution.py:26
  46.7 3.5 %collective-permute-start.14 = (f32[16,16,512]{2,1,0:T(8,128)S(1)}, f32[16,16,512]{2,1,0:T(8,128)S(1)}, u32[]{:S(2)}, u32[]{:S(2)}) collective-permute-start(f32[16,16,512]{2,1,0:T(8,128)S(1)} %collective-permute-done.12.got), channel_id=1, source_target_pairs={{8,16},{16,24},{9,17},{17,25},{10,18},{18,26},{11,19},{19,27},{12,... | collective-permute-start | bytes 1572872 | tf_op jit(solution)/shard_map/ppermute | solution.py:26
  50.2 2.4 %shard_map.52 = (f32[4,16,16,512]{3,2,1,0:T(8,128)}, f32[16,16,512]{2,1,0:T(8,128)S(1)}) custom-call(s32[1]{0:T(128)} %bitcast.section, f32[3,16,16,512]{3,2,1,0:T(8,128)S(1)} %bitcast.13, f32[16,16,512]{2,1,0:T(8,128)S(1)} %collective-permute-done.12.got, f32[16,16,512]{2,1,0:T(8,128)S(1)} %shard_map.51.early, ...), custom_call_target="tpu_custom_call" | custom-call | flops 2415919104 | bytes 7864320 | tf_op jit(solution)/shard_map/pallas_call | solution.py:53
  52.6 1.9 %collective-permute-start.13 = (f32[16,16,512]{2,1,0:T(8,128)S(1)}, f32[16,16,512]{2,1,0:T(8,128)S(1)}, u32[]{:S(2)}, u32[]{:S(2)}) collective-permute-start(f32[16,16,512]{2,1,0:T(8,128)S(1)} %get-tuple-element.51.past), channel_id=1, source_target_pairs={{0,8},{8,16},{16,24},{1,9},{9,17},{17,25},{2,10},{10,18},{18,26},{... | collective-permute-start | bytes 1572872 | tf_op jit(solution)/shard_map/ppermute | solution.py:26
  54.5 9.0 %collective-permute-done.14.got = f32[16,16,512]{2,1,0:T(8,128)S(1)} collective-permute-done((f32[16,16,512]{2,1,0:T(8,128)S(1)}, f32[16,16,512]{2,1,0:T(8,128)S(1)}, u32[]{:S(2)}, u32[]{:S(2)}) %collective-permute-start.14) | collective-permute-done | bytes 524320 | tf_op jit(solution)/shard_map/ppermute | solution.py:26
  64.3 6.2 %collective-permute-done.16.far = f32[1,296,512]{2,1,0:T(8,128)S(1)} collective-permute-done((f32[1,296,512]{2,1,0:T(8,128)S(1)}, f32[1,296,512]{2,1,0:T(8,128)S(1)}, u32[]{:S(2)}, u32[]{:S(2)}) %collective-permute-start.16) | collective-permute-done | bytes 606240 | tf_op jit(solution)/shard_map/ppermute | solution.py:30
  71.0 2.0 %collective-permute-done.13.got = f32[16,16,512]{2,1,0:T(8,128)S(1)} collective-permute-done((f32[16,16,512]{2,1,0:T(8,128)S(1)}, f32[16,16,512]{2,1,0:T(8,128)S(1)}, u32[]{:S(2)}, u32[]{:S(2)}) %collective-permute-start.13) | collective-permute-done | bytes 524320 | tf_op jit(solution)/shard_map/ppermute | solution.py:26
  73.0 2.3 %shard_map.54 = (f32[4,16,16,512]{3,2,1,0:T(8,128)}, f32[16,16,512]{2,1,0:T(8,128)S(1)}) custom-call(s32[1]{0:T(128)} %bitcast.section, f32[3,16,16,512]{3,2,1,0:T(8,128)S(1)} %bitcast.15, f32[16,16,512]{2,1,0:T(8,128)S(1)} %collective-permute-done.13.got, f32[16,16,512]{2,1,0:T(8,128)S(1)} %shard_map.53.early, ...), custom_call_target="tpu_custom_call", output_to_operand_aliasing={{0}: (8, {})} | custom-call | flops 14495514624 | bytes 39321600 | tf_op jit(solution)/shard_map/pallas_call | solution.py:53
  75.9 3.0 %shard_map.58 = (f32[4,16,16,512]{3,2,1,0:T(8,128)}, f32[16,16,512]{2,1,0:T(8,128)S(1)}) custom-call(s32[1]{0:T(128)} %bitcast.section, f32[3,16,16,512]{3,2,1,0:T(8,128)S(1)} %bitcast.16, f32[16,16,512]{2,1,0:T(8,128)S(1)} %collective-permute-done.13.got, f32[16,16,512]{2,1,0:T(8,128)S(1)} %get-tuple-element.54.newest, ...), custom_call_target="tpu_custom_call", output_to_operand_aliasing={{0}: (7, {})} | custom-call | flops 2818572288 | bytes 8912896 | tf_op jit(solution)/shard_map/pallas_call | solution.py:53
  78.9 3.5 %collective-permute-start.19 = (f32[16,16,512]{2,1,0:T(8,128)S(1)}, f32[16,16,512]{2,1,0:T(8,128)S(1)}, u32[]{:S(2)}, u32[]{:S(2)}) collective-permute-start(f32[16,16,512]{2,1,0:T(8,128)S(1)} %get-tuple-element.65), channel_id=1, source_target_pairs={{0,8},{8,16},{16,24},{1,9},{9,17},{17,25},{2,10},{10,18},{18,26},{... | collective-permute-start | bytes 1572872 | tf_op jit(solution)/shard_map/ppermute | solution.py:26
  82.4 2.8 %shard_map.59.own = f32[16,16,512]{2,1,0:T(8,128)S(1)} custom-call(f32[3,16,16,512]{3,2,1,0:T(8,128)S(1)} %bitcast.17, f32[4,4,9,128]{3,2,1,0:T(8,128)S(1)} %get-tuple-element.48.table, bf16[4,512,512]{2,1,0:T(8,128)(2,1)S(1)} %get-tuple-element.49.highs, bf16[4,512,512]{2,1,0:T(8,128)(2,1)S(1)} %get-tuple-element.50.lows), custom_call_target="tpu_custom_call" | custom-call | flops 1610612736 | bytes 5767168 | tf_op jit(solution)/shard_map/pallas_call | solution.py:53
  85.2 9.0 %collective-permute-done.19.got = f32[16,16,512]{2,1,0:T(8,128)S(1)} collective-permute-done((f32[16,16,512]{2,1,0:T(8,128)S(1)}, f32[16,16,512]{2,1,0:T(8,128)S(1)}, u32[]{:S(2)}, u32[]{:S(2)}) %collective-permute-start.19) | collective-permute-done | bytes 524320 | tf_op jit(solution)/shard_map/ppermute | solution.py:26
  (40 shorter events, 12.6 us)
Async XLA Ops:
  0.0 19.7 %copy-start.2 = (f32[1,4,64,512]{3,2,1,0:T(8,128)S(1)}, f32[1,4,64,512]{3,2,1,0:T(8,128)}, u32[]{:S(2)}) copy-start(f32[1,4,64,512]{3,2,1,0:T(8,128)} %refs_0_.2) | copy-start | bytes 1572868
  0.0 13.9 %collective-permute-start.3 = (f32[1,4,64,512]{3,2,1,0:T(8,128)}, f32[1,4,64,512]{3,2,1,0:T(8,128)S(1)}, u32[]{:S(2)}, u32[]{:S(2)}) collective-permute-start(f32[1,4,64,512]{3,2,1,0:T(8,128)} %refs_0_.2), channel_id=1, source_target_pairs={{0,4},{1,5},{2,6},{3,7},{4,0},{5,1},{6,2},{7,3},{8,12},{9,13},{10,... | collective-permute-start | bytes 1572872 | tf_op jit(solution)/shard_map/ppermute | solution.py:20
  1.5 13.9 %collective-permute-start.2 = (f32[1,4,64,512]{3,2,1,0:T(8,128)}, f32[1,4,64,512]{3,2,1,0:T(8,128)S(1)}, u32[]{:S(2)}, u32[]{:S(2)}) collective-permute-start(f32[1,4,64,512]{3,2,1,0:T(8,128)} %refs_0_.2), channel_id=1, source_target_pairs={{0,2},{1,3},{2,0},{3,1},{4,6},{5,7},{6,4},{7,5},{8,10},{9,11},{10,... | collective-permute-start | bytes 1572872 | tf_op jit(solution)/shard_map/ppermute | solution.py:20
  3.0 12.5 %collective-permute-start.1 = (f32[1,4,64,512]{3,2,1,0:T(8,128)}, f32[1,4,64,512]{3,2,1,0:T(8,128)S(1)}, u32[]{:S(2)}, u32[]{:S(2)}) collective-permute-start(f32[1,4,64,512]{3,2,1,0:T(8,128)} %refs_0_.2), channel_id=1, source_target_pairs={{0,1},{1,0},{2,3},{3,2},{4,5},{5,4},{6,7},{7,6},{8,9},{9,8},{10,11... | collective-permute-start | bytes 1572872 | tf_op jit(solution)/shard_map/ppermute | solution.py:20
  3.7 1.6 %collective-permute-start = (f32[4,9,64]{2,1,0:T(8,128)S(1)}, f32[4,9,64]{2,1,0:T(8,128)S(1)}, u32[]{:S(2)}, u32[]{:S(2)}) collective-permute-start(f32[4,9,64]{2,1,0:T(8,128)S(1)} %bitcast.20), channel_id=1, source_target_pairs={{0,1},{1,0},{2,3},{3,2},{4,5},{5,4},{6,7},{7,6},{8,9},{9,8},{10,11... | collective-permute-start | bytes 27656 | tf_op jit(solution)/shard_map/ppermute | solution.py:20
  5.4 10.4 %collective-permute-start.4 = (f32[4,9,128]{2,1,0:T(8,128)S(1)}, f32[4,9,128]{2,1,0:T(8,128)S(1)}, u32[]{:S(2)}, u32[]{:S(2)}) collective-permute-start(f32[4,9,128]{2,1,0:T(8,128)S(1)} %maximum_select_fusion.refs_0_.refs_4_), channel_id=1, source_target_pairs={{0,2},{1,3},{2,0},{3,1},{4,6},{5,7},{6,4},{7,5},{8,10},{9,11},{10,... | collective-permute-start | bytes 55304 | tf_op jit(solution)/shard_map/ppermute | solution.py:20
  6.0 13.7 %collective-permute-start.9 = (f32[16,16,512]{2,1,0:T(8,128)S(1)}, f32[16,16,512]{2,1,0:T(8,128)S(1)}, u32[]{:S(2)}, u32[]{:S(2)}) collective-permute-start(f32[16,16,512]{2,1,0:T(8,128)S(1)} %slice_bitcast_fusion.newest), channel_id=1, source_target_pairs={{0,8},{8,16},{16,24},{24,0},{1,9},{9,17},{17,25},{25,1},{2,10},{10... | collective-permute-start | bytes 1572872 | tf_op jit(solution)/shard_map/ppermute | solution.py:26
  14.2 5.5 %collective-permute-start.6 = (f32[1,4,64,512]{3,2,1,0:T(8,128)S(1)}, f32[1,4,64,512]{3,2,1,0:T(8,128)S(1)}, u32[]{:S(2)}, u32[]{:S(2)}) collective-permute-start(f32[1,4,64,512]{3,2,1,0:T(8,128)S(1)} %collective-permute-done.3.block.refs_3_.refs_2_), channel_id=1, source_target_pairs={{0,1},{1,0},{2,3},{3,2},{4,5},{5,4},{6,7},{7,6},{8,9},{9,8},{10,11... | collective-permute-start | bytes 1572872 | tf_op jit(solution)/shard_map/ppermute | solution.py:20
  16.2 3.5 %collective-permute-start.5 = (f32[1,4,64,512]{3,2,1,0:T(8,128)S(1)}, f32[1,4,64,512]{3,2,1,0:T(8,128)S(1)}, u32[]{:S(2)}, u32[]{:S(2)}) collective-permute-start(f32[1,4,64,512]{3,2,1,0:T(8,128)S(1)} %collective-permute-done.2.block.refs_2_.refs_1_), channel_id=1, source_target_pairs={{0,1},{1,0},{2,3},{3,2},{4,5},{5,4},{6,7},{7,6},{8,9},{9,8},{10,11... | collective-permute-start | bytes 1572872 | tf_op jit(solution)/shard_map/ppermute | solution.py:20
  16.2 10.1 %collective-permute-start.8 = (f32[1,160,512]{2,1,0:T(8,128)S(1)}, f32[1,160,512]{2,1,0:T(8,128)S(1)}, u32[]{:S(2)}, u32[]{:S(2)}) collective-permute-start(f32[1,160,512]{2,1,0:T(8,128)S(1)} %shard_map.46), channel_id=1, source_target_pairs={{0,4},{1,5},{2,6},{3,7},{4,0},{5,1},{6,2},{7,3},{8,12},{9,13},{10,... | collective-permute-start | bytes 983048 | tf_op jit(solution)/shard_map/ppermute | solution.py:20
  16.8 8.4 %collective-permute-start.7 = (f32[1,128,512]{2,1,0:T(8,128)S(1)}, f32[1,128,512]{2,1,0:T(8,128)S(1)}, u32[]{:S(2)}, u32[]{:S(2)}) collective-permute-start(f32[1,128,512]{2,1,0:T(8,128)S(1)} %shard_map.47), channel_id=1, source_target_pairs={{0,2},{1,3},{2,0},{3,1},{4,6},{5,7},{6,4},{7,5},{8,10},{9,11},{10,... | collective-permute-start | bytes 786440 | tf_op jit(solution)/shard_map/ppermute | solution.py:20
  20.1 2.7 %copy-start.1 = (f32[1,2,1,16,16,512]{5,4,3,2,1,0:T(8,128)S(1)}, f32[1,2,1,16,16,512]{5,4,3,2,1,0:T(8,128)}, u32[]{:S(2)}) copy-start(f32[1,2,1,16,16,512]{5,4,3,2,1,0:T(8,128)} %param.4) | copy-start | bytes 3145732
  20.3 50.3 %collective-permute-start.15 = (f32[3,1,4,64,512]{4,3,2,1,0:T(8,128)S(1)}, f32[3,1,4,64,512]{4,3,2,1,0:T(8,128)S(1)}, u32[]{:S(2)}, u32[]{:S(2)}) collective-permute-start(f32[3,1,4,64,512]{4,3,2,1,0:T(8,128)S(1)} %shard_map.55), channel_id=1, source_target_pairs={{8,0},{16,8},{24,16},{9,1},{17,9},{25,17},{10,2},{18,10},{26,18},{... | collective-permute-start | bytes 4718600 | tf_op jit(solution)/shard_map/ppermute | solution.py:30
  23.7 10.7 %copy-start = (f32[3,1,16,16,512]{4,3,2,1,0:T(8,128)S(1)}, f32[3,1,16,16,512]{4,3,2,1,0:T(8,128)}, u32[]{:S(2)}) copy-start(f32[3,1,16,16,512]{4,3,2,1,0:T(8,128)} %param.5) | copy-start | bytes 4718596
  26.4 2.0 %collective-permute-start.11 = (f32[1,160,512]{2,1,0:T(8,128)S(1)}, f32[1,160,512]{2,1,0:T(8,128)S(1)}, u32[]{:S(2)}, u32[]{:S(2)}) collective-permute-start(f32[1,160,512]{2,1,0:T(8,128)S(1)} %collective-permute-done.8.refs_2_.two), channel_id=1, source_target_pairs={{0,1},{1,0},{2,3},{3,2},{4,5},{5,4},{6,7},{7,6},{8,9},{9,8},{10,11... | collective-permute-start | bytes 983048 | tf_op jit(solution)/shard_map/ppermute | solution.py:20
  26.4 2.0 %collective-permute-start.10 = (f32[1,128,512]{2,1,0:T(8,128)S(1)}, f32[1,128,512]{2,1,0:T(8,128)S(1)}, u32[]{:S(2)}, u32[]{:S(2)}) collective-permute-start(f32[1,128,512]{2,1,0:T(8,128)S(1)} %collective-permute-done.7.refs_0_.one), channel_id=1, source_target_pairs={{0,1},{1,0},{2,3},{3,2},{4,5},{5,4},{6,7},{7,6},{8,9},{9,8},{10,11... | collective-permute-start | bytes 786440 | tf_op jit(solution)/shard_map/ppermute | solution.py:20
  30.9 15.9 %collective-permute-start.12 = (f32[16,16,512]{2,1,0:T(8,128)S(1)}, f32[16,16,512]{2,1,0:T(8,128)S(1)}, u32[]{:S(2)}, u32[]{:S(2)}) collective-permute-start(f32[16,16,512]{2,1,0:T(8,128)S(1)} %get-tuple-element.47.past), channel_id=1, source_target_pairs={{0,8},{8,16},{16,24},{1,9},{9,17},{17,25},{2,10},{10,18},{18,26},{... | collective-permute-start | bytes 1572872 | tf_op jit(solution)/shard_map/ppermute | solution.py:26
  35.3 35.2 %collective-permute-start.16 = (f32[1,296,512]{2,1,0:T(8,128)S(1)}, f32[1,296,512]{2,1,0:T(8,128)S(1)}, u32[]{:S(2)}, u32[]{:S(2)}) collective-permute-start(f32[1,296,512]{2,1,0:T(8,128)S(1)} %shard_map.56), channel_id=1, source_target_pairs={{8,0},{16,8},{24,16},{9,1},{17,9},{25,17},{10,2},{18,10},{26,18},{... | collective-permute-start | bytes 1818632 | tf_op jit(solution)/shard_map/ppermute | solution.py:30
  46.7 16.7 %collective-permute-start.14 = (f32[16,16,512]{2,1,0:T(8,128)S(1)}, f32[16,16,512]{2,1,0:T(8,128)S(1)}, u32[]{:S(2)}, u32[]{:S(2)}) collective-permute-start(f32[16,16,512]{2,1,0:T(8,128)S(1)} %collective-permute-done.12.got), channel_id=1, source_target_pairs={{8,16},{16,24},{9,17},{17,25},{10,18},{18,26},{11,19},{19,27},{12,... | collective-permute-start | bytes 1572872 | tf_op jit(solution)/shard_map/ppermute | solution.py:26
  52.6 20.4 %collective-permute-start.13 = (f32[16,16,512]{2,1,0:T(8,128)S(1)}, f32[16,16,512]{2,1,0:T(8,128)S(1)}, u32[]{:S(2)}, u32[]{:S(2)}) collective-permute-start(f32[16,16,512]{2,1,0:T(8,128)S(1)} %get-tuple-element.51.past), channel_id=1, source_target_pairs={{0,8},{8,16},{16,24},{1,9},{9,17},{17,25},{2,10},{10,18},{18,26},{... | collective-permute-start | bytes 1572872 | tf_op jit(solution)/shard_map/ppermute | solution.py:26
  70.5 4.8 %collective-permute-start.17 = (f32[3,1,4,64,512]{4,3,2,1,0:T(8,128)S(1)}, f32[3,1,4,64,512]{4,3,2,1,0:T(8,128)S(1)}, u32[]{:S(2)}, u32[]{:S(2)}) collective-permute-start(f32[3,1,4,64,512]{4,3,2,1,0:T(8,128)S(1)} %collective-permute-done.15.near), channel_id=1, source_target_pairs={{0,1},{1,0},{2,3},{3,2},{4,5},{5,4},{6,7},{7,6},{8,9},{9,8},{10,11... | collective-permute-start | bytes 4718600 | tf_op jit(solution)/shard_map/ppermute | solution.py:20
  70.5 4.8 %collective-permute-start.18 = (f32[1,296,512]{2,1,0:T(8,128)S(1)}, f32[1,296,512]{2,1,0:T(8,128)S(1)}, u32[]{:S(2)}, u32[]{:S(2)}) collective-permute-start(f32[1,296,512]{2,1,0:T(8,128)S(1)} %collective-permute-done.16.far), channel_id=1, source_target_pairs={{0,1},{1,0},{2,3},{3,2},{4,5},{5,4},{6,7},{7,6},{8,9},{9,8},{10,11... | collective-permute-start | bytes 1818632 | tf_op jit(solution)/shard_map/ppermute | solution.py:20
  78.9 15.3 %collective-permute-start.19 = (f32[16,16,512]{2,1,0:T(8,128)S(1)}, f32[16,16,512]{2,1,0:T(8,128)S(1)}, u32[]{:S(2)}, u32[]{:S(2)}) collective-permute-start(f32[16,16,512]{2,1,0:T(8,128)S(1)} %get-tuple-element.65), channel_id=1, source_target_pairs={{0,8},{8,16},{16,24},{1,9},{9,17},{17,25},{2,10},{10,18},{18,26},{... | collective-permute-start | bytes 1572872 | tf_op jit(solution)/shard_map/ppermute | solution.py:26

commit v8 on v5

--- a/solution.py
+++ b/solution.py
@@ -512,7 +512,7 @@
     else:
         own, x, y = from_neighbours(shard, "dp")
         near = {0: own, 1: swap(own, "dp", 1), 2: x, 4: y}
-        two = half_of(after(x, near[1]), 1, *(taps if len(taps) > 1 else ()))
+        two = half_of(x, 1, *(taps if len(taps) > 1 else ()))
         one = half_of(y, 0)
         x_late, y_late = after(x, two), after(y, one)
         near.update({3: swap(x_late, "dp", 1), 5: swap(y_late, "dp", 1)})

time: 96.1 us -> 96.7 us (level)
  waiting for transfers between devices: 48.7 us -> 50.7 us
  starting transfers between devices: 26.2 us -> 24.7 us
    ppermute x13, starting transfers between devices: 7.35 us -> 5.82 us  [swap(): return lax.ppermute(x, axis, [(i, i ^ bit) for i in range(size)])]
    ppermute x13, waiting for transfers between devices: 11.9 us -> 13.1 us  [swap(): return lax.ppermute(x, axis, [(i, i ^ bit) for i in range(size)])]
    ppermute x5, waiting for transfers between devices: 30.6 us -> 31.7 us  [from_behind(): lax.ppermute(x, axis, pairs + [(size - 1, 0)] * (around and size > 1))]
  transfers between devices with their start and end apart: 20 -> 20, of which waited for: 12 -> 11; matrix products, arithmetic and copies ran while one was open for 2% -> 2% of each run, Pallas kernels for 14% -> 14%
where the time goes in v8:
time: 96.7 us; the launch traced here: 95.8 us
  waiting for transfers between devices  50.7 us (52%)
  starting transfers between devices  24.7 us (26%)
  Pallas kernels  18 us (19%)
  local copies, waits for them, and re-layouts  1.82 us (2%)
    ppermute x5, waiting for transfers between devices, from_behind(): lax.ppermute(x, axis, pairs + [(size - 1, 0)] * (around and size > 1))  31.7 us
    pallas_call x15, Pallas kernels, call(): pl.pallas_call(kernel, out_shape=outs, in_specs=[spec(x, i, apart) for i,...  18 us
    ppermute x5, starting transfers between devices, from_behind(): lax.ppermute(x, axis, pairs + [(size - 1, 0)] * (around and size > 1))  14 us
    ppermute x13, waiting for transfers between devices, swap(): return lax.ppermute(x, axis, [(i, i ^ bit) for i in range(size)])  13.1 us
    ppermute x2, waiting for transfers between devices, from_ahead(): lax.ppermute(x, axis, [(i + 1, i) for i in range(lax.axis_size(axis) - 1)])  5.96 us
    ppermute x13, starting transfers between devices, swap(): return lax.ppermute(x, axis, [(i, i ^ bit) for i in range(size)])  5.82 us
    ppermute x2, starting transfers between devices, from_ahead(): lax.ppermute(x, axis, [(i + 1, i) for i in range(lax.axis_size(axis) - 1)])  4.85 us
  transfers between devices with their start and end apart: 20, of which 11 were waited for; matrix products, arithmetic and copies ran while one was open for 2% of the time, Pallas kernels for 14%

profile of v8, /device:TPU:16, one launch (start us, length us, event | category | flops | bytes accessed | tf_op | source)
XLA Modules:
  0.0 95.8 jit_solution(7588838538703101229)
XLA Ops:
  0.0 1.5 %collective-permute-start.3 = (f32[1,4,64,512]{3,2,1,0:T(8,128)}, f32[1,4,64,512]{3,2,1,0:T(8,128)S(1)}, u32[]{:S(2)}, u32[]{:S(2)}) collective-permute-start(f32[1,4,64,512]{3,2,1,0:T(8,128)} %refs_0_.2), channel_id=1, source_target_pairs={{0,4},{1,5},{2,6},{3,7},{4,0},{5,1},{6,2},{7,3},{8,12},{9,13},{10,... | collective-permute-start | bytes 1572872 | tf_op jit(solution)/shard_map/ppermute | solution.py:20
  1.5 1.5 %collective-permute-start.2 = (f32[1,4,64,512]{3,2,1,0:T(8,128)}, f32[1,4,64,512]{3,2,1,0:T(8,128)S(1)}, u32[]{:S(2)}, u32[]{:S(2)}) collective-permute-start(f32[1,4,64,512]{3,2,1,0:T(8,128)} %refs_0_.2), channel_id=1, source_target_pairs={{0,2},{1,3},{2,0},{3,1},{4,6},{5,7},{6,4},{7,5},{8,10},{9,11},{10,... | collective-permute-start | bytes 1572872 | tf_op jit(solution)/shard_map/ppermute | solution.py:20
  5.0 1.6 %collective-permute-start.9 = (f32[16,16,512]{2,1,0:T(8,128)S(1)}, f32[16,16,512]{2,1,0:T(8,128)S(1)}, u32[]{:S(2)}, u32[]{:S(2)}) collective-permute-start(f32[16,16,512]{2,1,0:T(8,128)S(1)} %slice_bitcast_fusion.newest), channel_id=1, source_target_pairs={{0,8},{8,16},{16,24},{24,0},{1,9},{9,17},{17,25},{25,1},{2,10},{10... | collective-permute-start | bytes 1572872 | tf_op jit(solution)/shard_map/ppermute | solution.py:26
  7.2 6.7 %collective-permute-done.3.block.refs_3_.refs_2_ = f32[1,4,64,512]{3,2,1,0:T(8,128)S(1)} collective-permute-done((f32[1,4,64,512]{3,2,1,0:T(8,128)}, f32[1,4,64,512]{3,2,1,0:T(8,128)S(1)}, u32[]{:S(2)}, u32[]{:S(2)}) %collective-permute-start.3) | collective-permute-done | bytes 524320 | tf_op jit(solution)/shard_map/ppermute | solution.py:20
  14.3 1.5 %collective-permute-done.4.refs_1_.refs_5_ = f32[4,9,128]{2,1,0:T(8,128)S(1)} collective-permute-done((f32[4,9,128]{2,1,0:T(8,128)S(1)}, f32[4,9,128]{2,1,0:T(8,128)S(1)}, u32[]{:S(2)}, u32[]{:S(2)}) %collective-permute-start.4) | collective-permute-done | bytes 18464 | tf_op jit(solution)/shard_map/ppermute | solution.py:20
  16.8 2.5 %collective-permute-done.9.got = f32[16,16,512]{2,1,0:T(8,128)S(1)} collective-permute-done((f32[16,16,512]{2,1,0:T(8,128)S(1)}, f32[16,16,512]{2,1,0:T(8,128)S(1)}, u32[]{:S(2)}, u32[]{:S(2)}) %collective-permute-start.9) | collective-permute-done | bytes 524320 | tf_op jit(solution)/shard_map/ppermute | solution.py:26
  20.5 2.5 %collective-permute-start.15 = (f32[3,1,4,64,512]{4,3,2,1,0:T(8,128)S(1)}, f32[3,1,4,64,512]{4,3,2,1,0:T(8,128)S(1)}, u32[]{:S(2)}, u32[]{:S(2)}) collective-permute-start(f32[3,1,4,64,512]{4,3,2,1,0:T(8,128)S(1)} %shard_map.55), channel_id=1, source_target_pairs={{8,0},{16,8},{24,16},{9,1},{17,9},{25,17},{10,2},{18,10},{26,18},{... | collective-permute-start | bytes 4718600 | tf_op jit(solution)/shard_map/ppermute | solution.py:30
  23.9 3.3 %collective-permute-done.7.refs_0_.one = f32[1,128,512]{2,1,0:T(8,128)S(1)} collective-permute-done((f32[1,128,512]{2,1,0:T(8,128)S(1)}, f32[1,128,512]{2,1,0:T(8,128)S(1)}, u32[]{:S(2)}, u32[]{:S(2)}) %collective-permute-start.7) | collective-permute-done | bytes 262176 | tf_op jit(solution)/shard_map/ppermute | solution.py:20
  27.7 1.5 %collective-permute-done.10.refs_1_ = f32[1,128,512]{2,1,0:T(8,128)S(1)} collective-permute-done((f32[1,128,512]{2,1,0:T(8,128)S(1)}, f32[1,128,512]{2,1,0:T(8,128)S(1)}, u32[]{:S(2)}, u32[]{:S(2)}) %collective-permute-start.10) | collective-permute-done | bytes 262176 | tf_op jit(solution)/shard_map/ppermute | solution.py:20
  29.2 2.5 %shard_map.50 = (f32[16,16,512]{2,1,0:T(8,128)S(1)}, bf16[4,512,512]{2,1,0:T(8,128)(2,1)S(1)}, bf16[4,512,512]{2,1,0:T(8,128)(2,1)S(1)}, f32[4,4,9,128]{3,2,1,0:T(8,128)S(1)}) custom-call(s32[1]{0:T(128)} %bitcast.2.position, f32[16,16,512]{2,1,0:T(8,128)S(1)} %slice_bitcast_fusion.newest, ...), custom_call_target="tpu_custom_call", output_to_operand_aliasing={{1}: (3, {}), {2}: (4, {})} | custom-call | flops 1610612736 | bytes 5767168 | tf_op jit(solution)/shard_map/pallas_call | solution.py:53
  31.7 3.5 %collective-permute-start.12 = (f32[16,16,512]{2,1,0:T(8,128)S(1)}, f32[16,16,512]{2,1,0:T(8,128)S(1)}, u32[]{:S(2)}, u32[]{:S(2)}) collective-permute-start(f32[16,16,512]{2,1,0:T(8,128)S(1)} %get-tuple-element.45.past), channel_id=1, source_target_pairs={{0,8},{8,16},{16,24},{1,9},{9,17},{17,25},{2,10},{10,18},{18,26},{... | collective-permute-start | bytes 1572872 | tf_op jit(solution)/shard_map/ppermute | solution.py:26
  36.2 2.4 %collective-permute-start.16 = (f32[1,296,512]{2,1,0:T(8,128)S(1)}, f32[1,296,512]{2,1,0:T(8,128)S(1)}, u32[]{:S(2)}, u32[]{:S(2)}) collective-permute-start(f32[1,296,512]{2,1,0:T(8,128)S(1)} %shard_map.56), channel_id=1, source_target_pairs={{8,0},{16,8},{24,16},{9,1},{17,9},{25,17},{10,2},{18,10},{26,18},{... | collective-permute-start | bytes 1818632 | tf_op jit(solution)/shard_map/ppermute | solution.py:30
  38.5 9.1 %collective-permute-done.12.got = f32[16,16,512]{2,1,0:T(8,128)S(1)} collective-permute-done((f32[16,16,512]{2,1,0:T(8,128)S(1)}, f32[16,16,512]{2,1,0:T(8,128)S(1)}, u32[]{:S(2)}, u32[]{:S(2)}) %collective-permute-start.12) | collective-permute-done | bytes 524320 | tf_op jit(solution)/shard_map/ppermute | solution.py:26
  47.6 3.5 %collective-permute-start.14 = (f32[16,16,512]{2,1,0:T(8,128)S(1)}, f32[16,16,512]{2,1,0:T(8,128)S(1)}, u32[]{:S(2)}, u32[]{:S(2)}) collective-permute-start(f32[16,16,512]{2,1,0:T(8,128)S(1)} %collective-permute-done.12.got), channel_id=1, source_target_pairs={{8,16},{16,24},{9,17},{17,25},{10,18},{18,26},{11,19},{19,27},{12,... | collective-permute-start | bytes 1572872 | tf_op jit(solution)/shard_map/ppermute | solution.py:26
  51.1 2.3 %shard_map.52 = (f32[4,16,16,512]{3,2,1,0:T(8,128)}, f32[16,16,512]{2,1,0:T(8,128)S(1)}) custom-call(s32[1]{0:T(128)} %bitcast.section, f32[3,16,16,512]{3,2,1,0:T(8,128)S(1)} %bitcast.13, f32[16,16,512]{2,1,0:T(8,128)S(1)} %collective-permute-done.12.got, f32[16,16,512]{2,1,0:T(8,128)S(1)} %shard_map.51.early, ...), custom_call_target="tpu_custom_call" | custom-call | flops 2415919104 | bytes 7864320 | tf_op jit(solution)/shard_map/pallas_call | solution.py:53
  53.4 1.9 %collective-permute-start.13 = (f32[16,16,512]{2,1,0:T(8,128)S(1)}, f32[16,16,512]{2,1,0:T(8,128)S(1)}, u32[]{:S(2)}, u32[]{:S(2)}) collective-permute-start(f32[16,16,512]{2,1,0:T(8,128)S(1)} %get-tuple-element.49.past), channel_id=1, source_target_pairs={{0,8},{8,16},{16,24},{1,9},{9,17},{17,25},{2,10},{10,18},{18,26},{... | collective-permute-start | bytes 1572872 | tf_op jit(solution)/shard_map/ppermute | solution.py:26
  55.3 9.0 %collective-permute-done.14.got = f32[16,16,512]{2,1,0:T(8,128)S(1)} collective-permute-done((f32[16,16,512]{2,1,0:T(8,128)S(1)}, f32[16,16,512]{2,1,0:T(8,128)S(1)}, u32[]{:S(2)}, u32[]{:S(2)}) %collective-permute-start.14) | collective-permute-done | bytes 524320 | tf_op jit(solution)/shard_map/ppermute | solution.py:26
  65.2 6.0 %collective-permute-done.16.far = f32[1,296,512]{2,1,0:T(8,128)S(1)} collective-permute-done((f32[1,296,512]{2,1,0:T(8,128)S(1)}, f32[1,296,512]{2,1,0:T(8,128)S(1)}, u32[]{:S(2)}, u32[]{:S(2)}) %collective-permute-start.16) | collective-permute-done | bytes 606240 | tf_op jit(solution)/shard_map/ppermute | solution.py:30
  71.6 2.2 %collective-permute-done.13.got = f32[16,16,512]{2,1,0:T(8,128)S(1)} collective-permute-done((f32[16,16,512]{2,1,0:T(8,128)S(1)}, f32[16,16,512]{2,1,0:T(8,128)S(1)}, u32[]{:S(2)}, u32[]{:S(2)}) %collective-permute-start.13) | collective-permute-done | bytes 524320 | tf_op jit(solution)/shard_map/ppermute | solution.py:26
  73.8 2.2 %shard_map.54 = (f32[4,16,16,512]{3,2,1,0:T(8,128)}, f32[16,16,512]{2,1,0:T(8,128)S(1)}) custom-call(s32[1]{0:T(128)} %bitcast.section, f32[3,16,16,512]{3,2,1,0:T(8,128)S(1)} %bitcast.15, f32[16,16,512]{2,1,0:T(8,128)S(1)} %collective-permute-done.13.got, f32[16,16,512]{2,1,0:T(8,128)S(1)} %shard_map.53.early, ...), custom_call_target="tpu_custom_call", output_to_operand_aliasing={{0}: (8, {})} | custom-call | flops 14495514624 | bytes 39321600 | tf_op jit(solution)/shard_map/pallas_call | solution.py:53
  76.6 3.0 %shard_map.58 = (f32[4,16,16,512]{3,2,1,0:T(8,128)}, f32[16,16,512]{2,1,0:T(8,128)S(1)}) custom-call(s32[1]{0:T(128)} %bitcast.section, f32[3,16,16,512]{3,2,1,0:T(8,128)S(1)} %bitcast.16, f32[16,16,512]{2,1,0:T(8,128)S(1)} %collective-permute-done.13.got, f32[16,16,512]{2,1,0:T(8,128)S(1)} %get-tuple-element.52.newest, ...), custom_call_target="tpu_custom_call", output_to_operand_aliasing={{0}: (7, {})} | custom-call | flops 2818572288 | bytes 8912896 | tf_op jit(solution)/shard_map/pallas_call | solution.py:53
  79.7 3.5 %collective-permute-start.19 = (f32[16,16,512]{2,1,0:T(8,128)S(1)}, f32[16,16,512]{2,1,0:T(8,128)S(1)}, u32[]{:S(2)}, u32[]{:S(2)}) collective-permute-start(f32[16,16,512]{2,1,0:T(8,128)S(1)} %get-tuple-element.63), channel_id=1, source_target_pairs={{0,8},{8,16},{16,24},{1,9},{9,17},{17,25},{2,10},{10,18},{18,26},{... | collective-permute-start | bytes 1572872 | tf_op jit(solution)/shard_map/ppermute | solution.py:26
  83.2 2.8 %shard_map.59.own = f32[16,16,512]{2,1,0:T(8,128)S(1)} custom-call(f32[3,16,16,512]{3,2,1,0:T(8,128)S(1)} %bitcast.17, f32[4,4,9,128]{3,2,1,0:T(8,128)S(1)} %get-tuple-element.46.table, bf16[4,512,512]{2,1,0:T(8,128)(2,1)S(1)} %get-tuple-element.47.highs, bf16[4,512,512]{2,1,0:T(8,128)(2,1)S(1)} %get-tuple-element.48.lows), custom_call_target="tpu_custom_call" | custom-call | flops 1610612736 | bytes 5767168 | tf_op jit(solution)/shard_map/pallas_call | solution.py:53
  86.0 8.8 %collective-permute-done.19.got = f32[16,16,512]{2,1,0:T(8,128)S(1)} collective-permute-done((f32[16,16,512]{2,1,0:T(8,128)S(1)}, f32[16,16,512]{2,1,0:T(8,128)S(1)}, u32[]{:S(2)}, u32[]{:S(2)}) %collective-permute-start.19) | collective-permute-done | bytes 524320 | tf_op jit(solution)/shard_map/ppermute | solution.py:26
  (40 shorter events, 10.0 us)
Async XLA Ops:
  0.0 19.9 %copy-start.2 = (f32[1,4,64,512]{3,2,1,0:T(8,128)S(1)}, f32[1,4,64,512]{3,2,1,0:T(8,128)}, u32[]{:S(2)}) copy-start(f32[1,4,64,512]{3,2,1,0:T(8,128)} %refs_0_.2) | copy-start | bytes 1572868
  0.0 13.9 %collective-permute-start.3 = (f32[1,4,64,512]{3,2,1,0:T(8,128)}, f32[1,4,64,512]{3,2,1,0:T(8,128)S(1)}, u32[]{:S(2)}, u32[]{:S(2)}) collective-permute-start(f32[1,4,64,512]{3,2,1,0:T(8,128)} %refs_0_.2), channel_id=1, source_target_pairs={{0,4},{1,5},{2,6},{3,7},{4,0},{5,1},{6,2},{7,3},{8,12},{9,13},{10,... | collective-permute-start | bytes 1572872 | tf_op jit(solution)/shard_map/ppermute | solution.py:20
  1.5 14.3 %collective-permute-start.2 = (f32[1,4,64,512]{3,2,1,0:T(8,128)}, f32[1,4,64,512]{3,2,1,0:T(8,128)S(1)}, u32[]{:S(2)}, u32[]{:S(2)}) collective-permute-start(f32[1,4,64,512]{3,2,1,0:T(8,128)} %refs_0_.2), channel_id=1, source_target_pairs={{0,2},{1,3},{2,0},{3,1},{4,6},{5,7},{6,4},{7,5},{8,10},{9,11},{10,... | collective-permute-start | bytes 1572872 | tf_op jit(solution)/shard_map/ppermute | solution.py:20
  3.7 1.2 %collective-permute-start = (f32[4,9,64]{2,1,0:T(8,128)S(1)}, f32[4,9,64]{2,1,0:T(8,128)S(1)}, u32[]{:S(2)}, u32[]{:S(2)}) collective-permute-start(f32[4,9,64]{2,1,0:T(8,128)S(1)} %bitcast.20), channel_id=1, source_target_pairs={{0,1},{1,0},{2,3},{3,2},{4,5},{5,4},{6,7},{7,6},{8,9},{9,8},{10,11... | collective-permute-start | bytes 27656 | tf_op jit(solution)/shard_map/ppermute | solution.py:20
  5.0 14.3 %collective-permute-start.9 = (f32[16,16,512]{2,1,0:T(8,128)S(1)}, f32[16,16,512]{2,1,0:T(8,128)S(1)}, u32[]{:S(2)}, u32[]{:S(2)}) collective-permute-start(f32[16,16,512]{2,1,0:T(8,128)S(1)} %slice_bitcast_fusion.newest), channel_id=1, source_target_pairs={{0,8},{8,16},{16,24},{24,0},{1,9},{9,17},{17,25},{25,1},{2,10},{10... | collective-permute-start | bytes 1572872 | tf_op jit(solution)/shard_map/ppermute | solution.py:26
  6.7 9.2 %collective-permute-start.4 = (f32[4,9,128]{2,1,0:T(8,128)S(1)}, f32[4,9,128]{2,1,0:T(8,128)S(1)}, u32[]{:S(2)}, u32[]{:S(2)}) collective-permute-start(f32[4,9,128]{2,1,0:T(8,128)S(1)} %maximum_select_fusion.refs_0_.refs_4_), channel_id=1, source_target_pairs={{0,2},{1,3},{2,0},{3,1},{4,6},{5,7},{6,4},{7,5},{8,10},{9,11},{10,... | collective-permute-start | bytes 55304 | tf_op jit(solution)/shard_map/ppermute | solution.py:20
  7.2 12.7 %collective-permute-start.1 = (f32[1,4,64,512]{3,2,1,0:T(8,128)}, f32[1,4,64,512]{3,2,1,0:T(8,128)S(1)}, u32[]{:S(2)}, u32[]{:S(2)}) collective-permute-start(f32[1,4,64,512]{3,2,1,0:T(8,128)} %refs_0_.2), channel_id=1, source_target_pairs={{0,1},{1,0},{2,3},{3,2},{4,5},{5,4},{6,7},{7,6},{8,9},{9,8},{10,11... | collective-permute-start | bytes 1572872 | tf_op jit(solution)/shard_map/ppermute | solution.py:20
  14.2 5.7 %collective-permute-start.6 = (f32[1,4,64,512]{3,2,1,0:T(8,128)S(1)}, f32[1,4,64,512]{3,2,1,0:T(8,128)S(1)}, u32[]{:S(2)}, u32[]{:S(2)}) collective-permute-start(f32[1,4,64,512]{3,2,1,0:T(8,128)S(1)} %collective-permute-done.3.block.refs_3_.refs_2_), channel_id=1, source_target_pairs={{0,1},{1,0},{2,3},{3,2},{4,5},{5,4},{6,7},{7,6},{8,9},{9,8},{10,11... | collective-permute-start | bytes 1572872 | tf_op jit(solution)/shard_map/ppermute | solution.py:20
  16.2 3.7 %collective-permute-start.5 = (f32[1,4,64,512]{3,2,1,0:T(8,128)S(1)}, f32[1,4,64,512]{3,2,1,0:T(8,128)S(1)}, u32[]{:S(2)}, u32[]{:S(2)}) collective-permute-start(f32[1,4,64,512]{3,2,1,0:T(8,128)S(1)} %collective-permute-done.2.block.refs_2_.refs_1_), channel_id=1, source_target_pairs={{0,1},{1,0},{2,3},{3,2},{4,5},{5,4},{6,7},{7,6},{8,9},{9,8},{10,11... | collective-permute-start | bytes 1572872 | tf_op jit(solution)/shard_map/ppermute | solution.py:20
  16.3 10.9 %collective-permute-start.8 = (f32[1,160,512]{2,1,0:T(8,128)S(1)}, f32[1,160,512]{2,1,0:T(8,128)S(1)}, u32[]{:S(2)}, u32[]{:S(2)}) collective-permute-start(f32[1,160,512]{2,1,0:T(8,128)S(1)} %shard_map.46), channel_id=1, source_target_pairs={{0,4},{1,5},{2,6},{3,7},{4,0},{5,1},{6,2},{7,3},{8,12},{9,13},{10,... | collective-permute-start | bytes 983048 | tf_op jit(solution)/shard_map/ppermute | solution.py:20
  19.3 7.8 %collective-permute-start.7 = (f32[1,128,512]{2,1,0:T(8,128)S(1)}, f32[1,128,512]{2,1,0:T(8,128)S(1)}, u32[]{:S(2)}, u32[]{:S(2)}) collective-permute-start(f32[1,128,512]{2,1,0:T(8,128)S(1)} %shard_map.47), channel_id=1, source_target_pairs={{0,2},{1,3},{2,0},{3,1},{4,6},{5,7},{6,4},{7,5},{8,10},{9,11},{10,... | collective-permute-start | bytes 786440 | tf_op jit(solution)/shard_map/ppermute | solution.py:20
  20.3 2.7 %copy-start.1 = (f32[1,2,1,16,16,512]{5,4,3,2,1,0:T(8,128)S(1)}, f32[1,2,1,16,16,512]{5,4,3,2,1,0:T(8,128)}, u32[]{:S(2)}) copy-start(f32[1,2,1,16,16,512]{5,4,3,2,1,0:T(8,128)} %param.4) | copy-start | bytes 3145732
  20.5 50.7 %collective-permute-start.15 = (f32[3,1,4,64,512]{4,3,2,1,0:T(8,128)S(1)}, f32[3,1,4,64,512]{4,3,2,1,0:T(8,128)S(1)}, u32[]{:S(2)}, u32[]{:S(2)}) collective-permute-start(f32[3,1,4,64,512]{4,3,2,1,0:T(8,128)S(1)} %shard_map.55), channel_id=1, source_target_pairs={{8,0},{16,8},{24,16},{9,1},{17,9},{25,17},{10,2},{18,10},{26,18},{... | collective-permute-start | bytes 4718600 | tf_op jit(solution)/shard_map/ppermute | solution.py:30
  23.9 11.3 %copy-start = (f32[3,1,16,16,512]{4,3,2,1,0:T(8,128)S(1)}, f32[3,1,16,16,512]{4,3,2,1,0:T(8,128)}, u32[]{:S(2)}) copy-start(f32[3,1,16,16,512]{4,3,2,1,0:T(8,128)} %param.5) | copy-start | bytes 4718596
  27.2 2.0 %collective-permute-start.11 = (f32[1,160,512]{2,1,0:T(8,128)S(1)}, f32[1,160,512]{2,1,0:T(8,128)S(1)}, u32[]{:S(2)}, u32[]{:S(2)}) collective-permute-start(f32[1,160,512]{2,1,0:T(8,128)S(1)} %collective-permute-done.8.refs_2_.two), channel_id=1, source_target_pairs={{0,1},{1,0},{2,3},{3,2},{4,5},{5,4},{6,7},{7,6},{8,9},{9,8},{10,11... | collective-permute-start | bytes 983048 | tf_op jit(solution)/shard_map/ppermute | solution.py:20
  27.2 2.0 %collective-permute-start.10 = (f32[1,128,512]{2,1,0:T(8,128)S(1)}, f32[1,128,512]{2,1,0:T(8,128)S(1)}, u32[]{:S(2)}, u32[]{:S(2)}) collective-permute-start(f32[1,128,512]{2,1,0:T(8,128)S(1)} %collective-permute-done.7.refs_0_.one), channel_id=1, source_target_pairs={{0,1},{1,0},{2,3},{3,2},{4,5},{5,4},{6,7},{7,6},{8,9},{9,8},{10,11... | collective-permute-start | bytes 786440 | tf_op jit(solution)/shard_map/ppermute | solution.py:20
  31.7 15.9 %collective-permute-start.12 = (f32[16,16,512]{2,1,0:T(8,128)S(1)}, f32[16,16,512]{2,1,0:T(8,128)S(1)}, u32[]{:S(2)}, u32[]{:S(2)}) collective-permute-start(f32[16,16,512]{2,1,0:T(8,128)S(1)} %get-tuple-element.45.past), channel_id=1, source_target_pairs={{0,8},{8,16},{16,24},{1,9},{9,17},{17,25},{2,10},{10,18},{18,26},{... | collective-permute-start | bytes 1572872 | tf_op jit(solution)/shard_map/ppermute | solution.py:26
  36.2 35.0 %collective-permute-start.16 = (f32[1,296,512]{2,1,0:T(8,128)S(1)}, f32[1,296,512]{2,1,0:T(8,128)S(1)}, u32[]{:S(2)}, u32[]{:S(2)}) collective-permute-start(f32[1,296,512]{2,1,0:T(8,128)S(1)} %shard_map.56), channel_id=1, source_target_pairs={{8,0},{16,8},{24,16},{9,1},{17,9},{25,17},{10,2},{18,10},{26,18},{... | collective-permute-start | bytes 1818632 | tf_op jit(solution)/shard_map/ppermute | solution.py:30
  47.6 16.7 %collective-permute-start.14 = (f32[16,16,512]{2,1,0:T(8,128)S(1)}, f32[16,16,512]{2,1,0:T(8,128)S(1)}, u32[]{:S(2)}, u32[]{:S(2)}) collective-permute-start(f32[16,16,512]{2,1,0:T(8,128)S(1)} %collective-permute-done.12.got), channel_id=1, source_target_pairs={{8,16},{16,24},{9,17},{17,25},{10,18},{18,26},{11,19},{19,27},{12,... | collective-permute-start | bytes 1572872 | tf_op jit(solution)/shard_map/ppermute | solution.py:26
  53.4 20.5 %collective-permute-start.13 = (f32[16,16,512]{2,1,0:T(8,128)S(1)}, f32[16,16,512]{2,1,0:T(8,128)S(1)}, u32[]{:S(2)}, u32[]{:S(2)}) collective-permute-start(f32[16,16,512]{2,1,0:T(8,128)S(1)} %get-tuple-element.49.past), channel_id=1, source_target_pairs={{0,8},{8,16},{16,24},{1,9},{9,17},{17,25},{2,10},{10,18},{18,26},{... | collective-permute-start | bytes 1572872 | tf_op jit(solution)/shard_map/ppermute | solution.py:26
  71.1 5.0 %collective-permute-start.17 = (f32[3,1,4,64,512]{4,3,2,1,0:T(8,128)S(1)}, f32[3,1,4,64,512]{4,3,2,1,0:T(8,128)S(1)}, u32[]{:S(2)}, u32[]{:S(2)}) collective-permute-start(f32[3,1,4,64,512]{4,3,2,1,0:T(8,128)S(1)} %collective-permute-done.15.near), channel_id=1, source_target_pairs={{0,1},{1,0},{2,3},{3,2},{4,5},{5,4},{6,7},{7,6},{8,9},{9,8},{10,11... | collective-permute-start | bytes 4718600 | tf_op jit(solution)/shard_map/ppermute | solution.py:20
  71.1 5.0 %collective-permute-start.18 = (f32[1,296,512]{2,1,0:T(8,128)S(1)}, f32[1,296,512]{2,1,0:T(8,128)S(1)}, u32[]{:S(2)}, u32[]{:S(2)}) collective-permute-start(f32[1,296,512]{2,1,0:T(8,128)S(1)} %collective-permute-done.16.far), channel_id=1, source_target_pairs={{0,1},{1,0},{2,3},{3,2},{4,5},{5,4},{6,7},{7,6},{8,9},{9,8},{10,11... | collective-permute-start | bytes 1818632 | tf_op jit(solution)/shard_map/ppermute | solution.py:20
  79.7 15.2 %collective-permute-start.19 = (f32[16,16,512]{2,1,0:T(8,128)S(1)}, f32[16,16,512]{2,1,0:T(8,128)S(1)}, u32[]{:S(2)}, u32[]{:S(2)}) collective-permute-start(f32[16,16,512]{2,1,0:T(8,128)S(1)} %get-tuple-element.63), channel_id=1, source_target_pairs={{0,8},{8,16},{16,24},{1,9},{9,17},{17,25},{2,10},{10,18},{18,26},{... | collective-permute-start | bytes 1572872 | tf_op jit(solution)/shard_map/ppermute | solution.py:26
